TPU v7x, 128 devices: a whole 4x4x4 slice. The times are simulated.
128 devices in a mesh: dp: 8 (over z, core), mp: 16 (over x, y).
Axes of the slice: x: 4, y: 4, z: 4, core: 2. Of those that a mesh axis runs over, the one named last changes fastest.
Arguments:
- rhs: float32 [4096, 128], P(('dp', 'mp')), may hold values from -24 to 24
- blocks: bfloat16 [8, 16, 384, 128, 128], P('dp', 'mp'), may hold values from -0.5 to 0.5
- block_rows: int32 [8, 16, 384], P('dp', 'mp'), may hold values from 0 to 511
- block_cols: int32 [8, 16, 384], P('dp', 'mp'), may hold values from 0 to 767
- counts: int32 [8, 16], P('dp', 'mp'), may hold values from 128 to 384, as said below
Outputs:
- solution: float32 [12288, 128], P(('mp', 'dp'))
Inputs may be any that keep to these rules, and one draw needn't show every extreme that they name: `counts`: one tile holds exactly 384 live slots and one exactly 128; slots at or beyond a tile's count hold entries that are not used.
All inputs are finite; a program needn't handle non-finite values.
Results may differ from a plain program's by a relative error of at most 0.009.
Values may be sent and summed in bfloat16 or wider, within the bound.
No kernel may reach another device: no remote copies, remote signals or barrier semaphores. Data moves between devices by JAX's collectives and lax.ppermute only.
A program may use at most 64 MiB of HBM per device.

v0:
```python
import jax
import jax.numpy as jnp
from jax import lax
from jax.sharding import PartitionSpec as P

RB = 512
CB = 768
ITERS = 2


def body(rhs, blocks, block_rows, block_cols, counts):
    tile_blocks = blocks[0, 0]
    slot_rows = block_rows[0, 0]
    slot_cols = block_cols[0, 0]
    live_count = counts[0, 0]
    slot_total = tile_blocks.shape[0]
    slot_live = (jnp.arange(slot_total, dtype=jnp.int32) < live_count)[:, None]
    onehot_rows = (slot_rows[None, :] == jnp.arange(RB, dtype=jnp.int32)[:, None]).astype(
        jnp.float32
    )
    onehot_cols = (slot_cols[None, :] == jnp.arange(CB, dtype=jnp.int32)[:, None]).astype(
        jnp.float32
    )

    def cols_partial(data_group):
        picked = data_group[slot_rows]
        products = jnp.einsum("kab,ka->kb", tile_blocks, picked, preferred_element_type=jnp.float32)
        products = jnp.where(slot_live, products, jnp.zeros_like(products))
        return jnp.dot(onehot_cols, products, precision=lax.Precision.HIGHEST)

    def adjoint(data_vec):
        whole = lax.all_gather(data_vec.astype(jnp.bfloat16), "mp", axis=0, tiled=True)
        return lax.psum_scatter(cols_partial(whole), "dp", scatter_dimension=0, tiled=True)

    def total_norm(vector):
        return jnp.sqrt(lax.psum(jnp.sum(vector * vector), ("dp", "mp")))

    beta_now = total_norm(rhs)
    data_vec = rhs / beta_now
    model_vec = adjoint(data_vec)
    alpha_now = total_norm(model_vec)
    model_vec = model_vec / alpha_now
    search_dir = model_vec
    solution = jnp.zeros_like(model_vec)
    phi_bar = beta_now
    rho_bar = alpha_now
    for iteration in range(ITERS):
        forward_whole = lax.all_gather(model_vec.astype(jnp.bfloat16), "dp", axis=0, tiled=True)
        rows_picked = forward_whole[slot_cols]
        rows_products = jnp.einsum(
            "kab,kb->ka", tile_blocks, rows_picked, preferred_element_type=jnp.float32
        )
        rows_products = jnp.where(slot_live, rows_products, jnp.zeros_like(rows_products))
        data_vec = (
            lax.psum_scatter(
                jnp.dot(onehot_rows, rows_products, precision=lax.Precision.HIGHEST).astype(
                    jnp.bfloat16
                ),
                "mp",
                scatter_dimension=0,
                tiled=True,
            ).astype(jnp.float32)
            - alpha_now * data_vec
        )
        beta_now = total_norm(data_vec)
        data_vec = data_vec / beta_now
        model_vec = adjoint(data_vec) - beta_now * model_vec
        alpha_now = total_norm(model_vec)
        model_vec = model_vec / alpha_now
        rho_now = jnp.sqrt(rho_bar * rho_bar + beta_now * beta_now)
        cosine = rho_bar / rho_now
        sine = beta_now / rho_now
        theta_now = sine * alpha_now
        rho_bar = -cosine * alpha_now
        phi_now = cosine * phi_bar
        phi_bar = sine * phi_bar
        solution = solution + phi_now / rho_now * search_dir
        search_dir = model_vec - theta_now / rho_now * search_dir
    return solution


def solution(mesh):
    placed = (
        P(("dp", "mp"), None),
        P("dp", "mp", None, None, None),
        P("dp", "mp", None),
        P("dp", "mp", None),
        P("dp", "mp"),
    )
    return jax.shard_map(
        body, mesh=mesh, in_specs=placed, out_specs=P(("mp", "dp"), None), check_vma=False
    )
```

profile of v0, /device:TPU:1, one launch (start us, length us, event | category | flops | bytes accessed | tf_op | source)
XLA Modules:
  0.0 662.9 jit_solution(1826946689988683846)
XLA Ops:
  7.9 68.7 %psum.35 = f32[]{:T(128)} all-reduce(f32[]{:T(128)} %multiply_reduce_fusion.4), channel_id=1, replica_groups=mesh['dp'=8,'mp'=16] {'dp','mp'}, use_global_device_ids=true, to_apply=%region_1.0 | all-reduce | flops 1 | bytes 8 | tf_op jit(solution)/shard_map/psum | solution.py:36
  78.0 16.0 %all_gather.12 = bf16[512,128]{1,0:T(8,128)(2,1)S(1)} all-gather(bf16[32,128]{1,0:T(8,128)(2,1)S(1)} %fusion.39), channel_id=1, replica_groups=mesh['dp'=8,'mp'=16] {'mp'}, dimensions={0}, use_global_device_ids=true | all-gather | bytes 139264 | tf_op jit(solution)/shard_map/all_gather | solution.py:32
  96.0 1.4 gather_fusion
  97.5 6.4 fusion.6
  103.9 1.5 fusion.9
  105.4 31.4 %reduce-scatter.5.cloned.1.call-done = f32[96,128]{1,0:T(8,128)} async-done(((f32[768,128]{1,0:T(8,128)}), f32[96,128]{1,0:T(8,128)}) %reduce-scatter.5.cloned.1.call-update) | async-done | bytes 49168 | tf_op jit(solution)/shard_map/reduce_scatter | solution.py:33
  138.3 67.6 %psum.36 = f32[]{:T(128)} all-reduce(f32[]{:T(128)} %multiply_reduce_fusion.1), channel_id=1, replica_groups=mesh['dp'=8,'mp'=16] {'dp','mp'}, use_global_device_ids=true, to_apply=%region_4.5 | all-reduce | flops 1 | bytes 8 | tf_op jit(solution)/shard_map/psum | solution.py:36
  207.4 13.7 %all_gather.13 = bf16[768,128]{1,0:T(8,128)(2,1)S(1)} all-gather(bf16[96,128]{1,0:T(8,128)(2,1)S(1)} %fusion.40), channel_id=1, replica_groups=mesh['dp'=8,'mp'=16] {'dp'}, dimensions={0}, use_global_device_ids=true | all-gather | bytes 221184 | tf_op jit(solution)/shard_map/all_gather | solution.py:48
  221.1 1.4 gather_fusion.1
  222.6 9.5 %fusion.4 = f32[384,1,128]{2,1,0:T(1,128)S(1)} fusion(bf16[1,1,384,128,128]{4,3,2,1,0:T(8,128)(2,1)} %param.6, bf16[384,128,1]{1,0,2:T(8,128)(2,1)S(1)} %bitcast.32), kind=kOutput, calls=%fused_computation.8 | convolution fusion | flops 12582912 | bytes 12877824 | tf_op jit(solution)/shard_map/kab,kb->ka/dot_general | solution.py:50
  233.3 65.8 %reduce-scatter.7.cloned.1.call-done = bf16[32,128]{1,0:T(8,128)(2,1)} async-done(((bf16[512,128]{1,0:T(8,128)(2,1)}), bf16[32,128]{1,0:T(8,128)(2,1)}) %reduce-scatter.7.cloned.1.call-update) | async-done | bytes 8208 | tf_op jit(solution)/shard_map/reduce_scatter | solution.py:55
  300.5 66.3 %psum.37 = f32[]{:T(128)} all-reduce(f32[]{:T(128)} %multiply_reduce_fusion.3), channel_id=1, replica_groups=mesh['dp'=8,'mp'=16] {'dp','mp'}, use_global_device_ids=true, to_apply=%region_7.8 | all-reduce | flops 1 | bytes 8 | tf_op jit(solution)/shard_map/psum | solution.py:36
  368.2 16.2 %all_gather.14 = bf16[512,128]{1,0:T(8,128)(2,1)S(1)} all-gather(bf16[32,128]{1,0:T(8,128)(2,1)S(1)} %fusion.34), channel_id=1, replica_groups=mesh['dp'=8,'mp'=16] {'mp'}, dimensions={0}, use_global_device_ids=true | all-gather | bytes 139264 | tf_op jit(solution)/shard_map/all_gather | solution.py:32
  384.4 1.4 gather_fusion.2
  385.8 6.4 fusion.2
  392.2 1.5 fusion.8
  393.7 31.3 %reduce-scatter.9.cloned.1.call-done = f32[96,128]{1,0:T(8,128)} async-done(((f32[768,128]{1,0:T(8,128)}), f32[96,128]{1,0:T(8,128)}) %reduce-scatter.9.cloned.1.call-update) | async-done | bytes 49168 | tf_op jit(solution)/shard_map/reduce_scatter | solution.py:33
  425.0 1.5 multiply_reduce_fusion
  426.5 67.4 %psum.38 = f32[]{:T(128)} all-reduce(f32[]{:T(128)} %multiply_reduce_fusion), channel_id=1, replica_groups=mesh['dp'=8,'mp'=16] {'dp','mp'}, use_global_device_ids=true, to_apply=%region_10.11 | all-reduce | flops 1 | bytes 8 | tf_op jit(solution)/shard_map/psum | solution.py:36
  495.4 13.6 %all_gather.15 = bf16[768,128]{1,0:T(8,128)(2,1)S(1)} all-gather(bf16[96,128]{1,0:T(8,128)(2,1)S(1)} %fusion.30), channel_id=1, replica_groups=mesh['dp'=8,'mp'=16] {'dp'}, dimensions={0}, use_global_device_ids=true | all-gather | bytes 221184 | tf_op jit(solution)/shard_map/all_gather | solution.py:48
  509.0 1.4 gather_fusion.3
  510.4 9.5 %fusion = f32[384,1,128]{2,1,0:T(1,128)S(1)} fusion(bf16[1,1,384,128,128]{4,3,2,1,0:T(8,128)(2,1)} %param.6, bf16[384,128,1]{1,0,2:T(8,128)(2,1)S(1)} %bitcast.31), kind=kOutput, calls=%fused_computation.4 | convolution fusion | flops 12582912 | bytes 12877824 | tf_op jit(solution)/shard_map/kab,kb->ka/dot_general | solution.py:50
  521.4 65.8 %reduce-scatter.11.cloned.1.call-done = bf16[32,128]{1,0:T(8,128)(2,1)} async-done(((bf16[512,128]{1,0:T(8,128)(2,1)}), bf16[32,128]{1,0:T(8,128)(2,1)}) %reduce-scatter.11.cloned.1.call-update) | async-done | bytes 8208 | tf_op jit(solution)/shard_map/reduce_scatter | solution.py:55
  588.5 66.4 %psum.39 = f32[]{:T(128)} all-reduce(f32[]{:T(128)} %multiply_reduce_fusion.2), channel_id=1, replica_groups=mesh['dp'=8,'mp'=16] {'dp','mp'}, use_global_device_ids=true, to_apply=%region_13.14 | all-reduce | flops 1 | bytes 8 | tf_op jit(solution)/shard_map/psum | solution.py:36
  (38 shorter events, 13.2 us)
Async XLA Ops:
  6.5 131.8 %copy-start.5 = (s32[1,1,384]{2,1,0:T(1,128)S(1)}, s32[1,1,384]{2,1,0:T(1,128)}, u32[]{:S(2)}) copy-start(s32[1,1,384]{2,1,0:T(1,128)} %param.7) | copy-start | bytes 4612
  6.5 98.8 %copy-start.4 = (s32[1,1,384]{2,1,0:T(1,128)S(1)}, s32[1,1,384]{2,1,0:T(1,128)}, u32[]{:S(2)}) copy-start(s32[1,1,384]{2,1,0:T(1,128)} %param.8) | copy-start | bytes 4612
  6.5 130.3 %reduce-scatter.5.cloned.1.call-start = ((), (), s32[]{:S(2)}) async-start(), calls=%async_computation.4 | async-start | bytes 442368 | tf_op jit(solution)/shard_map/reduce_scatter | solution.py:33
  103.9 195.3 %copy-start.2 = (f32[32,128]{1,0:T(8,128)S(1)}, f32[32,128]{1,0:T(8,128)}, u32[]{:S(2)}) copy-start(f32[32,128]{1,0:T(8,128)} %param.5) | copy-start | bytes 49156
  105.3 193.8 %reduce-scatter.7.cloned.1.call-start = ((), (), s32[]{:S(2)}) async-start(), calls=%async_computation.5 | async-start | bytes 139264 | tf_op jit(solution)/shard_map/reduce_scatter | solution.py:55
  232.0 193.0 %copy-start = (f32[96,128]{1,0:T(8,128)S(1)}, f32[96,128]{1,0:T(8,128)}, u32[]{:S(2)}) copy-start(f32[96,128]{1,0:T(8,128)} %reduce-scatter.5.cloned.1.call-done) | copy-start | bytes 147460
  233.3 191.7 %reduce-scatter.9.cloned.1.call-start = ((), (), s32[]{:S(2)}) async-start(), calls=%async_computation.6 | async-start | bytes 442368 | tf_op jit(solution)/shard_map/reduce_scatter | solution.py:33
  392.2 195.0 %copy-start.3 = (bf16[32,128]{1,0:T(8,128)(2,1)S(1)}, bf16[32,128]{1,0:T(8,128)(2,1)}, u32[]{:S(2)}) copy-start(bf16[32,128]{1,0:T(8,128)(2,1)} %reduce-scatter.7.cloned.1.call-done) | copy-start | bytes 24580
  393.7 193.5 %reduce-scatter.11.cloned.1.call-start = ((), (), s32[]{:S(2)}) async-start(), calls=%async_computation.7 | async-start | bytes 139264 | tf_op jit(solution)/shard_map/reduce_scatter | solution.py:55
  425.0 230.7 %copy-start.1 = (f32[96,128]{1,0:T(8,128)S(1)}, f32[96,128]{1,0:T(8,128)}, u32[]{:S(2)}) copy-start(f32[96,128]{1,0:T(8,128)} %reduce-scatter.9.cloned.1.call-done) | copy-start | bytes 147460
Sparse Core Ops, SparseCore 0:
  105.5 31.3 reduce-scatter.4
  233.4 65.7 reduce-scatter.6
  393.8 31.1 reduce-scatter.8
  521.3 65.8 reduce-scatter.10
where the time goes:
time: 664 us; the launch traced here: 663 us
  blocking collectives  396 us (60%)
  waiting for transfers between devices  194 us (29%)
  matrix products  37 us (6%)
  between operations  17.7 us (3%)
  other arithmetic  12.1 us (2%)
    psum x5, blocking collectives, total_norm(): return jnp.sqrt(lax.psum(jnp.sum(vector * vector), ('dp', 'mp')))  336 us
    reduce_scatter x2, waiting for transfers between devices, body(): lax.psum_scatter(jnp.dot(onehot_rows, rows_products, precision=lax.Precis...  132 us
    reduce_scatter x2, waiting for transfers between devices, adjoint(): lax.psum_scatter(cols_partial(whole), 'dp', scatter_dimension=0, tiled=True)  62.7 us
    all_gather x2, blocking collectives, adjoint(): lax.all_gather(data_vec.astype(jnp.bfloat16), 'mp', axis=0, tiled=True)  32.2 us
    all_gather x2, blocking collectives, body(): lax.all_gather(model_vec.astype(jnp.bfloat16), 'dp', axis=0, tiled=True)  27.3 us
    dot_general x2, matrix products, body(): jnp.einsum('kab,kb->ka', tile_blocks, rows_picked, preferred_element_type...  18.9 us
  transfers between devices with their start and end apart: 4, of which 4 were waited for; matrix products, arithmetic and copies ran while one was open for 0% of the time, Pallas kernels for 0%

commit v1 on v0

v1 whole, which is shorter than its diff:
```python
import functools

import jax
import jax.numpy as jnp
from jax import lax
from jax.experimental import pallas as pl
from jax.experimental.pallas import tpu as pltpu
from jax.sharding import PartitionSpec as P

BS = 128
RB = 512
CB = 768
HALF = CB // 2
CHUNK = 96
GROUP = 16
EXTRA = 16
F32 = jnp.float32
BF16 = jnp.bfloat16


def split_rows(value):
    row = lax.broadcasted_iota(jnp.int32, (EXTRA, BS), 0)
    value = jnp.broadcast_to(value, (EXTRA, BS))
    high = value.astype(BF16).astype(F32)
    rest = value - high
    middle = rest.astype(BF16).astype(F32)
    low = rest - middle
    zero = jnp.zeros_like(value)
    return jnp.where(row == 0, high, jnp.where(row == 1, middle, jnp.where(row == 2, low, zero))).astype(BF16)


def joined_rows(rows):
    return jnp.sum(rows.astype(F32), axis=0, keepdims=True)


def square_sum(x):
    return jnp.sum(jnp.sum(x * x, axis=0, keepdims=True), axis=1, keepdims=True)


def column(index):
    pieces = []
    for start in range(0, index.shape[1], BS):
        row = jnp.broadcast_to(index[:, start : start + BS].astype(F32), (BS, BS))
        pieces.append(jnp.transpose(row))
    return jnp.concatenate(pieces, 0)


def gather(source, index):
    at = column(index)
    lane = lax.broadcasted_iota(jnp.int32, at.shape, 1)
    hot = jnp.concatenate(
        [
            jnp.where(at == (lane + start).astype(F32), 1.0, 0.0).astype(BF16)
            for start in range(0, source.shape[0], BS)
        ],
        1,
    )
    return jnp.dot(hot, source, preferred_element_type=F32).astype(BF16)


def scatter(products, index, size, live):
    slots = products.shape[0]
    slot = lax.broadcasted_iota(jnp.int32, (slots, BS), 0)
    products = jnp.where(slot < live, products, 0.0)
    lane = lax.broadcasted_iota(jnp.int32, (size, slots), 1)
    row = lax.broadcasted_iota(jnp.int32, (size, slots), 0)
    hot = jnp.where((jnp.broadcast_to(index, (size, slots)) == row) & (lane < live), 1.0, 0.0).astype(BF16)
    high = products.astype(BF16)
    low = (products - high.astype(F32)).astype(BF16)
    both = jnp.dot(hot, jnp.concatenate([high, low], 1), preferred_element_type=F32)
    return both[:, :BS] + both[:, BS:]


def spread(picked):
    row = lax.broadcasted_iota(jnp.int32, (GROUP, BS), 0)
    wide = picked.astype(F32)
    return jnp.concatenate([jnp.where(row == slot, wide, 0.0).astype(BF16) for slot in range(GROUP)], 1)


def multiply(transposed, blocks_ref, picked_ref, products_ref):
    for start in range(0, picked_ref.shape[0], GROUP):
        picked = spread(picked_ref[start : start + GROUP, :])
        if transposed:
            tile = blocks_ref[start : start + GROUP].reshape(GROUP * BS, BS)
            product = jnp.dot(picked, tile, preferred_element_type=F32)
        else:
            tile = jnp.concatenate([blocks_ref[start + slot] for slot in range(GROUP)], 1)
            product = lax.dot_general(picked, tile, (((1,), (1,)), ((), ())), preferred_element_type=F32)
        products_ref[start : start + GROUP, :] = product


def adjoint_tail(live_ref, data, rows_ref, cols_ref, blocks_ref, keep_ref, send_ref, picked_ref, products_ref):
    picked_ref[...] = gather(data.astype(BF16), rows_ref[...])
    multiply(True, blocks_ref, picked_ref, products_ref)
    partial = scatter(products_ref[...], cols_ref[...], CB, live_ref[0])
    keep_ref[...] = partial[:HALF]
    send_ref[:HALF, :] = partial[HALF:].astype(BF16)
    send_ref[HALF:, :] = split_rows(square_sum(data))


def first_adjoint(
    live_ref, data_ref, rows_ref, cols_ref, blocks_ref, keep_ref, send_ref, picked_ref, products_ref
):
    adjoint_tail(
        live_ref, data_ref[...], rows_ref, cols_ref, blocks_ref, keep_ref, send_ref, picked_ref, products_ref
    )


def forward_sum(own_ref, one_ref, two_ref, three_ref):
    parts = [ref[...].astype(F32) for ref in (own_ref, one_ref, two_ref, three_ref)]
    return (parts[0] + parts[1]) + (parts[2] + parts[3])


def next_data(own_ref, one_ref, two_ref, three_ref, data_ref, beta2_ref):
    whole = forward_sum(own_ref, one_ref, two_ref, three_ref)
    alpha2 = joined_rows(whole[RB:])
    alpha = jnp.sqrt(alpha2)
    beta = jnp.sqrt(beta2_ref[0:1, :])
    return whole[:RB] / alpha - alpha * (data_ref[...] / beta), alpha2


def second_adjoint(
    live_ref,
    own_ref,
    one_ref,
    two_ref,
    three_ref,
    data_ref,
    beta2_ref,
    rows_ref,
    cols_ref,
    blocks_ref,
    next_ref,
    alpha2_ref,
    keep_ref,
    send_ref,
    picked_ref,
    products_ref,
):
    data, alpha2 = next_data(own_ref, one_ref, two_ref, three_ref, data_ref, beta2_ref)
    next_ref[...] = data
    alpha2_ref[...] = jnp.broadcast_to(alpha2, alpha2_ref.shape)
    adjoint_tail(live_ref, data, rows_ref, cols_ref, blocks_ref, keep_ref, send_ref, picked_ref, products_ref)


def chip_sum(keep_ref, send_ref, got_ref, out_ref):
    out_ref[:HALF, :] = (keep_ref[...] + got_ref[:HALF, :].astype(F32)).astype(BF16)
    out_ref[HALF:, :] = split_rows(joined_rows(send_ref[HALF:, :]) + joined_rows(got_ref[HALF:, :]))


def model_sum(own_ref, one_ref, two_ref, three_ref):
    whole = forward_sum(own_ref, one_ref, two_ref, three_ref)
    return whole[:HALF], joined_rows(whole[HALF:])


def model_out(model, beta2, model_ref, send_ref, beta2_ref):
    model_ref[...] = model
    send_ref[:HALF, :] = model.astype(BF16)
    send_ref[HALF:, :] = split_rows(square_sum(model))
    beta2_ref[...] = jnp.broadcast_to(beta2, beta2_ref.shape)


def first_model(own_ref, one_ref, two_ref, three_ref, model_ref, send_ref, beta2_ref):
    total, beta2 = model_sum(own_ref, one_ref, two_ref, three_ref)
    model_out(total / jnp.sqrt(beta2), beta2, model_ref, send_ref, beta2_ref)


def second_model(
    own_ref, one_ref, two_ref, three_ref, last_ref, alpha2_ref, model_ref, send_ref, beta2_ref
):
    total, beta2 = model_sum(own_ref, one_ref, two_ref, three_ref)
    beta = jnp.sqrt(beta2)
    last = last_ref[...] / jnp.sqrt(alpha2_ref[0:1, :])
    model_out(total / beta - beta * last, beta2, model_ref, send_ref, beta2_ref)


def forward(live_ref, own_ref, got_ref, rows_ref, cols_ref, blocks_ref, out_ref, picked_ref, products_ref):
    model = jnp.concatenate([own_ref[:HALF, :], got_ref[:HALF, :]], 0)
    picked_ref[...] = gather(model, cols_ref[...])
    multiply(False, blocks_ref, picked_ref, products_ref)
    out_ref[:RB, :] = scatter(products_ref[...], rows_ref[...], RB, live_ref[0]).astype(BF16)
    out_ref[RB:, :] = split_rows(joined_rows(own_ref[HALF:, :]) + joined_rows(got_ref[HALF:, :]))


def row_sum(own_ref, one_ref, two_ref, three_ref, out_ref):
    whole = forward_sum(own_ref, one_ref, two_ref, three_ref)
    out_ref[:RB, :] = whole[:RB].astype(BF16)
    out_ref[RB:, :] = split_rows(joined_rows(whole[RB:]))


def last_data(own_ref, one_ref, two_ref, three_ref, data_ref, beta2_ref, alpha2_ref, square_ref):
    data, alpha2 = next_data(own_ref, one_ref, two_ref, three_ref, data_ref, beta2_ref)
    alpha2_ref[...] = jnp.broadcast_to(alpha2, alpha2_ref.shape)
    square_ref[...] = jnp.broadcast_to(square_sum(data), square_ref.shape)


def finish(
    place_ref,
    own_ref,
    one_ref,
    two_ref,
    three_ref,
    beta0_ref,
    alpha0_ref,
    beta1_ref,
    alpha1_ref,
    model0_ref,
    model1_ref,
    out_ref,
):
    beta0 = jnp.sqrt(beta0_ref[0:1, :])
    alpha0 = jnp.sqrt(alpha0_ref[0:1, :])
    beta1 = jnp.sqrt(beta1_ref[0:1, :])
    alpha1 = jnp.sqrt(alpha1_ref[0:1, :])
    beta2 = jnp.sqrt(forward_sum(own_ref, one_ref, two_ref, three_ref)[0:1, :])
    chunk = pl.ds(pl.multiple_of(place_ref[0] * CHUNK, CHUNK), CHUNK)
    model0 = model0_ref[chunk, :] / alpha0
    model1 = model1_ref[chunk, :] / alpha1
    rho1 = jnp.sqrt(alpha0 * alpha0 + beta1 * beta1)
    cosine = alpha0 / rho1
    sine = beta1 / rho1
    theta = sine * alpha1
    rho_bar = -cosine * alpha1
    phi1 = cosine * beta0
    phi_bar = sine * beta0
    search = model1 - theta / rho1 * model0
    rho2 = jnp.sqrt(rho_bar * rho_bar + beta2 * beta2)
    phi2 = rho_bar / rho2 * phi_bar
    out_ref[...] = phi1 / rho1 * model0 + phi2 / rho2 * search


SCALAR = pl.BlockSpec(memory_space=pltpu.SMEM)
VECTOR = pl.BlockSpec(memory_space=pltpu.VMEM)


def call(kernel, outs, vectors, scalars=(), slots=0):
    scratch = [pltpu.VMEM((slots, BS), BF16), pltpu.VMEM((slots, BS), F32)] if slots else []
    return pl.pallas_call(
        kernel,
        out_shape=[jax.ShapeDtypeStruct((rows, BS), dtype) for rows, dtype in outs],
        in_specs=[SCALAR] * len(scalars) + [VECTOR] * len(vectors),
        out_specs=[VECTOR] * len(outs),
        scratch_shapes=scratch,
        compiler_params=pltpu.CompilerParams(vmem_limit_bytes=16 * 2**20),
        name=kernel.__name__,
    )(*scalars, *vectors)


def body(rhs, blocks, block_rows, block_cols, counts):
    slots = blocks.shape[2]
    tile = pltpu.with_memory_space_constraint(blocks[0, 0], pltpu.VMEM)
    rows = block_rows[0]
    cols = block_cols[0]
    live = counts[0]
    place = lax.axis_index("dp")
    core = place % 2
    chip = place // 2
    cols = jnp.where((cols // CHUNK) % 2 == core, 0, HALF) + cols // (2 * CHUNK) * CHUNK + cols % CHUNK

    def over_core(x):
        return lax.ppermute(x, "dp", [(i, i ^ 1) for i in range(8)])

    def over_chips(x):
        return [lax.ppermute(x, "dp", [(i, (i + 2 * hop) % 8) for i in range(8)]) for hop in (1, 2, 3)]

    def over_x(x):
        return [lax.ppermute(x, "mp", [(i, (i + 4 * hop) % 16) for i in range(16)]) for hop in (1, 2, 3)]

    def over_y(x):
        return [
            lax.ppermute(x, "mp", [(i, i // 4 * 4 + (i + hop) % 4) for i in range(16)]) for hop in (1, 2, 3)
        ]

    message = (HALF + EXTRA, BF16)
    scalar = (8, F32)
    model_outs = [(HALF, F32), message, scalar]

    def forward_whole(own):
        (part,) = call(forward, [(RB + EXTRA, BF16)], [own, over_core(own), rows, cols, tile], [live], slots)
        (part,) = call(row_sum, [(RB + EXTRA, BF16)], [part, *over_x(part)])
        return [part, *over_y(part)]

    def chips_whole(keep, send):
        (part,) = call(chip_sum, [message], [keep, send, over_core(send)])
        return [part, *over_chips(part)]

    shares = jnp.broadcast_to(rhs[None], (16, *rhs.shape))
    data0 = lax.all_to_all(shares, "mp", 0, 0).reshape(RB, BS)
    keep, send = call(first_adjoint, [(HALF, F32), message], [data0, rows, cols, tile], [live], slots)
    model0, own, beta0 = call(first_model, model_outs, chips_whole(keep, send))
    data1, alpha0, keep, send = call(
        second_adjoint,
        [(RB, F32), scalar, (HALF, F32), message],
        [*forward_whole(own), data0, beta0, rows, cols, tile],
        [live],
        slots,
    )
    model1, own, beta1 = call(second_model, model_outs, [*chips_whole(keep, send), model0, alpha0])
    alpha1, square = call(last_data, [scalar, scalar], [*forward_whole(own), data1, beta1])
    square = square + over_core(square)
    (out,) = call(
        finish,
        [(CHUNK, F32)],
        [square, *over_chips(square), beta0, alpha0, beta1, alpha1, model0, model1],
        [chip[None]],
    )
    return out


def solution(mesh):
    placed = (
        P(("dp", "mp"), None),
        P("dp", "mp", None, None, None),
        P("dp", "mp", None),
        P("dp", "mp", None),
        P("dp", "mp"),
    )
    return jax.shard_map(
        body, mesh=mesh, in_specs=placed, out_specs=P(("mp", "dp"), None), check_vma=False
    )
```

time: 664 us -> 114 us (0.17)
  blocking collectives: 396 us -> 0 us
  waiting for transfers between devices: 194 us -> 60.8 us
  matrix products: 37 us -> 0 us
  starting transfers between devices: 0.13 us -> 29.3 us
  between operations: 17.7 us -> 0.74 us
  Pallas kernels: 0 us -> 15.2 us
  other arithmetic: 12.1 us -> 0.72 us
    psum x5 -> x0, blocking collectives: 336 us -> none  [total_norm(): return jnp.sqrt(lax.psum(jnp.sum(vector * vector), ('dp', 'mp')))]
    reduce_scatter x4 -> x0, waiting for transfers between devices: 194 us -> none  [the longest x2 132 us: body(): lax.psum_scatter(jnp.dot(onehot_rows, rows_products, precision=lax.Precis...]
    all_gather x4 -> x0, blocking collectives: 59.5 us -> none  [the longest x2 32.2 us: adjoint(): lax.all_gather(data_vec.astype(jnp.bfloat16), 'mp', axis=0, tiled=True)]
    ppermute x0 -> x26, waiting for transfers between devices: none -> 54.7 us  [the longest x9 18.2 us: over_chips(): lax.ppermute(x, 'dp', [(i, (i + 2 * hop) % 8) for i in range(8)])]
    dot_general x8 -> x0, matrix products: 37 us -> none  [the longest x2 18.9 us: body(): jnp.einsum('kab,kb->ka', tile_blocks, rows_picked, preferred_element_type...]
    ppermute x0 -> x26, starting transfers between devices: none -> 21.7 us  [the longest x9 7.53 us: over_chips(): lax.ppermute(x, 'dp', [(i, (i + 2 * hop) % 8) for i in range(8)])]
    pallas_call x0 -> x12, Pallas kernels: none -> 15.2 us  [call(): pl.pallas_call(kernel, out_shape=[jax.ShapeDtypeStruct((rows, BS), dtype)...]
    all_to_all x0 -> x1, starting transfers between devices: none -> 7.58 us  [body(): data0 = lax.all_to_all(shares, 'mp', 0, 0).reshape(RB, BS)]
  transfers between devices with their start and end apart: 4 -> 27, of which waited for: 4 -> 27; matrix products, arithmetic and copies ran while one was open for 0% -> 1% of each run, Pallas kernels for 0% -> 0%
where the time goes in v1:
time: 114 us; the launch traced here: 113 us
  waiting for transfers between devices  60.8 us (53%)
  starting transfers between devices  29.3 us (26%)
  Pallas kernels  15.2 us (13%)
  local copies, waits for them, and re-layouts  6.71 us (6%)
    ppermute x9, waiting for transfers between devices, over_chips(): lax.ppermute(x, 'dp', [(i, (i + 2 * hop) % 8) for i in range(8)])  18.2 us
    ppermute x6, waiting for transfers between devices, over_x(): lax.ppermute(x, 'mp', [(i, (i + 4 * hop) % 16) for i in range(16)])  16.7 us
    pallas_call x12, Pallas kernels, call(): pl.pallas_call(kernel, out_shape=[jax.ShapeDtypeStruct((rows, BS), dtype)...  15.2 us
    ppermute x6, waiting for transfers between devices, over_y(): lax.ppermute(x, 'mp', [(i, i // 4 * 4 + (i + hop) % 4) for i in range(16)])  15.2 us
    all_to_all x1, starting transfers between devices, body(): data0 = lax.all_to_all(shares, 'mp', 0, 0).reshape(RB, BS)  7.58 us
    ppermute x9, starting transfers between devices, over_chips(): lax.ppermute(x, 'dp', [(i, (i + 2 * hop) % 8) for i in range(8)])  7.53 us
    all_to_all x1, waiting for transfers between devices, body(): data0 = lax.all_to_all(shares, 'mp', 0, 0).reshape(RB, BS)  6.08 us
    ppermute x5, starting transfers between devices, over_core(): return lax.ppermute(x, 'dp', [(i, i ^ 1) for i in range(8)])  5.55 us
  transfers between devices with their start and end apart: 27, of which 27 were waited for; matrix products, arithmetic and copies ran while one was open for 1% of the time, Pallas kernels for 0%

profile of v1, /device:TPU:1, one launch (start us, length us, event | category | flops | bytes accessed | tf_op | source)
XLA Modules:
  0.0 113.5 jit_solution(5815582048495137763)
XLA Ops:
  1.5 7.6 %all-to-all-start = ((f32[16,32,128]{2,1,0:T(8,128)}), f32[16,32,128]{2,1,0:T(8,128)S(1)}, u32[]{:S(2)}, u32[]{:S(2)}) async-start(f32[16,32,128]{2,1,0:T(8,128)} %broadcast_in_dim.16), calls=%async_computation | async-start | bytes 524288 | tf_op jit(solution)/shard_map/all_to_all | solution.py:288
  10.4 6.1 %all-to-all-done = f32[16,32,128]{2,1,0:T(8,128)S(1)} async-done(((f32[16,32,128]{2,1,0:T(8,128)}), f32[16,32,128]{2,1,0:T(8,128)S(1)}, u32[]{:S(2)}, u32[]{:S(2)}) %all-to-all-start) | async-done | bytes 262176 | tf_op jit(solution)/shard_map/all_to_all | solution.py:288
  16.5 4.6 %copy-done = bf16[1,1,384,128,128]{4,3,2,1,0:T(8,128)(2,1)S(1)} copy-done((bf16[1,1,384,128,128]{4,3,2,1,0:T(8,128)(2,1)S(1)}, bf16[1,1,384,128,128]{4,3,2,1,0:T(8,128)(2,1)}, u32[]{:S(2)}) %copy-start) | copy-done | bytes 12582936
  21.8 2.5 %first_adjoint.1 = (f32[384,128]{1,0:T(8,128)S(1)}, bf16[400,128]{1,0:T(8,128)(2,1)S(1)}) custom-call(s32[1]{0:T(128)} %bitcast.30.live_ref, f32[512,128]{1,0:T(8,128)S(1)} %bitcast.38, s32[1,384]{1,0:T(1,128)S(1)} %bitcast.40, s32[1,384]{1,0:T(1,128)S(1)} %fusion.2.cols_ref, bf16[384,128,128]{2,1,0:T(8,128)(2,1)S(1)} %bitcast.34), custom_call_target="tpu_custom_call" | custom-call | tf_op jit(solution)/shard_map/first_adjoint/pallas_call | solution.py:238
  24.2 2.1 %collective-permute-start = (bf16[400,128]{1,0:T(8,128)(2,1)S(1)}, bf16[400,128]{1,0:T(8,128)(2,1)S(1)}, u32[]{:S(2)}, u32[]{:S(2)}) collective-permute-start(bf16[400,128]{1,0:T(8,128)(2,1)S(1)} %get-tuple-element.20.send_ref), channel_id=1, source_target_pairs={{0,16},{16,0},{32,48},{48,32},{64,80},{80,64},{96,112},{112,96},{1... | collective-permute-start | bytes 307208 | tf_op jit(solution)/shard_map/ppermute | solution.py:261
  27.3 3.8 %collective-permute-start.3 = (bf16[400,128]{1,0:T(8,128)(2,1)S(1)}, bf16[400,128]{1,0:T(8,128)(2,1)S(1)}, u32[]{:S(2)}, u32[]{:S(2)}) collective-permute-start(bf16[400,128]{1,0:T(8,128)(2,1)S(1)} %chip_sum.2.own_ref), channel_id=1, source_target_pairs={{0,96},{16,112},{32,0},{48,16},{64,32},{80,48},{96,64},{112,80},{1... | collective-permute-start | bytes 307208 | tf_op jit(solution)/shard_map/ppermute | solution.py:264
  31.8 3.6 %collective-permute-done.3.three_ref = bf16[400,128]{1,0:T(8,128)(2,1)S(1)} collective-permute-done((bf16[400,128]{1,0:T(8,128)(2,1)S(1)}, bf16[400,128]{1,0:T(8,128)(2,1)S(1)}, u32[]{:S(2)}, u32[]{:S(2)}) %collective-permute-start.3) | collective-permute-done | bytes 102432 | tf_op jit(solution)/shard_map/ppermute | solution.py:264
  36.5 2.5 %collective-permute-done.1.one_ref = bf16[400,128]{1,0:T(8,128)(2,1)S(1)} collective-permute-done((bf16[400,128]{1,0:T(8,128)(2,1)S(1)}, bf16[400,128]{1,0:T(8,128)(2,1)S(1)}, u32[]{:S(2)}, u32[]{:S(2)}) %collective-permute-start.1) | collective-permute-done | bytes 102432 | tf_op jit(solution)/shard_map/ppermute | solution.py:264
  41.0 4.3 %forward.2.own_ref = bf16[528,128]{1,0:T(8,128)(2,1)S(1)} custom-call(s32[1]{0:T(128)} %bitcast.31.live_ref, bf16[400,128]{1,0:T(8,128)(2,1)S(1)} %get-tuple-element.21.own_ref, bf16[400,128]{1,0:T(8,128)(2,1)S(1)} %collective-permute-done.4.got_ref, s32[1,384]{1,0:T(1,128)S(1)} %bitcast.41, s32[1,384]{1,0:T(1,128)S(1)} %fusion.2.cols_ref, ...), custom_call_target="tpu_custom_call" | custom-call | tf_op jit(solution)/shard_map/forward/pallas_call | solution.py:238
  47.3 2.9 %collective-permute-done.7.three_ref = bf16[528,128]{1,0:T(8,128)(2,1)S(1)} collective-permute-done((bf16[528,128]{1,0:T(8,128)(2,1)S(1)}, bf16[528,128]{1,0:T(8,128)(2,1)S(1)}, u32[]{:S(2)}, u32[]{:S(2)}) %collective-permute-start.7) | collective-permute-done | bytes 135200 | tf_op jit(solution)/shard_map/ppermute | solution.py:267
  50.2 1.9 %collective-permute-done.6.two_ref = bf16[528,128]{1,0:T(8,128)(2,1)S(1)} collective-permute-done((bf16[528,128]{1,0:T(8,128)(2,1)S(1)}, bf16[528,128]{1,0:T(8,128)(2,1)S(1)}, u32[]{:S(2)}, u32[]{:S(2)}) %collective-permute-start.6) | collective-permute-done | bytes 135200 | tf_op jit(solution)/shard_map/ppermute | solution.py:267
  52.2 3.9 %collective-permute-done.5.one_ref = bf16[528,128]{1,0:T(8,128)(2,1)S(1)} collective-permute-done((bf16[528,128]{1,0:T(8,128)(2,1)S(1)}, bf16[528,128]{1,0:T(8,128)(2,1)S(1)}, u32[]{:S(2)}, u32[]{:S(2)}) %collective-permute-start.5) | collective-permute-done | bytes 135200 | tf_op jit(solution)/shard_map/ppermute | solution.py:267
  58.3 2.5 %collective-permute-done.10.three_ref = bf16[528,128]{1,0:T(8,128)(2,1)S(1)} collective-permute-done((bf16[528,128]{1,0:T(8,128)(2,1)S(1)}, bf16[528,128]{1,0:T(8,128)(2,1)S(1)}, u32[]{:S(2)}, u32[]{:S(2)}) %collective-permute-start.10) | collective-permute-done | bytes 135200 | tf_op jit(solution)/shard_map/ppermute | solution.py:271
  60.8 1.6 %collective-permute-done.9.two_ref = bf16[528,128]{1,0:T(8,128)(2,1)S(1)} collective-permute-done((bf16[528,128]{1,0:T(8,128)(2,1)S(1)}, bf16[528,128]{1,0:T(8,128)(2,1)S(1)}, u32[]{:S(2)}, u32[]{:S(2)}) %collective-permute-start.9) | collective-permute-done | bytes 135200 | tf_op jit(solution)/shard_map/ppermute | solution.py:271
  62.4 3.6 %collective-permute-done.8.one_ref = bf16[528,128]{1,0:T(8,128)(2,1)S(1)} collective-permute-done((bf16[528,128]{1,0:T(8,128)(2,1)S(1)}, bf16[528,128]{1,0:T(8,128)(2,1)S(1)}, u32[]{:S(2)}, u32[]{:S(2)}) %collective-permute-start.8) | collective-permute-done | bytes 135200 | tf_op jit(solution)/shard_map/ppermute | solution.py:271
  66.0 2.5 %second_adjoint.1 = (f32[512,128]{1,0:T(8,128)S(1)}, f32[8,128]{1,0:T(8,128)S(1)}, f32[384,128]{1,0:T(8,128)S(1)}, bf16[400,128]{1,0:T(8,128)(2,1)S(1)}) custom-call(s32[1]{0:T(128)} %bitcast.32.live_ref, bf16[528,128]{1,0:T(8,128)(2,1)S(1)} %row_sum.2.own_ref, bf16[528,128]{1,0:T(8,128)(2,1)S(1)} %collective-permute-done.8.one_ref, ...), custom_call_target="tpu_custom_call" | custom-call | tf_op jit(solution)/shard_map/second_adjoint/pallas_call | solution.py:238
  72.2 2.6 %collective-permute-done.14.three_ref = bf16[400,128]{1,0:T(8,128)(2,1)S(1)} collective-permute-done((bf16[400,128]{1,0:T(8,128)(2,1)S(1)}, bf16[400,128]{1,0:T(8,128)(2,1)S(1)}, u32[]{:S(2)}, u32[]{:S(2)}) %collective-permute-start.14) | collective-permute-done | bytes 102432 | tf_op jit(solution)/shard_map/ppermute | solution.py:264
  76.4 3.4 %collective-permute-done.12.one_ref = bf16[400,128]{1,0:T(8,128)(2,1)S(1)} collective-permute-done((bf16[400,128]{1,0:T(8,128)(2,1)S(1)}, bf16[400,128]{1,0:T(8,128)(2,1)S(1)}, u32[]{:S(2)}, u32[]{:S(2)}) %collective-permute-start.12) | collective-permute-done | bytes 102432 | tf_op jit(solution)/shard_map/ppermute | solution.py:264
  81.5 4.3 %forward.3.own_ref = bf16[528,128]{1,0:T(8,128)(2,1)S(1)} custom-call(s32[1]{0:T(128)} %bitcast.33.live_ref, bf16[400,128]{1,0:T(8,128)(2,1)S(1)} %get-tuple-element.27.own_ref, bf16[400,128]{1,0:T(8,128)(2,1)S(1)} %collective-permute-done.15.got_ref, s32[1,384]{1,0:T(1,128)S(1)} %bitcast.43, s32[1,384]{1,0:T(1,128)S(1)} %fusion.2.cols_ref, ...), custom_call_target="tpu_custom_call" | custom-call | tf_op jit(solution)/shard_map/forward/pallas_call | solution.py:238
  88.0 2.7 %collective-permute-done.18.three_ref = bf16[528,128]{1,0:T(8,128)(2,1)S(1)} collective-permute-done((bf16[528,128]{1,0:T(8,128)(2,1)S(1)}, bf16[528,128]{1,0:T(8,128)(2,1)S(1)}, u32[]{:S(2)}, u32[]{:S(2)}) %collective-permute-start.18) | collective-permute-done | bytes 135200 | tf_op jit(solution)/shard_map/ppermute | solution.py:267
  92.3 3.6 %collective-permute-done.16.one_ref = bf16[528,128]{1,0:T(8,128)(2,1)S(1)} collective-permute-done((bf16[528,128]{1,0:T(8,128)(2,1)S(1)}, bf16[528,128]{1,0:T(8,128)(2,1)S(1)}, u32[]{:S(2)}, u32[]{:S(2)}) %collective-permute-start.16) | collective-permute-done | bytes 135200 | tf_op jit(solution)/shard_map/ppermute | solution.py:267
  98.4 2.3 %collective-permute-done.21.three_ref = bf16[528,128]{1,0:T(8,128)(2,1)S(1)} collective-permute-done((bf16[528,128]{1,0:T(8,128)(2,1)S(1)}, bf16[528,128]{1,0:T(8,128)(2,1)S(1)}, u32[]{:S(2)}, u32[]{:S(2)}) %collective-permute-start.21) | collective-permute-done | bytes 135200 | tf_op jit(solution)/shard_map/ppermute | solution.py:271
  102.2 3.6 %collective-permute-done.19.one_ref = bf16[528,128]{1,0:T(8,128)(2,1)S(1)} collective-permute-done((bf16[528,128]{1,0:T(8,128)(2,1)S(1)}, bf16[528,128]{1,0:T(8,128)(2,1)S(1)}, u32[]{:S(2)}, u32[]{:S(2)}) %collective-permute-start.19) | collective-permute-done | bytes 135200 | tf_op jit(solution)/shard_map/ppermute | solution.py:271
  110.4 1.8 %collective-permute-done.24.two_ref = f32[8,128]{1,0:T(8,128)S(1)} collective-permute-done((f32[8,128]{1,0:T(8,128)S(1)}, f32[8,128]{1,0:T(8,128)S(1)}, u32[]{:S(2)}, u32[]{:S(2)}) %collective-permute-start.24) | collective-permute-done | bytes 4128 | tf_op jit(solution)/shard_map/ppermute | solution.py:264
  (53 shorter events, 32.4 us)
Async XLA Ops:
  1.5 15.0 %all-to-all-start = ((f32[16,32,128]{2,1,0:T(8,128)}), f32[16,32,128]{2,1,0:T(8,128)S(1)}, u32[]{:S(2)}, u32[]{:S(2)}) async-start(f32[16,32,128]{2,1,0:T(8,128)} %broadcast_in_dim.16), calls=%async_computation | async-start | bytes 524288 | tf_op jit(solution)/shard_map/all_to_all | solution.py:288
  24.2 3.0 %collective-permute-start = (bf16[400,128]{1,0:T(8,128)(2,1)S(1)}, bf16[400,128]{1,0:T(8,128)(2,1)S(1)}, u32[]{:S(2)}, u32[]{:S(2)}) collective-permute-start(bf16[400,128]{1,0:T(8,128)(2,1)S(1)} %get-tuple-element.20.send_ref), channel_id=1, source_target_pairs={{0,16},{16,0},{32,48},{48,32},{64,80},{80,64},{96,112},{112,96},{1... | collective-permute-start | bytes 307208 | tf_op jit(solution)/shard_map/ppermute | solution.py:261
  27.3 8.1 %collective-permute-start.3 = (bf16[400,128]{1,0:T(8,128)(2,1)S(1)}, bf16[400,128]{1,0:T(8,128)(2,1)S(1)}, u32[]{:S(2)}, u32[]{:S(2)}) collective-permute-start(bf16[400,128]{1,0:T(8,128)(2,1)S(1)} %chip_sum.2.own_ref), channel_id=1, source_target_pairs={{0,96},{16,112},{32,0},{48,16},{64,32},{80,48},{96,64},{112,80},{1... | collective-permute-start | bytes 307208 | tf_op jit(solution)/shard_map/ppermute | solution.py:264
  31.1 5.4 %collective-permute-start.2 = (bf16[400,128]{1,0:T(8,128)(2,1)S(1)}, bf16[400,128]{1,0:T(8,128)(2,1)S(1)}, u32[]{:S(2)}, u32[]{:S(2)}) collective-permute-start(bf16[400,128]{1,0:T(8,128)(2,1)S(1)} %chip_sum.2.own_ref), channel_id=1, source_target_pairs={{0,64},{16,80},{32,96},{48,112},{64,0},{80,16},{96,32},{112,48},{1... | collective-permute-start | bytes 307208 | tf_op jit(solution)/shard_map/ppermute | solution.py:264
  31.1 7.9 %collective-permute-start.1 = (bf16[400,128]{1,0:T(8,128)(2,1)S(1)}, bf16[400,128]{1,0:T(8,128)(2,1)S(1)}, u32[]{:S(2)}, u32[]{:S(2)}) collective-permute-start(bf16[400,128]{1,0:T(8,128)(2,1)S(1)} %chip_sum.2.own_ref), channel_id=1, source_target_pairs={{0,32},{16,48},{32,64},{48,80},{64,96},{80,112},{96,0},{112,16},{1... | collective-permute-start | bytes 307208 | tf_op jit(solution)/shard_map/ppermute | solution.py:264
  45.3 4.9 %collective-permute-start.7 = (bf16[528,128]{1,0:T(8,128)(2,1)S(1)}, bf16[528,128]{1,0:T(8,128)(2,1)S(1)}, u32[]{:S(2)}, u32[]{:S(2)}) collective-permute-start(bf16[528,128]{1,0:T(8,128)(2,1)S(1)} %forward.2.own_ref), channel_id=1, source_target_pairs={{0,12},{1,13},{2,14},{3,15},{4,0},{5,1},{6,2},{7,3},{8,4},{9,5},{1... | collective-permute-start | bytes 405512 | tf_op jit(solution)/shard_map/ppermute | solution.py:267
  46.1 6.0 %collective-permute-start.6 = (bf16[528,128]{1,0:T(8,128)(2,1)S(1)}, bf16[528,128]{1,0:T(8,128)(2,1)S(1)}, u32[]{:S(2)}, u32[]{:S(2)}) collective-permute-start(bf16[528,128]{1,0:T(8,128)(2,1)S(1)} %forward.2.own_ref), channel_id=1, source_target_pairs={{0,8},{1,9},{2,10},{3,11},{4,12},{5,13},{6,14},{7,15},{8,0},{9,1},... | collective-permute-start | bytes 405512 | tf_op jit(solution)/shard_map/ppermute | solution.py:267
  47.1 8.9 %collective-permute-start.5 = (bf16[528,128]{1,0:T(8,128)(2,1)S(1)}, bf16[528,128]{1,0:T(8,128)(2,1)S(1)}, u32[]{:S(2)}, u32[]{:S(2)}) collective-permute-start(bf16[528,128]{1,0:T(8,128)(2,1)S(1)} %forward.2.own_ref), channel_id=1, source_target_pairs={{0,4},{1,5},{2,6},{3,7},{4,8},{5,9},{6,10},{7,11},{8,12},{9,13},{1... | collective-permute-start | bytes 405512 | tf_op jit(solution)/shard_map/ppermute | solution.py:267
  56.1 4.7 %collective-permute-start.10 = (bf16[528,128]{1,0:T(8,128)(2,1)S(1)}, bf16[528,128]{1,0:T(8,128)(2,1)S(1)}, u32[]{:S(2)}, u32[]{:S(2)}) collective-permute-start(bf16[528,128]{1,0:T(8,128)(2,1)S(1)} %row_sum.2.own_ref), channel_id=1, source_target_pairs={{0,3},{1,0},{2,1},{3,2},{4,7},{5,4},{6,5},{7,6},{8,11},{9,8},{10,9... | collective-permute-start | bytes 405512 | tf_op jit(solution)/shard_map/ppermute | solution.py:271
  56.7 5.7 %collective-permute-start.9 = (bf16[528,128]{1,0:T(8,128)(2,1)S(1)}, bf16[528,128]{1,0:T(8,128)(2,1)S(1)}, u32[]{:S(2)}, u32[]{:S(2)}) collective-permute-start(bf16[528,128]{1,0:T(8,128)(2,1)S(1)} %row_sum.2.own_ref), channel_id=1, source_target_pairs={{0,2},{1,3},{2,0},{3,1},{4,6},{5,7},{6,4},{7,5},{8,10},{9,11},{10,... | collective-permute-start | bytes 405512 | tf_op jit(solution)/shard_map/ppermute | solution.py:271
  58.3 7.7 %collective-permute-start.8 = (bf16[528,128]{1,0:T(8,128)(2,1)S(1)}, bf16[528,128]{1,0:T(8,128)(2,1)S(1)}, u32[]{:S(2)}, u32[]{:S(2)}) collective-permute-start(bf16[528,128]{1,0:T(8,128)(2,1)S(1)} %row_sum.2.own_ref), channel_id=1, source_target_pairs={{0,1},{1,2},{2,3},{3,0},{4,5},{5,6},{6,7},{7,4},{8,9},{9,10},{10,1... | collective-permute-start | bytes 405512 | tf_op jit(solution)/shard_map/ppermute | solution.py:271
  68.5 2.1 %collective-permute-start.11 = (bf16[400,128]{1,0:T(8,128)(2,1)S(1)}, bf16[400,128]{1,0:T(8,128)(2,1)S(1)}, u32[]{:S(2)}, u32[]{:S(2)}) collective-permute-start(bf16[400,128]{1,0:T(8,128)(2,1)S(1)} %get-tuple-element.24.send_ref), channel_id=1, source_target_pairs={{0,16},{16,0},{32,48},{48,32},{64,80},{80,64},{96,112},{112,96},{1... | collective-permute-start | bytes 307208 | tf_op jit(solution)/shard_map/ppermute | solution.py:261
  70.6 4.2 %collective-permute-start.14 = (bf16[400,128]{1,0:T(8,128)(2,1)S(1)}, bf16[400,128]{1,0:T(8,128)(2,1)S(1)}, u32[]{:S(2)}, u32[]{:S(2)}) collective-permute-start(bf16[400,128]{1,0:T(8,128)(2,1)S(1)} %chip_sum.3.own_ref), channel_id=1, source_target_pairs={{0,96},{16,112},{32,0},{48,16},{64,32},{80,48},{96,64},{112,80},{1... | collective-permute-start | bytes 307208 | tf_op jit(solution)/shard_map/ppermute | solution.py:264
  71.3 5.1 %collective-permute-start.13 = (bf16[400,128]{1,0:T(8,128)(2,1)S(1)}, bf16[400,128]{1,0:T(8,128)(2,1)S(1)}, u32[]{:S(2)}, u32[]{:S(2)}) collective-permute-start(bf16[400,128]{1,0:T(8,128)(2,1)S(1)} %chip_sum.3.own_ref), channel_id=1, source_target_pairs={{0,64},{16,80},{32,96},{48,112},{64,0},{80,16},{96,32},{112,48},{1... | collective-permute-start | bytes 307208 | tf_op jit(solution)/shard_map/ppermute | solution.py:264
  71.3 8.5 %collective-permute-start.12 = (bf16[400,128]{1,0:T(8,128)(2,1)S(1)}, bf16[400,128]{1,0:T(8,128)(2,1)S(1)}, u32[]{:S(2)}, u32[]{:S(2)}) collective-permute-start(bf16[400,128]{1,0:T(8,128)(2,1)S(1)} %chip_sum.3.own_ref), channel_id=1, source_target_pairs={{0,32},{16,48},{32,64},{48,80},{64,96},{80,112},{96,0},{112,16},{1... | collective-permute-start | bytes 307208 | tf_op jit(solution)/shard_map/ppermute | solution.py:264
  85.8 4.9 %collective-permute-start.18 = (bf16[528,128]{1,0:T(8,128)(2,1)S(1)}, bf16[528,128]{1,0:T(8,128)(2,1)S(1)}, u32[]{:S(2)}, u32[]{:S(2)}) collective-permute-start(bf16[528,128]{1,0:T(8,128)(2,1)S(1)} %forward.3.own_ref), channel_id=1, source_target_pairs={{0,12},{1,13},{2,14},{3,15},{4,0},{5,1},{6,2},{7,3},{8,4},{9,5},{1... | collective-permute-start | bytes 405512 | tf_op jit(solution)/shard_map/ppermute | solution.py:267
  85.9 6.4 %collective-permute-start.17 = (bf16[528,128]{1,0:T(8,128)(2,1)S(1)}, bf16[528,128]{1,0:T(8,128)(2,1)S(1)}, u32[]{:S(2)}, u32[]{:S(2)}) collective-permute-start(bf16[528,128]{1,0:T(8,128)(2,1)S(1)} %forward.3.own_ref), channel_id=1, source_target_pairs={{0,8},{1,9},{2,10},{3,11},{4,12},{5,13},{6,14},{7,15},{8,0},{9,1},... | collective-permute-start | bytes 405512 | tf_op jit(solution)/shard_map/ppermute | solution.py:267
  87.2 8.7 %collective-permute-start.16 = (bf16[528,128]{1,0:T(8,128)(2,1)S(1)}, bf16[528,128]{1,0:T(8,128)(2,1)S(1)}, u32[]{:S(2)}, u32[]{:S(2)}) collective-permute-start(bf16[528,128]{1,0:T(8,128)(2,1)S(1)} %forward.3.own_ref), channel_id=1, source_target_pairs={{0,4},{1,5},{2,6},{3,7},{4,8},{5,9},{6,10},{7,11},{8,12},{9,13},{1... | collective-permute-start | bytes 405512 | tf_op jit(solution)/shard_map/ppermute | solution.py:267
  96.0 4.7 %collective-permute-start.21 = (bf16[528,128]{1,0:T(8,128)(2,1)S(1)}, bf16[528,128]{1,0:T(8,128)(2,1)S(1)}, u32[]{:S(2)}, u32[]{:S(2)}) collective-permute-start(bf16[528,128]{1,0:T(8,128)(2,1)S(1)} %row_sum.3.own_ref), channel_id=1, source_target_pairs={{0,3},{1,0},{2,1},{3,2},{4,7},{5,4},{6,5},{7,6},{8,11},{9,8},{10,9... | collective-permute-start | bytes 405512 | tf_op jit(solution)/shard_map/ppermute | solution.py:271
  96.4 5.8 %collective-permute-start.20 = (bf16[528,128]{1,0:T(8,128)(2,1)S(1)}, bf16[528,128]{1,0:T(8,128)(2,1)S(1)}, u32[]{:S(2)}, u32[]{:S(2)}) collective-permute-start(bf16[528,128]{1,0:T(8,128)(2,1)S(1)} %row_sum.3.own_ref), channel_id=1, source_target_pairs={{0,2},{1,3},{2,0},{3,1},{4,6},{5,7},{6,4},{7,5},{8,10},{9,11},{10,... | collective-permute-start | bytes 405512 | tf_op jit(solution)/shard_map/ppermute | solution.py:271
  97.9 7.9 %collective-permute-start.19 = (bf16[528,128]{1,0:T(8,128)(2,1)S(1)}, bf16[528,128]{1,0:T(8,128)(2,1)S(1)}, u32[]{:S(2)}, u32[]{:S(2)}) collective-permute-start(bf16[528,128]{1,0:T(8,128)(2,1)S(1)} %row_sum.3.own_ref), channel_id=1, source_target_pairs={{0,1},{1,2},{2,3},{3,0},{4,5},{5,6},{6,7},{7,4},{8,9},{9,10},{10,1... | collective-permute-start | bytes 405512 | tf_op jit(solution)/shard_map/ppermute | solution.py:271
  108.0 2.5 %collective-permute-start.25 = (f32[8,128]{1,0:T(8,128)S(1)}, f32[8,128]{1,0:T(8,128)S(1)}, u32[]{:S(2)}, u32[]{:S(2)}) collective-permute-start(f32[8,128]{1,0:T(8,128)S(1)} %add.71.own_ref), channel_id=1, source_target_pairs={{0,96},{16,112},{32,0},{48,16},{64,32},{80,48},{96,64},{112,80},{1... | collective-permute-start | bytes 12296 | tf_op jit(solution)/shard_map/ppermute | solution.py:264
  108.2 4.0 %collective-permute-start.24 = (f32[8,128]{1,0:T(8,128)S(1)}, f32[8,128]{1,0:T(8,128)S(1)}, u32[]{:S(2)}, u32[]{:S(2)}) collective-permute-start(f32[8,128]{1,0:T(8,128)S(1)} %add.71.own_ref), channel_id=1, source_target_pairs={{0,64},{16,80},{32,96},{48,112},{64,0},{80,16},{96,32},{112,48},{1... | collective-permute-start | bytes 12296 | tf_op jit(solution)/shard_map/ppermute | solution.py:264
  108.4 4.4 %collective-permute-start.23 = (f32[8,128]{1,0:T(8,128)S(1)}, f32[8,128]{1,0:T(8,128)S(1)}, u32[]{:S(2)}, u32[]{:S(2)}) collective-permute-start(f32[8,128]{1,0:T(8,128)S(1)} %add.71.own_ref), channel_id=1, source_target_pairs={{0,32},{16,48},{32,64},{48,80},{64,96},{80,112},{96,0},{112,16},{1... | collective-permute-start | bytes 12296 | tf_op jit(solution)/shard_map/ppermute | solution.py:264
  (7 other events, 70.6 us)

commit v2 on v1

--- a/solution.py
+++ b/solution.py
@@ -14,8 +14,16 @@
 CHUNK = 96
 GROUP = 16
 EXTRA = 16
+LOADS = 8
+SHARE = 32
+NEAR = (1, 3)
+FAR = (3, 1)
 F32 = jnp.float32
 BF16 = jnp.bfloat16
+
+
+def square(other_x, other_y):
+    return 4 * other_x, other_y, 4 * other_x + other_y
 
 
 def split_rows(value):
@@ -77,32 +85,50 @@
     return jnp.concatenate([jnp.where(row == slot, wide, 0.0).astype(BF16) for slot in range(GROUP)], 1)
 
 
-def multiply(transposed, blocks_ref, picked_ref, products_ref):
-    for start in range(0, picked_ref.shape[0], GROUP):
-        picked = spread(picked_ref[start : start + GROUP, :])
-        if transposed:
-            tile = blocks_ref[start : start + GROUP].reshape(GROUP * BS, BS)
-            product = jnp.dot(picked, tile, preferred_element_type=F32)
-        else:
-            tile = jnp.concatenate([blocks_ref[start + slot] for slot in range(GROUP)], 1)
-            product = lax.dot_general(picked, tile, (((1,), (1,)), ((), ())), preferred_element_type=F32)
-        products_ref[start : start + GROUP, :] = product
-
-
-def adjoint_tail(live_ref, data, rows_ref, cols_ref, blocks_ref, keep_ref, send_ref, picked_ref, products_ref):
+def multiply(blocks_refs, picked_ref, products_ref):
+    base = 0
+    for ref in blocks_refs:
+        for start in range(0, ref.shape[0], GROUP):
+            slots = slice(base + start, base + start + GROUP)
+            tile = ref[start : start + GROUP].reshape(GROUP * BS, BS)
+            products_ref[slots, :] = jnp.dot(spread(picked_ref[slots, :]), tile, preferred_element_type=F32)
+        base += ref.shape[0]
+
+
+def adjoint_tail(live_ref, data, rows_ref, cols_ref, blocks_refs, keep_ref, send_ref, picked_ref, products_ref):
     picked_ref[...] = gather(data.astype(BF16), rows_ref[...])
-    multiply(True, blocks_ref, picked_ref, products_ref)
-    partial = scatter(products_ref[...], cols_ref[...], CB, live_ref[0])
+    multiply(blocks_refs, picked_ref, products_ref)
+    partial = scatter(products_ref[...], cols_ref[...], CB, live_ref[0, 0])
     keep_ref[...] = partial[:HALF]
     send_ref[:HALF, :] = partial[HALF:].astype(BF16)
     send_ref[HALF:, :] = split_rows(square_sum(data))
 
 
 def first_adjoint(
-    live_ref, data_ref, rows_ref, cols_ref, blocks_ref, keep_ref, send_ref, picked_ref, products_ref
+    live_ref,
+    place_ref,
+    own_ref,
+    one_ref,
+    two_ref,
+    three_ref,
+    rows_ref,
+    cols_ref,
+    first_ref,
+    second_ref,
+    data_ref,
+    keep_ref,
+    send_ref,
+    picked_ref,
+    products_ref,
 ):
+    near, far = square(*NEAR), square(*FAR)
+    for step, ref in zip((0, *far), (own_ref, one_ref, two_ref, three_ref)):
+        for piece, hop in enumerate((0, *near)):
+            at = pl.multiple_of((place_ref[0] ^ step ^ hop) * SHARE, SHARE)
+            data_ref[pl.ds(at, SHARE), :] = ref[piece * SHARE : (piece + 1) * SHARE, :]
+    blocks_refs = (first_ref, second_ref)
     adjoint_tail(
-        live_ref, data_ref[...], rows_ref, cols_ref, blocks_ref, keep_ref, send_ref, picked_ref, products_ref
+        live_ref, data_ref[...], rows_ref, cols_ref, blocks_refs, keep_ref, send_ref, picked_ref, products_ref
     )
 
 
@@ -129,7 +155,8 @@
     beta2_ref,
     rows_ref,
     cols_ref,
-    blocks_ref,
+    first_ref,
+    second_ref,
     next_ref,
     alpha2_ref,
     keep_ref,
@@ -140,7 +167,8 @@
     data, alpha2 = next_data(own_ref, one_ref, two_ref, three_ref, data_ref, beta2_ref)
     next_ref[...] = data
     alpha2_ref[...] = jnp.broadcast_to(alpha2, alpha2_ref.shape)
-    adjoint_tail(live_ref, data, rows_ref, cols_ref, blocks_ref, keep_ref, send_ref, picked_ref, products_ref)
+    blocks_refs = (first_ref, second_ref)
+    adjoint_tail(live_ref, data, rows_ref, cols_ref, blocks_refs, keep_ref, send_ref, picked_ref, products_ref)
 
 
 def chip_sum(keep_ref, send_ref, got_ref, out_ref):
@@ -160,7 +188,7 @@
     beta2_ref[...] = jnp.broadcast_to(beta2, beta2_ref.shape)
 
 
-def first_model(own_ref, one_ref, two_ref, three_ref, model_ref, send_ref, beta2_ref):
+def first_model(own_ref, one_ref, two_ref, three_ref, turned_ref, model_ref, send_ref, beta2_ref):
     total, beta2 = model_sum(own_ref, one_ref, two_ref, three_ref)
     model_out(total / jnp.sqrt(beta2), beta2, model_ref, send_ref, beta2_ref)
 
@@ -177,8 +205,8 @@
 def forward(live_ref, own_ref, got_ref, rows_ref, cols_ref, blocks_ref, out_ref, picked_ref, products_ref):
     model = jnp.concatenate([own_ref[:HALF, :], got_ref[:HALF, :]], 0)
     picked_ref[...] = gather(model, cols_ref[...])
-    multiply(False, blocks_ref, picked_ref, products_ref)
-    out_ref[:RB, :] = scatter(products_ref[...], rows_ref[...], RB, live_ref[0]).astype(BF16)
+    multiply((blocks_ref,), picked_ref, products_ref)
+    out_ref[:RB, :] = scatter(products_ref[...], rows_ref[...], RB, live_ref[0, 0]).astype(BF16)
     out_ref[RB:, :] = split_rows(joined_rows(own_ref[HALF:, :]) + joined_rows(got_ref[HALF:, :]))
 
 
@@ -194,8 +222,12 @@
     square_ref[...] = jnp.broadcast_to(square_sum(data), square_ref.shape)
 
 
+def add(own_ref, got_ref, out_ref):
+    out_ref[...] = own_ref[...] + got_ref[...]
+
+
 def finish(
-    place_ref,
+    chip_ref,
     own_ref,
     one_ref,
     two_ref,
@@ -213,7 +245,7 @@
     beta1 = jnp.sqrt(beta1_ref[0:1, :])
     alpha1 = jnp.sqrt(alpha1_ref[0:1, :])
     beta2 = jnp.sqrt(forward_sum(own_ref, one_ref, two_ref, three_ref)[0:1, :])
-    chunk = pl.ds(pl.multiple_of(place_ref[0] * CHUNK, CHUNK), CHUNK)
+    chunk = pl.ds(pl.multiple_of(chip_ref[0] * CHUNK, CHUNK), CHUNK)
     model0 = model0_ref[chunk, :] / alpha0
     model1 = model1_ref[chunk, :] / alpha1
     rho1 = jnp.sqrt(alpha0 * alpha0 + beta1 * beta1)
@@ -229,6 +261,76 @@
     out_ref[...] = phi1 / rho1 * model0 + phi2 / rho2 * search
 
 
+def read(blocks_ref, tile_ref, sems, first):
+    pieces = sems.shape[0]
+    size = tile_ref.shape[0] // pieces
+    return [
+        pltpu.make_async_copy(
+            blocks_ref.at[pl.ds(first + piece * size, size)],
+            tile_ref.at[pl.ds(piece * size, size)],
+            sems.at[piece],
+        )
+        for piece in range(pieces)
+    ]
+
+
+def load_first(
+    core_ref,
+    chip_ref,
+    place_ref,
+    live_ref,
+    data_ref,
+    rows_ref,
+    cols_ref,
+    blocks_ref,
+    data_out,
+    rows_out,
+    cols_out,
+    tile_ref,
+    held_ref,
+    small_sems,
+    sems,
+):
+    small = [
+        pltpu.make_async_copy(cols_ref, held_ref, small_sems.at[0]),
+        pltpu.make_async_copy(rows_ref, rows_out, small_sems.at[1]),
+        pltpu.make_async_copy(data_ref, data_out, small_sems.at[2]),
+    ]
+    large = read(blocks_ref, tile_ref, sems, 0)
+    for copy in small + large:
+        copy.start()
+    small[0].wait()
+    cols = held_ref[...]
+    chunk = jnp.zeros_like(cols)
+    for edge in range(CHUNK, CB, CHUNK):
+        chunk += jnp.where(cols >= edge, 1, 0)
+    half = jnp.where((chunk & 1) == core_ref[0], 0, HALF)
+    cols_out[...] = half + (chunk >> 1) * CHUNK + cols - chunk * CHUNK
+    for copy in small[1:] + large:
+        copy.wait()
+
+
+def load_second(after_ref, blocks_ref, tile_ref, sems):
+    large = read(blocks_ref, tile_ref, sems, tile_ref.shape[0])
+    for copy in large:
+        copy.start()
+    for copy in large:
+        copy.wait()
+
+
+def transpose(after_ref, first_ref, second_ref, out_ref):
+    half = first_ref.shape[0]
+    for slot in range(half):
+        out_ref[slot] = jnp.transpose(first_ref[slot])
+        out_ref[half + slot] = jnp.transpose(second_ref[slot])
+
+
+def collect(own_ref, one_ref, two_ref, three_ref, after_ref, out_ref):
+    size = own_ref.shape[0]
+    for piece, ref in enumerate((own_ref, one_ref, two_ref, three_ref)):
+        out_ref[piece * size : (piece + 1) * size, :] = ref[...]
+
+
 SCALAR = pl.BlockSpec(memory_space=pltpu.SMEM)
 VECTOR = pl.BlockSpec(memory_space=pltpu.VMEM)
 
@@ -248,14 +350,10 @@
 
 def body(rhs, blocks, block_rows, block_cols, counts):
     slots = blocks.shape[2]
-    tile = pltpu.with_memory_space_constraint(blocks[0, 0], pltpu.VMEM)
-    rows = block_rows[0]
-    cols = block_cols[0]
-    live = counts[0]
-    place = lax.axis_index("dp")
-    core = place % 2
-    chip = place // 2
-    cols = jnp.where((cols // CHUNK) % 2 == core, 0, HALF) + cols // (2 * CHUNK) * CHUNK + cols % CHUNK
+    group = lax.axis_index("dp")
+    core = (group & 1)[None]
+    chip = (group >> 1)[None]
+    place = lax.axis_index("mp")[None]
 
     def over_core(x):
         return lax.ppermute(x, "dp", [(i, i ^ 1) for i in range(8)])
@@ -263,46 +361,96 @@
     def over_chips(x):
         return [lax.ppermute(x, "dp", [(i, (i + 2 * hop) % 8) for i in range(8)]) for hop in (1, 2, 3)]
 
-    def over_x(x):
-        return [lax.ppermute(x, "mp", [(i, (i + 4 * hop) % 16) for i in range(16)]) for hop in (1, 2, 3)]
-
-    def over_y(x):
-        return [
-            lax.ppermute(x, "mp", [(i, i // 4 * 4 + (i + hop) % 4) for i in range(16)]) for hop in (1, 2, 3)
-        ]
+    def over_square(x, others):
+        return [lax.ppermute(x, "mp", [(i, i ^ step) for i in range(16)]) for step in square(*others)]
 
     message = (HALF + EXTRA, BF16)
     scalar = (8, F32)
     model_outs = [(HALF, F32), message, scalar]
 
+    lies = pl.BlockSpec(memory_space=pltpu.HBM)
+    inputs = [
+        pltpu.with_memory_space_constraint(x, pltpu.HBM) for x in (rhs, block_rows[0], block_cols[0], blocks[0, 0])
+    ]
+    tile_shape = pltpu.VMEM((slots // 2, BS, BS), BF16)
+    params = pltpu.CompilerParams(vmem_limit_bytes=16 * 2**20)
+    cost = pl.CostEstimate(flops=0, bytes_accessed=slots * BS * BS * 2, transcendentals=0)
+    data, rows, cols, first = pl.pallas_call(
+        load_first,
+        out_shape=[
+            jax.ShapeDtypeStruct(rhs.shape, F32),
+            jax.ShapeDtypeStruct((1, slots), jnp.int32),
+            jax.ShapeDtypeStruct((1, slots), jnp.int32),
+            tile_shape,
+        ],
+        in_specs=[SCALAR] * 4 + [lies] * 4,
+        out_specs=[VECTOR] * 4,
+        scratch_shapes=[
+            pltpu.VMEM((1, slots), jnp.int32),
+            pltpu.SemaphoreType.DMA((3,)),
+            pltpu.SemaphoreType.DMA((LOADS,)),
+        ],
+        compiler_params=params,
+        cost_estimate=cost,
+        name="load_first",
+    )(core, chip, place, counts, *inputs)
+    first = pltpu.with_memory_space_constraint(first, pltpu.VMEM)
+    (quarter,) = call(collect, [(4 * SHARE, F32)], [data, *over_square(rhs, NEAR), first])
+    second = pl.pallas_call(
+        load_second,
+        out_shape=tile_shape,
+        in_specs=[VECTOR, lies],
+        out_specs=VECTOR,
+        scratch_shapes=[pltpu.SemaphoreType.DMA((LOADS,))],
+        compiler_params=params,
+        cost_estimate=cost,
+        name="load_second",
+    )(quarter, inputs[-1])
+    second = pltpu.with_memory_space_constraint(second, pltpu.VMEM)
+
     def forward_whole(own):
-        (part,) = call(forward, [(RB + EXTRA, BF16)], [own, over_core(own), rows, cols, tile], [live], slots)
-        (part,) = call(row_sum, [(RB + EXTRA, BF16)], [part, *over_x(part)])
-        return [part, *over_y(part)]
-
-    def chips_whole(keep, send):
-        (part,) = call(chip_sum, [message], [keep, send, over_core(send)])
+        (part,) = call(forward, [(RB + EXTRA, BF16)], [own, over_core(own), rows, cols, turned], [counts], slots)
+        (part,) = call(row_sum, [(RB + EXTRA, BF16)], [part, *over_square(part, NEAR)])
+        return [part, *over_square(part, FAR)]
+
+    def chips_whole(part):
         return [part, *over_chips(part)]
 
-    shares = jnp.broadcast_to(rhs[None], (16, *rhs.shape))
-    data0 = lax.all_to_all(shares, "mp", 0, 0).reshape(RB, BS)
-    keep, send = call(first_adjoint, [(HALF, F32), message], [data0, rows, cols, tile], [live], slots)
-    model0, own, beta0 = call(first_model, model_outs, chips_whole(keep, send))
+    data0, keep, send = call(
+        first_adjoint,
+        [(RB, F32), (HALF, F32), message],
+        [quarter, *over_square(quarter, FAR), rows, cols, first, second],
+        [counts, place],
+        slots,
+    )
+    (part,) = call(chip_sum, [message], [keep, send, over_core(send)])
+    turned = pl.pallas_call(
+        transpose,
+        out_shape=pltpu.VMEM((slots, BS, BS), BF16),
+        in_specs=[VECTOR] * 3,
+        out_specs=VECTOR,
+        compiler_params=params,
+        cost_estimate=cost,
+        name="transpose",
+    )(part, first, second)
+    turned = pltpu.with_memory_space_constraint(turned, pltpu.VMEM)
+    model0, own, beta0 = call(first_model, model_outs, [*chips_whole(part), turned])
     data1, alpha0, keep, send = call(
         second_adjoint,
         [(RB, F32), scalar, (HALF, F32), message],
-        [*forward_whole(own), data0, beta0, rows, cols, tile],
-        [live],
+        [*forward_whole(own), data0, beta0, rows, cols, first, second],
+        [counts],
         slots,
     )
-    model1, own, beta1 = call(second_model, model_outs, [*chips_whole(keep, send), model0, alpha0])
-    alpha1, square = call(last_data, [scalar, scalar], [*forward_whole(own), data1, beta1])
-    square = square + over_core(square)
+    (part,) = call(chip_sum, [message], [keep, send, over_core(send)])
+    model1, own, beta1 = call(second_model, model_outs, [*chips_whole(part), model0, alpha0])
+    alpha1, total = call(last_data, [scalar, scalar], [*forward_whole(own), data1, beta1])
+    (total,) = call(add, [scalar], [total, over_core(total)])
     (out,) = call(
         finish,
         [(CHUNK, F32)],
-        [square, *over_chips(square), beta0, alpha0, beta1, alpha1, model0, model1],
-        [chip[None]],
+        [total, *over_chips(total), beta0, alpha0, beta1, alpha1, model0, model1],
+        [chip],
     )
     return out
 

time: 114 us -> 104 us (0.912)
  waiting for transfers between devices: 60.8 us -> 41.4 us
  starting transfers between devices: 29.3 us -> 41 us
  local copies, waits for them, and re-layouts: 6.71 us -> 0 us
  Pallas kernels: 15.2 us -> 20.8 us
    ppermute x12 -> x18, starting transfers between devices: 8.64 us -> 24.4 us  [over_square(): lax.ppermute(x, 'mp', [(i, i ^ step) for i in range(16)])]
    ppermute x12 -> x18, waiting for transfers between devices: 31.9 us -> 21.8 us  [over_square(): lax.ppermute(x, 'mp', [(i, i ^ step) for i in range(16)])]
    pallas_call x0 -> x3, Pallas kernels: none -> 9.07 us  [the longest x1 3.28 us: body(): pl.pallas_call(transpose, out_shape=pltpu.VMEM((slots, BS, BS), BF16), in...]
    all_to_all x1 -> x0, starting transfers between devices: 7.58 us -> none  [body(): data0 = lax.all_to_all(shares, 'mp', 0, 0).reshape(RB, BS)]
    all_to_all x1 -> x0, waiting for transfers between devices: 6.08 us -> none  [body(): data0 = lax.all_to_all(shares, 'mp', 0, 0).reshape(RB, BS)]
    unnamed x8 -> x0, local copies, waits for them, and re-layouts: 5.26 us -> none
    ppermute x5, starting transfers between devices: 5.55 us -> 9.12 us  [over_core(): return lax.ppermute(x, 'dp', [(i, i ^ 1) for i in range(8)])]
    pallas_call x12 -> x14, Pallas kernels: 15.2 us -> 11.8 us  [call(): pl.pallas_call(kernel, out_shape=[jax.ShapeDtypeStruct((rows, BS), dtype)...]
  transfers between devices with their start and end apart: 27 -> 32, of which waited for: 27 -> 25; matrix products, arithmetic and copies ran while one was open for 1% -> 0% of each run, Pallas kernels for 0% -> 9%
where the time goes in v2:
time: 104 us
  waiting for transfers between devices  41.4 us (40%)
  starting transfers between devices  41 us (39%)
  Pallas kernels  20.8 us (20%)
    ppermute x18, starting transfers between devices, over_square(): lax.ppermute(x, 'mp', [(i, i ^ step) for i in range(16)])  24.4 us
    ppermute x18, waiting for transfers between devices, over_square(): lax.ppermute(x, 'mp', [(i, i ^ step) for i in range(16)])  21.8 us
    ppermute x9, waiting for transfers between devices, over_chips(): lax.ppermute(x, 'dp', [(i, (i + 2 * hop) % 8) for i in range(8)])  14.9 us
    pallas_call x14, Pallas kernels, call(): pl.pallas_call(kernel, out_shape=[jax.ShapeDtypeStruct((rows, BS), dtype)...  11.8 us
    ppermute x5, starting transfers between devices, over_core(): return lax.ppermute(x, 'dp', [(i, i ^ 1) for i in range(8)])  9.12 us
    ppermute x9, starting transfers between devices, over_chips(): lax.ppermute(x, 'dp', [(i, (i + 2 * hop) % 8) for i in range(8)])  7.53 us
    ppermute x5, waiting for transfers between devices, over_core(): return lax.ppermute(x, 'dp', [(i, i ^ 1) for i in range(8)])  4.62 us
    pallas_call x1, Pallas kernels, body(): pl.pallas_call(transpose, out_shape=pltpu.VMEM((slots, BS, BS), BF16), in...  3.28 us
  transfers between devices with their start and end apart: 32, of which 25 were waited for; matrix products, arithmetic and copies ran while one was open for 0% of the time, Pallas kernels for 9%

profile of v2, /device:TPU:1, one launch (start us, length us, event | category | flops | bytes accessed | tf_op | source)
XLA Modules:
  0.0 104.0 jit_solution(70667414424699176)
XLA Ops:
  2.0 2.7 %collective-permute-start.2 = (f32[32,128]{1,0:T(8,128)}, f32[32,128]{1,0:T(8,128)S(1)}, u32[]{:S(2)}, u32[]{:S(2)}) collective-permute-start(f32[32,128]{1,0:T(8,128)} %data_ref.1), channel_id=1, source_target_pairs={{0,7},{1,6},{2,5},{3,4},{4,3},{5,2},{6,1},{7,0},{8,15},{9,14},{10,... | collective-permute-start | bytes 49160 | tf_op jit(solution)/shard_map/ppermute | solution.py:365
  5.4 2.9 %load_first.1 = (f32[32,128]{1,0:T(8,128)S(1)}, s32[1,384]{1,0:T(1,128)S(1)}, s32[1,384]{1,0:T(1,128)S(1)}, bf16[192,128,128]{2,1,0:T(8,128)(2,1)S(1)}) custom-call(s32[1]{0:T(128)} %bitcast.2.core_ref, s32[1]{0:T(128)} %bitcast.chip_ref, s32[1]{0:T(128)} %bitcast.1.place_ref, s32[1,1]{1,0:T(1,128)S(6)} %copy.6.live_ref, f32[32,128]{1,0:T(8,128)} %data_ref.1, ...), custom_call_target="tpu_custom_call" | custom-call | bytes 12582912 | tf_op jit(solution)/shard_map/load_first/pallas_call | solution.py:378
  12.6 2.9 %load_second.1.second_ref = bf16[192,128,128]{2,1,0:T(8,128)(2,1)S(1)} custom-call(f32[128,128]{1,0:T(8,128)S(1)} %collect.1.after_ref.own_ref, bf16[384,128,128]{2,1,0:T(8,128)(2,1)} %bitcast.7), custom_call_target="tpu_custom_call" | custom-call | bytes 12582912 | tf_op jit(solution)/shard_map/load_second/pallas_call | solution.py:399
  17.0 2.5 %first_adjoint.1 = (f32[512,128]{1,0:T(8,128)S(1)}, f32[384,128]{1,0:T(8,128)S(1)}, bf16[400,128]{1,0:T(8,128)(2,1)S(1)}) custom-call(s32[1,1]{1,0:T(1,128)S(6)} %copy.6.live_ref, s32[1]{0:T(128)} %bitcast.1.place_ref, f32[128,128]{1,0:T(8,128)S(1)} %collect.1.after_ref.own_ref, f32[128,128]{1,0:T(8,128)S(1)} %collective-permute-done.3.one_ref, ...), custom_call_target="tpu_custom_call" | custom-call | tf_op jit(solution)/shard_map/first_adjoint/pallas_call | solution.py:340
  19.5 3.9 %collective-permute-start.6 = (bf16[400,128]{1,0:T(8,128)(2,1)S(1)}, bf16[400,128]{1,0:T(8,128)(2,1)S(1)}, u32[]{:S(2)}, u32[]{:S(2)}) collective-permute-start(bf16[400,128]{1,0:T(8,128)(2,1)S(1)} %get-tuple-element.29.send_ref), channel_id=1, source_target_pairs={{0,16},{16,0},{32,48},{48,32},{64,80},{80,64},{96,112},{112,96},{1... | collective-permute-start | bytes 307208 | tf_op jit(solution)/shard_map/ppermute | solution.py:359
  24.4 3.8 %collective-permute-start.9 = (bf16[400,128]{1,0:T(8,128)(2,1)S(1)}, bf16[400,128]{1,0:T(8,128)(2,1)S(1)}, u32[]{:S(2)}, u32[]{:S(2)}) collective-permute-start(bf16[400,128]{1,0:T(8,128)(2,1)S(1)} %chip_sum.2.after_ref.own_ref), channel_id=1, source_target_pairs={{0,96},{16,112},{32,0},{48,16},{64,32},{80,48},{96,64},{112,80},{1... | collective-permute-start | bytes 307208 | tf_op jit(solution)/shard_map/ppermute | solution.py:362
  28.9 3.3 %transpose.1.turned_ref.blocks_ref = bf16[384,128,128]{2,1,0:T(8,128)(2,1)S(1)} custom-call(bf16[400,128]{1,0:T(8,128)(2,1)S(1)} %chip_sum.2.after_ref.own_ref, bf16[192,128,128]{2,1,0:T(8,128)(2,1)S(1)} %get-tuple-element.25.after_ref.first_ref, bf16[192,128,128]{2,1,0:T(8,128)(2,1)S(1)} %load_second.1.second_ref), custom_call_target="tpu_custom_call" | custom-call | bytes 12582912 | tf_op jit(solution)/shard_map/transpose/pallas_call | solution.py:427
  33.6 2.5 %collective-permute-done.7.one_ref = bf16[400,128]{1,0:T(8,128)(2,1)S(1)} collective-permute-done((bf16[400,128]{1,0:T(8,128)(2,1)S(1)}, bf16[400,128]{1,0:T(8,128)(2,1)S(1)}, u32[]{:S(2)}, u32[]{:S(2)}) %collective-permute-start.7) | collective-permute-done | bytes 102432 | tf_op jit(solution)/shard_map/ppermute | solution.py:362
  38.1 2.6 %forward.2.own_ref = bf16[528,128]{1,0:T(8,128)(2,1)S(1)} custom-call(s32[1,1]{1,0:T(1,128)S(6)} %copy.6.live_ref, bf16[400,128]{1,0:T(8,128)(2,1)S(1)} %get-tuple-element.30.own_ref, bf16[400,128]{1,0:T(8,128)(2,1)S(1)} %collective-permute-done.10.got_ref, s32[1,384]{1,0:T(1,128)S(1)} %get-tuple-element.26.rows_ref, ...), custom_call_target="tpu_custom_call" | custom-call | tf_op jit(solution)/shard_map/forward/pallas_call | solution.py:340
  42.5 2.1 %collective-permute-start.11 = (bf16[528,128]{1,0:T(8,128)(2,1)S(1)}, bf16[528,128]{1,0:T(8,128)(2,1)S(1)}, u32[]{:S(2)}, u32[]{:S(2)}) collective-permute-start(bf16[528,128]{1,0:T(8,128)(2,1)S(1)} %forward.2.own_ref), channel_id=1, source_target_pairs={{0,4},{1,5},{2,6},{3,7},{4,0},{5,1},{6,2},{7,3},{8,12},{9,13},{10,... | collective-permute-start | bytes 405512 | tf_op jit(solution)/shard_map/ppermute | solution.py:365
  44.6 3.1 %collective-permute-done.13.three_ref = bf16[528,128]{1,0:T(8,128)(2,1)S(1)} collective-permute-done((bf16[528,128]{1,0:T(8,128)(2,1)S(1)}, bf16[528,128]{1,0:T(8,128)(2,1)S(1)}, u32[]{:S(2)}, u32[]{:S(2)}) %collective-permute-start.13) | collective-permute-done | bytes 135200 | tf_op jit(solution)/shard_map/ppermute | solution.py:365
  47.7 2.3 %collective-permute-done.12.two_ref = bf16[528,128]{1,0:T(8,128)(2,1)S(1)} collective-permute-done((bf16[528,128]{1,0:T(8,128)(2,1)S(1)}, bf16[528,128]{1,0:T(8,128)(2,1)S(1)}, u32[]{:S(2)}, u32[]{:S(2)}) %collective-permute-start.12) | collective-permute-done | bytes 135200 | tf_op jit(solution)/shard_map/ppermute | solution.py:365
  54.0 2.2 %collective-permute-done.16.three_ref = bf16[528,128]{1,0:T(8,128)(2,1)S(1)} collective-permute-done((bf16[528,128]{1,0:T(8,128)(2,1)S(1)}, bf16[528,128]{1,0:T(8,128)(2,1)S(1)}, u32[]{:S(2)}, u32[]{:S(2)}) %collective-permute-start.16) | collective-permute-done | bytes 135200 | tf_op jit(solution)/shard_map/ppermute | solution.py:365
  57.6 2.5 %second_adjoint.1 = (f32[512,128]{1,0:T(8,128)S(1)}, f32[8,128]{1,0:T(8,128)S(1)}, f32[384,128]{1,0:T(8,128)S(1)}, bf16[400,128]{1,0:T(8,128)(2,1)S(1)}) custom-call(s32[1,1]{1,0:T(1,128)S(6)} %copy.6.live_ref, bf16[528,128]{1,0:T(8,128)(2,1)S(1)} %row_sum.2.own_ref, bf16[528,128]{1,0:T(8,128)(2,1)S(1)} %collective-permute-done.14.one_ref, ...), custom_call_target="tpu_custom_call" | custom-call | tf_op jit(solution)/shard_map/second_adjoint/pallas_call | solution.py:340
  60.1 2.3 %collective-permute-start.17 = (bf16[400,128]{1,0:T(8,128)(2,1)S(1)}, bf16[400,128]{1,0:T(8,128)(2,1)S(1)}, u32[]{:S(2)}, u32[]{:S(2)}) collective-permute-start(bf16[400,128]{1,0:T(8,128)(2,1)S(1)} %get-tuple-element.34.send_ref), channel_id=1, source_target_pairs={{0,16},{16,0},{32,48},{48,32},{64,80},{80,64},{96,112},{112,96},{1... | collective-permute-start | bytes 307208 | tf_op jit(solution)/shard_map/ppermute | solution.py:359
  65.0 2.6 %collective-permute-done.20.three_ref = bf16[400,128]{1,0:T(8,128)(2,1)S(1)} collective-permute-done((bf16[400,128]{1,0:T(8,128)(2,1)S(1)}, bf16[400,128]{1,0:T(8,128)(2,1)S(1)}, u32[]{:S(2)}, u32[]{:S(2)}) %collective-permute-start.20) | collective-permute-done | bytes 102432 | tf_op jit(solution)/shard_map/ppermute | solution.py:362
  69.2 3.4 %collective-permute-done.18.one_ref = bf16[400,128]{1,0:T(8,128)(2,1)S(1)} collective-permute-done((bf16[400,128]{1,0:T(8,128)(2,1)S(1)}, bf16[400,128]{1,0:T(8,128)(2,1)S(1)}, u32[]{:S(2)}, u32[]{:S(2)}) %collective-permute-start.18) | collective-permute-done | bytes 102432 | tf_op jit(solution)/shard_map/ppermute | solution.py:362
  74.3 2.5 %forward.3.own_ref = bf16[528,128]{1,0:T(8,128)(2,1)S(1)} custom-call(s32[1,1]{1,0:T(1,128)S(6)} %copy.6.live_ref, bf16[400,128]{1,0:T(8,128)(2,1)S(1)} %get-tuple-element.37.own_ref, bf16[400,128]{1,0:T(8,128)(2,1)S(1)} %collective-permute-done.21.got_ref, s32[1,384]{1,0:T(1,128)S(1)} %get-tuple-element.26.rows_ref, ...), custom_call_target="tpu_custom_call" | custom-call | tf_op jit(solution)/shard_map/forward/pallas_call | solution.py:340
  78.4 2.4 %collective-permute-start.22 = (bf16[528,128]{1,0:T(8,128)(2,1)S(1)}, bf16[528,128]{1,0:T(8,128)(2,1)S(1)}, u32[]{:S(2)}, u32[]{:S(2)}) collective-permute-start(bf16[528,128]{1,0:T(8,128)(2,1)S(1)} %forward.3.own_ref), channel_id=1, source_target_pairs={{0,4},{1,5},{2,6},{3,7},{4,0},{5,1},{6,2},{7,3},{8,12},{9,13},{10,... | collective-permute-start | bytes 405512 | tf_op jit(solution)/shard_map/ppermute | solution.py:365
  80.8 3.1 %collective-permute-done.24.three_ref = bf16[528,128]{1,0:T(8,128)(2,1)S(1)} collective-permute-done((bf16[528,128]{1,0:T(8,128)(2,1)S(1)}, bf16[528,128]{1,0:T(8,128)(2,1)S(1)}, u32[]{:S(2)}, u32[]{:S(2)}) %collective-permute-start.24) | collective-permute-done | bytes 135200 | tf_op jit(solution)/shard_map/ppermute | solution.py:365
  83.9 2.2 %collective-permute-done.23.two_ref = bf16[528,128]{1,0:T(8,128)(2,1)S(1)} collective-permute-done((bf16[528,128]{1,0:T(8,128)(2,1)S(1)}, bf16[528,128]{1,0:T(8,128)(2,1)S(1)}, u32[]{:S(2)}, u32[]{:S(2)}) %collective-permute-start.23) | collective-permute-done | bytes 135200 | tf_op jit(solution)/shard_map/ppermute | solution.py:365
  87.3 2.1 %collective-permute-start.26 = (bf16[528,128]{1,0:T(8,128)(2,1)S(1)}, bf16[528,128]{1,0:T(8,128)(2,1)S(1)}, u32[]{:S(2)}, u32[]{:S(2)}) collective-permute-start(bf16[528,128]{1,0:T(8,128)(2,1)S(1)} %row_sum.3.own_ref), channel_id=1, source_target_pairs={{0,1},{1,0},{2,3},{3,2},{4,5},{5,4},{6,7},{7,6},{8,9},{9,8},{10,11... | collective-permute-start | bytes 405512 | tf_op jit(solution)/shard_map/ppermute | solution.py:365
  90.2 2.2 %collective-permute-done.27.three_ref = bf16[528,128]{1,0:T(8,128)(2,1)S(1)} collective-permute-done((bf16[528,128]{1,0:T(8,128)(2,1)S(1)}, bf16[528,128]{1,0:T(8,128)(2,1)S(1)}, u32[]{:S(2)}, u32[]{:S(2)}) %collective-permute-start.27) | collective-permute-done | bytes 135200 | tf_op jit(solution)/shard_map/ppermute | solution.py:365
  92.4 3.3 %collective-permute-done.26.two_ref = bf16[528,128]{1,0:T(8,128)(2,1)S(1)} collective-permute-done((bf16[528,128]{1,0:T(8,128)(2,1)S(1)}, bf16[528,128]{1,0:T(8,128)(2,1)S(1)}, u32[]{:S(2)}, u32[]{:S(2)}) %collective-permute-start.26) | collective-permute-done | bytes 135200 | tf_op jit(solution)/shard_map/ppermute | solution.py:365
  (57 shorter events, 37.7 us)
Async XLA Ops:
  0.0 8.4 %collective-permute-start = (f32[32,128]{1,0:T(8,128)}, f32[32,128]{1,0:T(8,128)S(1)}, u32[]{:S(2)}, u32[]{:S(2)}) collective-permute-start(f32[32,128]{1,0:T(8,128)} %data_ref.1), channel_id=1, source_target_pairs={{0,4},{1,5},{2,6},{3,7},{4,0},{5,1},{6,2},{7,3},{8,12},{9,13},{10,... | collective-permute-start | bytes 49160 | tf_op jit(solution)/shard_map/ppermute | solution.py:365
  2.0 6.3 %collective-permute-start.2 = (f32[32,128]{1,0:T(8,128)}, f32[32,128]{1,0:T(8,128)S(1)}, u32[]{:S(2)}, u32[]{:S(2)}) collective-permute-start(f32[32,128]{1,0:T(8,128)} %data_ref.1), channel_id=1, source_target_pairs={{0,7},{1,6},{2,5},{3,4},{4,3},{5,2},{6,1},{7,0},{8,15},{9,14},{10,... | collective-permute-start | bytes 49160 | tf_op jit(solution)/shard_map/ppermute | solution.py:365
  8.8 6.7 %collective-permute-start.5 = (f32[128,128]{1,0:T(8,128)S(1)}, f32[128,128]{1,0:T(8,128)S(1)}, u32[]{:S(2)}, u32[]{:S(2)}) collective-permute-start(f32[128,128]{1,0:T(8,128)S(1)} %collect.1.after_ref.own_ref), channel_id=1, source_target_pairs={{0,13},{1,12},{2,15},{3,14},{4,9},{5,8},{6,11},{7,10},{8,5},{9,4},... | collective-permute-start | bytes 196616 | tf_op jit(solution)/shard_map/ppermute | solution.py:365
  10.7 4.8 %collective-permute-start.4 = (f32[128,128]{1,0:T(8,128)S(1)}, f32[128,128]{1,0:T(8,128)S(1)}, u32[]{:S(2)}, u32[]{:S(2)}) collective-permute-start(f32[128,128]{1,0:T(8,128)S(1)} %collect.1.after_ref.own_ref), channel_id=1, source_target_pairs={{0,1},{1,0},{2,3},{3,2},{4,5},{5,4},{6,7},{7,6},{8,9},{9,8},{10,11... | collective-permute-start | bytes 196616 | tf_op jit(solution)/shard_map/ppermute | solution.py:365
  12.4 4.6 %collective-permute-start.3 = (f32[128,128]{1,0:T(8,128)S(1)}, f32[128,128]{1,0:T(8,128)S(1)}, u32[]{:S(2)}, u32[]{:S(2)}) collective-permute-start(f32[128,128]{1,0:T(8,128)S(1)} %collect.1.after_ref.own_ref), channel_id=1, source_target_pairs={{0,12},{1,13},{2,14},{3,15},{4,8},{5,9},{6,10},{7,11},{8,4},{9,5},... | collective-permute-start | bytes 196616 | tf_op jit(solution)/shard_map/ppermute | solution.py:365
  19.5 4.8 %collective-permute-start.6 = (bf16[400,128]{1,0:T(8,128)(2,1)S(1)}, bf16[400,128]{1,0:T(8,128)(2,1)S(1)}, u32[]{:S(2)}, u32[]{:S(2)}) collective-permute-start(bf16[400,128]{1,0:T(8,128)(2,1)S(1)} %get-tuple-element.29.send_ref), channel_id=1, source_target_pairs={{0,16},{16,0},{32,48},{48,32},{64,80},{80,64},{96,112},{112,96},{1... | collective-permute-start | bytes 307208 | tf_op jit(solution)/shard_map/ppermute | solution.py:359
  24.4 8.1 %collective-permute-start.9 = (bf16[400,128]{1,0:T(8,128)(2,1)S(1)}, bf16[400,128]{1,0:T(8,128)(2,1)S(1)}, u32[]{:S(2)}, u32[]{:S(2)}) collective-permute-start(bf16[400,128]{1,0:T(8,128)(2,1)S(1)} %chip_sum.2.after_ref.own_ref), channel_id=1, source_target_pairs={{0,96},{16,112},{32,0},{48,16},{64,32},{80,48},{96,64},{112,80},{1... | collective-permute-start | bytes 307208 | tf_op jit(solution)/shard_map/ppermute | solution.py:362
  28.2 5.4 %collective-permute-start.8 = (bf16[400,128]{1,0:T(8,128)(2,1)S(1)}, bf16[400,128]{1,0:T(8,128)(2,1)S(1)}, u32[]{:S(2)}, u32[]{:S(2)}) collective-permute-start(bf16[400,128]{1,0:T(8,128)(2,1)S(1)} %chip_sum.2.after_ref.own_ref), channel_id=1, source_target_pairs={{0,64},{16,80},{32,96},{48,112},{64,0},{80,16},{96,32},{112,48},{1... | collective-permute-start | bytes 307208 | tf_op jit(solution)/shard_map/ppermute | solution.py:362
  28.2 7.9 %collective-permute-start.7 = (bf16[400,128]{1,0:T(8,128)(2,1)S(1)}, bf16[400,128]{1,0:T(8,128)(2,1)S(1)}, u32[]{:S(2)}, u32[]{:S(2)}) collective-permute-start(bf16[400,128]{1,0:T(8,128)(2,1)S(1)} %chip_sum.2.after_ref.own_ref), channel_id=1, source_target_pairs={{0,32},{16,48},{32,64},{48,80},{64,96},{80,112},{96,0},{112,16},{1... | collective-permute-start | bytes 307208 | tf_op jit(solution)/shard_map/ppermute | solution.py:362
  40.7 7.0 %collective-permute-start.13 = (bf16[528,128]{1,0:T(8,128)(2,1)S(1)}, bf16[528,128]{1,0:T(8,128)(2,1)S(1)}, u32[]{:S(2)}, u32[]{:S(2)}) collective-permute-start(bf16[528,128]{1,0:T(8,128)(2,1)S(1)} %forward.2.own_ref), channel_id=1, source_target_pairs={{0,7},{1,6},{2,5},{3,4},{4,3},{5,2},{6,1},{7,0},{8,15},{9,14},{10,... | collective-permute-start | bytes 405512 | tf_op jit(solution)/shard_map/ppermute | solution.py:365
  40.7 9.3 %collective-permute-start.12 = (bf16[528,128]{1,0:T(8,128)(2,1)S(1)}, bf16[528,128]{1,0:T(8,128)(2,1)S(1)}, u32[]{:S(2)}, u32[]{:S(2)}) collective-permute-start(bf16[528,128]{1,0:T(8,128)(2,1)S(1)} %forward.2.own_ref), channel_id=1, source_target_pairs={{0,3},{1,2},{2,1},{3,0},{4,7},{5,6},{6,5},{7,4},{8,11},{9,10},{10,... | collective-permute-start | bytes 405512 | tf_op jit(solution)/shard_map/ppermute | solution.py:365
  42.5 7.5 %collective-permute-start.11 = (bf16[528,128]{1,0:T(8,128)(2,1)S(1)}, bf16[528,128]{1,0:T(8,128)(2,1)S(1)}, u32[]{:S(2)}, u32[]{:S(2)}) collective-permute-start(bf16[528,128]{1,0:T(8,128)(2,1)S(1)} %forward.2.own_ref), channel_id=1, source_target_pairs={{0,4},{1,5},{2,6},{3,7},{4,0},{5,1},{6,2},{7,3},{8,12},{9,13},{10,... | collective-permute-start | bytes 405512 | tf_op jit(solution)/shard_map/ppermute | solution.py:365
  50.1 6.2 %collective-permute-start.16 = (bf16[528,128]{1,0:T(8,128)(2,1)S(1)}, bf16[528,128]{1,0:T(8,128)(2,1)S(1)}, u32[]{:S(2)}, u32[]{:S(2)}) collective-permute-start(bf16[528,128]{1,0:T(8,128)(2,1)S(1)} %row_sum.2.own_ref), channel_id=1, source_target_pairs={{0,13},{1,12},{2,15},{3,14},{4,9},{5,8},{6,11},{7,10},{8,5},{9,4},... | collective-permute-start | bytes 405512 | tf_op jit(solution)/shard_map/ppermute | solution.py:365
  50.2 6.9 %collective-permute-start.15 = (bf16[528,128]{1,0:T(8,128)(2,1)S(1)}, bf16[528,128]{1,0:T(8,128)(2,1)S(1)}, u32[]{:S(2)}, u32[]{:S(2)}) collective-permute-start(bf16[528,128]{1,0:T(8,128)(2,1)S(1)} %row_sum.2.own_ref), channel_id=1, source_target_pairs={{0,1},{1,0},{2,3},{3,2},{4,5},{5,4},{6,7},{7,6},{8,9},{9,8},{10,11... | collective-permute-start | bytes 405512 | tf_op jit(solution)/shard_map/ppermute | solution.py:365
  52.3 5.4 %collective-permute-start.14 = (bf16[528,128]{1,0:T(8,128)(2,1)S(1)}, bf16[528,128]{1,0:T(8,128)(2,1)S(1)}, u32[]{:S(2)}, u32[]{:S(2)}) collective-permute-start(bf16[528,128]{1,0:T(8,128)(2,1)S(1)} %row_sum.2.own_ref), channel_id=1, source_target_pairs={{0,12},{1,13},{2,14},{3,15},{4,8},{5,9},{6,10},{7,11},{8,4},{9,5},... | collective-permute-start | bytes 405512 | tf_op jit(solution)/shard_map/ppermute | solution.py:365
  64.1 5.1 %collective-permute-start.19 = (bf16[400,128]{1,0:T(8,128)(2,1)S(1)}, bf16[400,128]{1,0:T(8,128)(2,1)S(1)}, u32[]{:S(2)}, u32[]{:S(2)}) collective-permute-start(bf16[400,128]{1,0:T(8,128)(2,1)S(1)} %chip_sum.3.own_ref), channel_id=1, source_target_pairs={{0,64},{16,80},{32,96},{48,112},{64,0},{80,16},{96,32},{112,48},{1... | collective-permute-start | bytes 307208 | tf_op jit(solution)/shard_map/ppermute | solution.py:362
  64.1 8.5 %collective-permute-start.18 = (bf16[400,128]{1,0:T(8,128)(2,1)S(1)}, bf16[400,128]{1,0:T(8,128)(2,1)S(1)}, u32[]{:S(2)}, u32[]{:S(2)}) collective-permute-start(bf16[400,128]{1,0:T(8,128)(2,1)S(1)} %chip_sum.3.own_ref), channel_id=1, source_target_pairs={{0,32},{16,48},{32,64},{48,80},{64,96},{80,112},{96,0},{112,16},{1... | collective-permute-start | bytes 307208 | tf_op jit(solution)/shard_map/ppermute | solution.py:362
  76.9 7.0 %collective-permute-start.24 = (bf16[528,128]{1,0:T(8,128)(2,1)S(1)}, bf16[528,128]{1,0:T(8,128)(2,1)S(1)}, u32[]{:S(2)}, u32[]{:S(2)}) collective-permute-start(bf16[528,128]{1,0:T(8,128)(2,1)S(1)} %forward.3.own_ref), channel_id=1, source_target_pairs={{0,7},{1,6},{2,5},{3,4},{4,3},{5,2},{6,1},{7,0},{8,15},{9,14},{10,... | collective-permute-start | bytes 405512 | tf_op jit(solution)/shard_map/ppermute | solution.py:365
  77.2 8.9 %collective-permute-start.23 = (bf16[528,128]{1,0:T(8,128)(2,1)S(1)}, bf16[528,128]{1,0:T(8,128)(2,1)S(1)}, u32[]{:S(2)}, u32[]{:S(2)}) collective-permute-start(bf16[528,128]{1,0:T(8,128)(2,1)S(1)} %forward.3.own_ref), channel_id=1, source_target_pairs={{0,3},{1,2},{2,1},{3,0},{4,7},{5,6},{6,5},{7,4},{8,11},{9,10},{10,... | collective-permute-start | bytes 405512 | tf_op jit(solution)/shard_map/ppermute | solution.py:365
  78.4 7.7 %collective-permute-start.22 = (bf16[528,128]{1,0:T(8,128)(2,1)S(1)}, bf16[528,128]{1,0:T(8,128)(2,1)S(1)}, u32[]{:S(2)}, u32[]{:S(2)}) collective-permute-start(bf16[528,128]{1,0:T(8,128)(2,1)S(1)} %forward.3.own_ref), channel_id=1, source_target_pairs={{0,4},{1,5},{2,6},{3,7},{4,0},{5,1},{6,2},{7,3},{8,12},{9,13},{10,... | collective-permute-start | bytes 405512 | tf_op jit(solution)/shard_map/ppermute | solution.py:365
  86.2 6.2 %collective-permute-start.27 = (bf16[528,128]{1,0:T(8,128)(2,1)S(1)}, bf16[528,128]{1,0:T(8,128)(2,1)S(1)}, u32[]{:S(2)}, u32[]{:S(2)}) collective-permute-start(bf16[528,128]{1,0:T(8,128)(2,1)S(1)} %row_sum.3.own_ref), channel_id=1, source_target_pairs={{0,13},{1,12},{2,15},{3,14},{4,9},{5,8},{6,11},{7,10},{8,5},{9,4},... | collective-permute-start | bytes 405512 | tf_op jit(solution)/shard_map/ppermute | solution.py:365
  87.3 8.4 %collective-permute-start.26 = (bf16[528,128]{1,0:T(8,128)(2,1)S(1)}, bf16[528,128]{1,0:T(8,128)(2,1)S(1)}, u32[]{:S(2)}, u32[]{:S(2)}) collective-permute-start(bf16[528,128]{1,0:T(8,128)(2,1)S(1)} %row_sum.3.own_ref), channel_id=1, source_target_pairs={{0,1},{1,0},{2,3},{3,2},{4,5},{5,4},{6,7},{7,6},{8,9},{9,8},{10,11... | collective-permute-start | bytes 405512 | tf_op jit(solution)/shard_map/ppermute | solution.py:365
  89.3 6.4 %collective-permute-start.25 = (bf16[528,128]{1,0:T(8,128)(2,1)S(1)}, bf16[528,128]{1,0:T(8,128)(2,1)S(1)}, u32[]{:S(2)}, u32[]{:S(2)}) collective-permute-start(bf16[528,128]{1,0:T(8,128)(2,1)S(1)} %row_sum.3.own_ref), channel_id=1, source_target_pairs={{0,12},{1,13},{2,14},{3,15},{4,8},{5,9},{6,10},{7,11},{8,4},{9,5},... | collective-permute-start | bytes 405512 | tf_op jit(solution)/shard_map/ppermute | solution.py:365
  98.9 4.4 %collective-permute-start.29 = (f32[8,128]{1,0:T(8,128)S(1)}, f32[8,128]{1,0:T(8,128)S(1)}, u32[]{:S(2)}, u32[]{:S(2)}) collective-permute-start(f32[8,128]{1,0:T(8,128)S(1)} %add.1.own_ref), channel_id=1, source_target_pairs={{0,32},{16,48},{32,64},{48,80},{64,96},{80,112},{96,0},{112,16},{1... | collective-permute-start | bytes 12296 | tf_op jit(solution)/shard_map/ppermute | solution.py:362
  (8 other events, 23.5 us)

commit v3 on v2

--- a/solution.py
+++ b/solution.py
@@ -23,7 +23,7 @@
 
 
 def square(other_x, other_y):
-    return 4 * other_x, other_y, 4 * other_x + other_y
+    return other_y, 4 * other_x, 4 * other_x + other_y
 
 
 def split_rows(value):
@@ -53,26 +53,28 @@
     return jnp.concatenate(pieces, 0)
 
 
-def gather(source, index):
+def picker(index, size):
     at = column(index)
     lane = lax.broadcasted_iota(jnp.int32, at.shape, 1)
-    hot = jnp.concatenate(
+    return jnp.concatenate(
         [
             jnp.where(at == (lane + start).astype(F32), 1.0, 0.0).astype(BF16)
-            for start in range(0, source.shape[0], BS)
+            for start in range(0, size, BS)
         ],
         1,
     )
-    return jnp.dot(hot, source, preferred_element_type=F32).astype(BF16)
-
-
-def scatter(products, index, size, live):
-    slots = products.shape[0]
-    slot = lax.broadcasted_iota(jnp.int32, (slots, BS), 0)
-    products = jnp.where(slot < live, products, 0.0)
+
+
+def adder(index, size, live):
+    slots = index.shape[1]
     lane = lax.broadcasted_iota(jnp.int32, (size, slots), 1)
     row = lax.broadcasted_iota(jnp.int32, (size, slots), 0)
-    hot = jnp.where((jnp.broadcast_to(index, (size, slots)) == row) & (lane < live), 1.0, 0.0).astype(BF16)
+    return jnp.where((jnp.broadcast_to(index, (size, slots)) == row) & (lane < live), 1.0, 0.0).astype(BF16)
+
+
+def scatter(products, hot, live):
+    slot = lax.broadcasted_iota(jnp.int32, products.shape, 0)
+    products = jnp.where(slot < live, products, 0.0)
     high = products.astype(BF16)
     low = (products - high.astype(F32)).astype(BF16)
     both = jnp.dot(hot, jnp.concatenate([high, low], 1), preferred_element_type=F32)
@@ -95,10 +97,10 @@
         base += ref.shape[0]
 
 
-def adjoint_tail(live_ref, data, rows_ref, cols_ref, blocks_refs, keep_ref, send_ref, picked_ref, products_ref):
-    picked_ref[...] = gather(data.astype(BF16), rows_ref[...])
+def adjoint_tail(live, data, pick, hot, blocks_refs, keep_ref, send_ref, picked_ref, products_ref):
+    picked_ref[...] = jnp.dot(pick, data.astype(BF16), preferred_element_type=F32).astype(BF16)
     multiply(blocks_refs, picked_ref, products_ref)
-    partial = scatter(products_ref[...], cols_ref[...], CB, live_ref[0, 0])
+    partial = scatter(products_ref[...], hot, live)
     keep_ref[...] = partial[:HALF]
     send_ref[:HALF, :] = partial[HALF:].astype(BF16)
     send_ref[HALF:, :] = split_rows(square_sum(data))
@@ -116,6 +118,8 @@
     first_ref,
     second_ref,
     data_ref,
+    pick_ref,
+    hot_ref,
     keep_ref,
     send_ref,
     picked_ref,
@@ -126,10 +130,13 @@
         for piece, hop in enumerate((0, *near)):
             at = pl.multiple_of((place_ref[0] ^ step ^ hop) * SHARE, SHARE)
             data_ref[pl.ds(at, SHARE), :] = ref[piece * SHARE : (piece + 1) * SHARE, :]
+    live = live_ref[0, 0]
+    pick = picker(rows_ref[...], RB)
+    hot = adder(cols_ref[...], CB, live)
+    pick_ref[...] = pick
+    hot_ref[...] = hot
     blocks_refs = (first_ref, second_ref)
-    adjoint_tail(
-        live_ref, data_ref[...], rows_ref, cols_ref, blocks_refs, keep_ref, send_ref, picked_ref, products_ref
-    )
+    adjoint_tail(live, data_ref[...], pick, hot, blocks_refs, keep_ref, send_ref, picked_ref, products_ref)
 
 
 def forward_sum(own_ref, one_ref, two_ref, three_ref):
@@ -153,8 +160,8 @@
     three_ref,
     data_ref,
     beta2_ref,
-    rows_ref,
-    cols_ref,
+    pick_ref,
+    hot_ref,
     first_ref,
     second_ref,
     next_ref,
@@ -168,7 +175,9 @@
     next_ref[...] = data
     alpha2_ref[...] = jnp.broadcast_to(alpha2, alpha2_ref.shape)
     blocks_refs = (first_ref, second_ref)
-    adjoint_tail(live_ref, data, rows_ref, cols_ref, blocks_refs, keep_ref, send_ref, picked_ref, products_ref)
+    adjoint_tail(
+        live_ref[0, 0], data, pick_ref[...], hot_ref[...], blocks_refs, keep_ref, send_ref, picked_ref, products_ref
+    )
 
 
 def chip_sum(keep_ref, send_ref, got_ref, out_ref):
@@ -202,11 +211,11 @@
     model_out(total / beta - beta * last, beta2, model_ref, send_ref, beta2_ref)
 
 
-def forward(live_ref, own_ref, got_ref, rows_ref, cols_ref, blocks_ref, out_ref, picked_ref, products_ref):
+def forward(live_ref, own_ref, got_ref, pick_ref, hot_ref, blocks_ref, out_ref, picked_ref, products_ref):
     model = jnp.concatenate([own_ref[:HALF, :], got_ref[:HALF, :]], 0)
-    picked_ref[...] = gather(model, cols_ref[...])
+    picked_ref[...] = jnp.dot(pick_ref[...], model, preferred_element_type=F32).astype(BF16)
     multiply((blocks_ref,), picked_ref, products_ref)
-    out_ref[:RB, :] = scatter(products_ref[...], rows_ref[...], RB, live_ref[0, 0]).astype(BF16)
+    out_ref[:RB, :] = scatter(products_ref[...], hot_ref[...], live_ref[0, 0]).astype(BF16)
     out_ref[RB:, :] = split_rows(joined_rows(own_ref[HALF:, :]) + joined_rows(got_ref[HALF:, :]))
 
 
@@ -318,7 +327,9 @@
         copy.wait()
 
 
-def transpose(after_ref, first_ref, second_ref, out_ref):
+def transpose(live_ref, after_ref, rows_ref, cols_ref, first_ref, second_ref, out_ref, pick_ref, hot_ref):
+    pick_ref[...] = picker(cols_ref[...], CB)
+    hot_ref[...] = adder(rows_ref[...], RB, live_ref[0, 0])
     half = first_ref.shape[0]
     for slot in range(half):
         out_ref[slot] = jnp.transpose(first_ref[slot])
@@ -339,7 +350,7 @@
     scratch = [pltpu.VMEM((slots, BS), BF16), pltpu.VMEM((slots, BS), F32)] if slots else []
     return pl.pallas_call(
         kernel,
-        out_shape=[jax.ShapeDtypeStruct((rows, BS), dtype) for rows, dtype in outs],
+        out_shape=[jax.ShapeDtypeStruct((rows, *(width or (BS,))), dtype) for rows, dtype, *width in outs],
         in_specs=[SCALAR] * len(scalars) + [VECTOR] * len(vectors),
         out_specs=[VECTOR] * len(outs),
         scratch_shapes=scratch,
@@ -359,10 +370,22 @@
         return lax.ppermute(x, "dp", [(i, i ^ 1) for i in range(8)])
 
     def over_chips(x):
-        return [lax.ppermute(x, "dp", [(i, (i + 2 * hop) % 8) for i in range(8)]) for hop in (1, 2, 3)]
+        steps = ((1, 3), (3, 1), (2, 2))
+        return [
+            lax.ppermute(x, "dp", [(i, (i >> 1 ^ step[i & 1]) * 2 + (i & 1)) for i in range(8)]) for step in steps
+        ]
 
     def over_square(x, others):
-        return [lax.ppermute(x, "mp", [(i, i ^ step) for i in range(16)]) for step in square(*others)]
+        steps = zip(square(*others), square(*others[::-1]))
+        return [
+            lax.ppermute(
+                x, ("dp", "mp"), [(i * 16 + j, i * 16 + (j ^ step[i & 1])) for i in range(8) for j in range(16)]
+            )
+            for step in steps
+        ]
+
+    def over_places(x, others):
+        return [lax.ppermute(x, "mp", [(j, j ^ step) for j in range(16)]) for step in square(*others)]
 
     message = (HALF + EXTRA, BF16)
     scalar = (8, F32)
@@ -395,7 +418,7 @@
         name="load_first",
     )(core, chip, place, counts, *inputs)
     first = pltpu.with_memory_space_constraint(first, pltpu.VMEM)
-    (quarter,) = call(collect, [(4 * SHARE, F32)], [data, *over_square(rhs, NEAR), first])
+    (quarter,) = call(collect, [(4 * SHARE, F32)], [data, *over_places(rhs, NEAR), first])
     second = pl.pallas_call(
         load_second,
         out_shape=tile_shape,
@@ -409,36 +432,40 @@
     second = pltpu.with_memory_space_constraint(second, pltpu.VMEM)
 
     def forward_whole(own):
-        (part,) = call(forward, [(RB + EXTRA, BF16)], [own, over_core(own), rows, cols, turned], [counts], slots)
+        (part,) = call(forward, [(RB + EXTRA, BF16)], [own, over_core(own), pick_cols, add_rows, turned], [counts], slots)
         (part,) = call(row_sum, [(RB + EXTRA, BF16)], [part, *over_square(part, NEAR)])
         return [part, *over_square(part, FAR)]
 
     def chips_whole(part):
         return [part, *over_chips(part)]
 
-    data0, keep, send = call(
+    data0, pick_rows, add_cols, keep, send = call(
         first_adjoint,
-        [(RB, F32), (HALF, F32), message],
-        [quarter, *over_square(quarter, FAR), rows, cols, first, second],
+        [(RB, F32), (slots, BF16, RB), (CB, BF16, slots), (HALF, F32), message],
+        [quarter, *over_places(quarter, FAR), rows, cols, first, second],
         [counts, place],
         slots,
     )
     (part,) = call(chip_sum, [message], [keep, send, over_core(send)])
-    turned = pl.pallas_call(
+    turned, pick_cols, add_rows = pl.pallas_call(
         transpose,
-        out_shape=pltpu.VMEM((slots, BS, BS), BF16),
-        in_specs=[VECTOR] * 3,
-        out_specs=VECTOR,
+        out_shape=[
+            pltpu.VMEM((slots, BS, BS), BF16),
+            jax.ShapeDtypeStruct((slots, CB), BF16),
+            jax.ShapeDtypeStruct((RB, slots), BF16),
+        ],
+        in_specs=[SCALAR] + [VECTOR] * 5,
+        out_specs=[VECTOR] * 3,
         compiler_params=params,
         cost_estimate=cost,
         name="transpose",
-    )(part, first, second)
+    )(counts, part, rows, cols, first, second)
     turned = pltpu.with_memory_space_constraint(turned, pltpu.VMEM)
     model0, own, beta0 = call(first_model, model_outs, [*chips_whole(part), turned])
     data1, alpha0, keep, send = call(
         second_adjoint,
         [(RB, F32), scalar, (HALF, F32), message],
-        [*forward_whole(own), data0, beta0, rows, cols, first, second],
+        [*forward_whole(own), data0, beta0, pick_rows, add_cols, first, second],
         [counts],
         slots,
     )

time: 104 us -> 97.9 us (0.941)
  waiting for transfers between devices: 41.4 us -> 33.2 us
  starting transfers between devices: 41 us -> 42.8 us
    ppermute x27, waiting for transfers between devices: 36.8 us -> 28.6 us  [the longest x12 17.4 us: over_square(): lax.ppermute(x, ('dp', 'mp'), [(i * 16 + j, i * 16 + (j ^ step[i & 1])) f...]
    ppermute x27, starting transfers between devices: 31.9 us -> 35.9 us  [the longest x12 16.2 us: over_square(): lax.ppermute(x, ('dp', 'mp'), [(i * 16 + j, i * 16 + (j ^ step[i & 1])) f...]
    ppermute x5, starting transfers between devices: 9.12 us -> 6.86 us  [over_core(): return lax.ppermute(x, 'dp', [(i, i ^ 1) for i in range(8)])]
  transfers between devices with their start and end apart: 32 -> 32, of which waited for: 25 -> 24; matrix products, arithmetic and copies ran while one was open for 0% -> 0% of each run, Pallas kernels for 9% -> 9%
where the time goes in v3:
time: 97.9 us; the launch traced here: 97.7 us
  starting transfers between devices  42.8 us (44%)
  waiting for transfers between devices  33.2 us (34%)
  Pallas kernels  20.9 us (21%)
    ppermute x12, waiting for transfers between devices, over_square(): lax.ppermute(x, ('dp', 'mp'), [(i * 16 + j, i * 16 + (j ^ step[i & 1])) f...  17.4 us
    ppermute x12, starting transfers between devices, over_square(): lax.ppermute(x, ('dp', 'mp'), [(i * 16 + j, i * 16 + (j ^ step[i & 1])) f...  16.2 us
    pallas_call x14, Pallas kernels, call(): pl.pallas_call(kernel, out_shape=[jax.ShapeDtypeStruct((rows, *(width or...  11.7 us
    ppermute x9, starting transfers between devices, over_chips(): lax.ppermute(x, 'dp', [(i, (i >> 1 ^ step[i & 1]) * 2 + (i & 1)) for i in...  11 us
    ppermute x9, waiting for transfers between devices, over_chips(): lax.ppermute(x, 'dp', [(i, (i >> 1 ^ step[i & 1]) * 2 + (i & 1)) for i in...  10.4 us
    ppermute x6, starting transfers between devices, over_places(): lax.ppermute(x, 'mp', [(j, j ^ step) for j in range(16)])  8.72 us
    ppermute x5, starting transfers between devices, over_core(): return lax.ppermute(x, 'dp', [(i, i ^ 1) for i in range(8)])  6.86 us
    ppermute x5, waiting for transfers between devices, over_core(): return lax.ppermute(x, 'dp', [(i, i ^ 1) for i in range(8)])  4.62 us
  transfers between devices with their start and end apart: 32, of which 24 were waited for; matrix products, arithmetic and copies ran while one was open for 0% of the time, Pallas kernels for 9%

profile of v3, /device:TPU:1, one launch (start us, length us, event | category | flops | bytes accessed | tf_op | source)
XLA Modules:
  0.0 97.7 jit_solution(15202103297049464626)
XLA Ops:
  0.0 3.6 %collective-permute-start = (f32[32,128]{1,0:T(8,128)}, f32[32,128]{1,0:T(8,128)S(1)}, u32[]{:S(2)}, u32[]{:S(2)}) collective-permute-start(f32[32,128]{1,0:T(8,128)} %data_ref.1), channel_id=1, source_target_pairs={{0,3},{1,2},{2,1},{3,0},{4,7},{5,6},{6,5},{7,4},{8,11},{9,10},{10,... | collective-permute-start | bytes 49160 | tf_op jit(solution)/shard_map/ppermute | solution.py:388
  5.4 2.9 %load_first.1 = (f32[32,128]{1,0:T(8,128)S(1)}, s32[1,384]{1,0:T(1,128)S(1)}, s32[1,384]{1,0:T(1,128)S(1)}, bf16[192,128,128]{2,1,0:T(8,128)(2,1)S(1)}) custom-call(s32[1]{0:T(128)} %bitcast.2.core_ref, s32[1]{0:T(128)} %bitcast.chip_ref, s32[1]{0:T(128)} %bitcast.1.place_ref, s32[1,1]{1,0:T(1,128)S(6)} %copy.6.live_ref, f32[32,128]{1,0:T(8,128)} %data_ref.1, ...), custom_call_target="tpu_custom_call" | custom-call | bytes 12582912 | tf_op jit(solution)/shard_map/load_first/pallas_call | solution.py:401
  8.5 2.2 %collective-permute-start.5 = (f32[128,128]{1,0:T(8,128)S(1)}, f32[128,128]{1,0:T(8,128)S(1)}, u32[]{:S(2)}, u32[]{:S(2)}) collective-permute-start(f32[128,128]{1,0:T(8,128)S(1)} %collect.1.after_ref.own_ref), channel_id=1, source_target_pairs={{0,13},{1,12},{2,15},{3,14},{4,9},{5,8},{6,11},{7,10},{8,5},{9,4},... | collective-permute-start | bytes 196616 | tf_op jit(solution)/shard_map/ppermute | solution.py:388
  12.4 2.9 %load_second.1.second_ref = bf16[192,128,128]{2,1,0:T(8,128)(2,1)S(1)} custom-call(f32[128,128]{1,0:T(8,128)S(1)} %collect.1.after_ref.own_ref, bf16[384,128,128]{2,1,0:T(8,128)(2,1)} %bitcast.7), custom_call_target="tpu_custom_call" | custom-call | bytes 12582912 | tf_op jit(solution)/shard_map/load_second/pallas_call | solution.py:422
  16.0 2.5 %first_adjoint.1 = (f32[512,128]{1,0:T(8,128)S(1)}, bf16[384,512]{1,0:T(8,128)(2,1)S(1)}, bf16[768,384]{1,0:T(8,128)(2,1)S(1)}, f32[384,128]{1,0:T(8,128)S(1)}, bf16[400,128]{1,0:T(8,128)(2,1)S(1)}) custom-call(s32[1,1]{1,0:T(1,128)S(6)} %copy.6.live_ref, s32[1]{0:T(128)} %bitcast.1.place_ref, f32[128,128]{1,0:T(8,128)S(1)} %collect.1.after_ref.own_ref, ...), custom_call_target="tpu_custom_call" | custom-call | tf_op jit(solution)/shard_map/first_adjoint/pallas_call | solution.py:351
  18.5 2.4 %collective-permute-start.6 = (bf16[400,128]{1,0:T(8,128)(2,1)S(1)}, bf16[400,128]{1,0:T(8,128)(2,1)S(1)}, u32[]{:S(2)}, u32[]{:S(2)}) collective-permute-start(bf16[400,128]{1,0:T(8,128)(2,1)S(1)} %get-tuple-element.34.send_ref), channel_id=1, source_target_pairs={{0,16},{16,0},{32,48},{48,32},{64,80},{80,64},{96,112},{112,96},{1... | collective-permute-start | bytes 307208 | tf_op jit(solution)/shard_map/ppermute | solution.py:370
  21.8 3.7 %collective-permute-start.9 = (bf16[400,128]{1,0:T(8,128)(2,1)S(1)}, bf16[400,128]{1,0:T(8,128)(2,1)S(1)}, u32[]{:S(2)}, u32[]{:S(2)}) collective-permute-start(bf16[400,128]{1,0:T(8,128)(2,1)S(1)} %chip_sum.2.after_ref.own_ref), channel_id=1, source_target_pairs={{0,64},{16,80},{32,96},{48,112},{64,0},{80,16},{96,32},{112,48},{1... | collective-permute-start | bytes 307208 | tf_op jit(solution)/shard_map/ppermute | solution.py:375
  26.2 3.4 %transpose.1 = (bf16[384,128,128]{2,1,0:T(8,128)(2,1)S(1)}, bf16[384,768]{1,0:T(8,128)(2,1)S(1)}, bf16[512,384]{1,0:T(8,128)(2,1)S(1)}) custom-call(s32[1,1]{1,0:T(1,128)S(6)} %copy.6.live_ref, bf16[400,128]{1,0:T(8,128)(2,1)S(1)} %chip_sum.2.after_ref.own_ref, s32[1,384]{1,0:T(1,128)S(1)} %get-tuple-element.31.rows_ref, ...), custom_call_target="tpu_custom_call" | custom-call | bytes 12582912 | tf_op jit(solution)/shard_map/transpose/pallas_call | solution.py:450
  33.9 2.5 %forward.2.own_ref = bf16[528,128]{1,0:T(8,128)(2,1)S(1)} custom-call(s32[1,1]{1,0:T(1,128)S(6)} %copy.6.live_ref, bf16[400,128]{1,0:T(8,128)(2,1)S(1)} %get-tuple-element.36.own_ref, bf16[400,128]{1,0:T(8,128)(2,1)S(1)} %collective-permute-done.10.got_ref, bf16[384,768]{1,0:T(8,128)(2,1)S(1)} %get-tuple-element.37.pick_ref, ...), custom_call_target="tpu_custom_call" | custom-call | tf_op jit(solution)/shard_map/forward/pallas_call | solution.py:351
  36.5 3.4 %collective-permute-start.13 = (bf16[528,128]{1,0:T(8,128)(2,1)S(1)}, bf16[528,128]{1,0:T(8,128)(2,1)S(1)}, u32[]{:S(2)}, u32[]{:S(2)}) collective-permute-start(bf16[528,128]{1,0:T(8,128)(2,1)S(1)} %forward.2.own_ref), channel_id=1, source_target_pairs={{0,7},{1,6},{2,5},{3,4},{4,3},{5,2},{6,1},{7,0},{8,15},{9,14},{10,... | collective-permute-start | bytes 405512 | tf_op jit(solution)/shard_map/ppermute | solution.py:381
  40.8 2.0 %collective-permute-done.13.three_ref = bf16[528,128]{1,0:T(8,128)(2,1)S(1)} collective-permute-done((bf16[528,128]{1,0:T(8,128)(2,1)S(1)}, bf16[528,128]{1,0:T(8,128)(2,1)S(1)}, u32[]{:S(2)}, u32[]{:S(2)}) %collective-permute-start.13) | collective-permute-done | bytes 135200 | tf_op jit(solution)/shard_map/ppermute | solution.py:381
  42.8 2.4 %collective-permute-done.12.two_ref = bf16[528,128]{1,0:T(8,128)(2,1)S(1)} collective-permute-done((bf16[528,128]{1,0:T(8,128)(2,1)S(1)}, bf16[528,128]{1,0:T(8,128)(2,1)S(1)}, u32[]{:S(2)}, u32[]{:S(2)}) %collective-permute-start.12) | collective-permute-done | bytes 135200 | tf_op jit(solution)/shard_map/ppermute | solution.py:381
  45.4 3.1 %collective-permute-start.15 = (bf16[528,128]{1,0:T(8,128)(2,1)S(1)}, bf16[528,128]{1,0:T(8,128)(2,1)S(1)}, u32[]{:S(2)}, u32[]{:S(2)}) collective-permute-start(bf16[528,128]{1,0:T(8,128)(2,1)S(1)} %row_sum.2.own_ref), channel_id=1, source_target_pairs={{0,12},{1,13},{2,14},{3,15},{4,8},{5,9},{6,10},{7,11},{8,4},{9,5},... | collective-permute-start | bytes 405512 | tf_op jit(solution)/shard_map/ppermute | solution.py:381
  49.2 2.1 %collective-permute-done.16.three_ref = bf16[528,128]{1,0:T(8,128)(2,1)S(1)} collective-permute-done((bf16[528,128]{1,0:T(8,128)(2,1)S(1)}, bf16[528,128]{1,0:T(8,128)(2,1)S(1)}, u32[]{:S(2)}, u32[]{:S(2)}) %collective-permute-start.16) | collective-permute-done | bytes 135200 | tf_op jit(solution)/shard_map/ppermute | solution.py:381
  53.9 2.5 %second_adjoint.1 = (f32[512,128]{1,0:T(8,128)S(1)}, f32[8,128]{1,0:T(8,128)S(1)}, f32[384,128]{1,0:T(8,128)S(1)}, bf16[400,128]{1,0:T(8,128)(2,1)S(1)}) custom-call(s32[1,1]{1,0:T(1,128)S(6)} %copy.6.live_ref, bf16[528,128]{1,0:T(8,128)(2,1)S(1)} %row_sum.2.own_ref, bf16[528,128]{1,0:T(8,128)(2,1)S(1)} %collective-permute-done.14.one_ref, ...), custom_call_target="tpu_custom_call" | custom-call | tf_op jit(solution)/shard_map/second_adjoint/pallas_call | solution.py:351
  56.3 1.8 %collective-permute-start.17 = (bf16[400,128]{1,0:T(8,128)(2,1)S(1)}, bf16[400,128]{1,0:T(8,128)(2,1)S(1)}, u32[]{:S(2)}, u32[]{:S(2)}) collective-permute-start(bf16[400,128]{1,0:T(8,128)(2,1)S(1)} %get-tuple-element.44.send_ref), channel_id=1, source_target_pairs={{0,16},{16,0},{32,48},{48,32},{64,80},{80,64},{96,112},{112,96},{1... | collective-permute-start | bytes 307208 | tf_op jit(solution)/shard_map/ppermute | solution.py:370
  59.1 1.8 %collective-permute-start.20 = (bf16[400,128]{1,0:T(8,128)(2,1)S(1)}, bf16[400,128]{1,0:T(8,128)(2,1)S(1)}, u32[]{:S(2)}, u32[]{:S(2)}) collective-permute-start(bf16[400,128]{1,0:T(8,128)(2,1)S(1)} %chip_sum.3.own_ref), channel_id=1, source_target_pairs={{0,64},{16,80},{32,96},{48,112},{64,0},{80,16},{96,32},{112,48},{1... | collective-permute-start | bytes 307208 | tf_op jit(solution)/shard_map/ppermute | solution.py:375
  62.5 2.4 %collective-permute-done.20.three_ref = bf16[400,128]{1,0:T(8,128)(2,1)S(1)} collective-permute-done((bf16[400,128]{1,0:T(8,128)(2,1)S(1)}, bf16[400,128]{1,0:T(8,128)(2,1)S(1)}, u32[]{:S(2)}, u32[]{:S(2)}) %collective-permute-start.20) | collective-permute-done | bytes 102432 | tf_op jit(solution)/shard_map/ppermute | solution.py:375
  69.8 2.5 %forward.3.own_ref = bf16[528,128]{1,0:T(8,128)(2,1)S(1)} custom-call(s32[1,1]{1,0:T(1,128)S(6)} %copy.6.live_ref, bf16[400,128]{1,0:T(8,128)(2,1)S(1)} %get-tuple-element.47.own_ref, bf16[400,128]{1,0:T(8,128)(2,1)S(1)} %collective-permute-done.21.got_ref, bf16[384,768]{1,0:T(8,128)(2,1)S(1)} %get-tuple-element.37.pick_ref, ...), custom_call_target="tpu_custom_call" | custom-call | tf_op jit(solution)/shard_map/forward/pallas_call | solution.py:351
  72.3 3.1 %collective-permute-start.24 = (bf16[528,128]{1,0:T(8,128)(2,1)S(1)}, bf16[528,128]{1,0:T(8,128)(2,1)S(1)}, u32[]{:S(2)}, u32[]{:S(2)}) collective-permute-start(bf16[528,128]{1,0:T(8,128)(2,1)S(1)} %forward.3.own_ref), channel_id=1, source_target_pairs={{0,7},{1,6},{2,5},{3,4},{4,3},{5,2},{6,1},{7,0},{8,15},{9,14},{10,... | collective-permute-start | bytes 405512 | tf_op jit(solution)/shard_map/ppermute | solution.py:381
  76.4 2.3 %collective-permute-done.24.three_ref = bf16[528,128]{1,0:T(8,128)(2,1)S(1)} collective-permute-done((bf16[528,128]{1,0:T(8,128)(2,1)S(1)}, bf16[528,128]{1,0:T(8,128)(2,1)S(1)}, u32[]{:S(2)}, u32[]{:S(2)}) %collective-permute-start.24) | collective-permute-done | bytes 135200 | tf_op jit(solution)/shard_map/ppermute | solution.py:381
  78.7 2.2 %collective-permute-done.23.two_ref = bf16[528,128]{1,0:T(8,128)(2,1)S(1)} collective-permute-done((bf16[528,128]{1,0:T(8,128)(2,1)S(1)}, bf16[528,128]{1,0:T(8,128)(2,1)S(1)}, u32[]{:S(2)}, u32[]{:S(2)}) %collective-permute-start.23) | collective-permute-done | bytes 135200 | tf_op jit(solution)/shard_map/ppermute | solution.py:381
  82.6 2.3 %collective-permute-start.25 = (bf16[528,128]{1,0:T(8,128)(2,1)S(1)}, bf16[528,128]{1,0:T(8,128)(2,1)S(1)}, u32[]{:S(2)}, u32[]{:S(2)}) collective-permute-start(bf16[528,128]{1,0:T(8,128)(2,1)S(1)} %row_sum.3.own_ref), channel_id=1, source_target_pairs={{0,1},{1,0},{2,3},{3,2},{4,5},{5,4},{6,7},{7,6},{8,9},{9,8},{10,11... | collective-permute-start | bytes 405512 | tf_op jit(solution)/shard_map/ppermute | solution.py:381
  84.8 2.4 %collective-permute-done.27.three_ref = bf16[528,128]{1,0:T(8,128)(2,1)S(1)} collective-permute-done((bf16[528,128]{1,0:T(8,128)(2,1)S(1)}, bf16[528,128]{1,0:T(8,128)(2,1)S(1)}, u32[]{:S(2)}, u32[]{:S(2)}) %collective-permute-start.27) | collective-permute-done | bytes 135200 | tf_op jit(solution)/shard_map/ppermute | solution.py:381
  (57 shorter events, 34.7 us)
Async XLA Ops:
  0.0 8.4 %collective-permute-start = (f32[32,128]{1,0:T(8,128)}, f32[32,128]{1,0:T(8,128)S(1)}, u32[]{:S(2)}, u32[]{:S(2)}) collective-permute-start(f32[32,128]{1,0:T(8,128)} %data_ref.1), channel_id=1, source_target_pairs={{0,3},{1,2},{2,1},{3,0},{4,7},{5,6},{6,5},{7,4},{8,11},{9,10},{10,... | collective-permute-start | bytes 49160 | tf_op jit(solution)/shard_map/ppermute | solution.py:388
  3.6 4.9 %collective-permute-start.2 = (f32[32,128]{1,0:T(8,128)}, f32[32,128]{1,0:T(8,128)S(1)}, u32[]{:S(2)}, u32[]{:S(2)}) collective-permute-start(f32[32,128]{1,0:T(8,128)} %data_ref.1), channel_id=1, source_target_pairs={{0,7},{1,6},{2,5},{3,4},{4,3},{5,2},{6,1},{7,0},{8,15},{9,14},{10,... | collective-permute-start | bytes 49160 | tf_op jit(solution)/shard_map/ppermute | solution.py:388
  4.5 4.0 %collective-permute-start.1 = (f32[32,128]{1,0:T(8,128)}, f32[32,128]{1,0:T(8,128)S(1)}, u32[]{:S(2)}, u32[]{:S(2)}) collective-permute-start(f32[32,128]{1,0:T(8,128)} %data_ref.1), channel_id=1, source_target_pairs={{0,4},{1,5},{2,6},{3,7},{4,0},{5,1},{6,2},{7,3},{8,12},{9,13},{10,... | collective-permute-start | bytes 49160 | tf_op jit(solution)/shard_map/ppermute | solution.py:388
  8.5 6.8 %collective-permute-start.5 = (f32[128,128]{1,0:T(8,128)S(1)}, f32[128,128]{1,0:T(8,128)S(1)}, u32[]{:S(2)}, u32[]{:S(2)}) collective-permute-start(f32[128,128]{1,0:T(8,128)S(1)} %collect.1.after_ref.own_ref), channel_id=1, source_target_pairs={{0,13},{1,12},{2,15},{3,14},{4,9},{5,8},{6,11},{7,10},{8,5},{9,4},... | collective-permute-start | bytes 196616 | tf_op jit(solution)/shard_map/ppermute | solution.py:388
  10.7 5.3 %collective-permute-start.4 = (f32[128,128]{1,0:T(8,128)S(1)}, f32[128,128]{1,0:T(8,128)S(1)}, u32[]{:S(2)}, u32[]{:S(2)}) collective-permute-start(f32[128,128]{1,0:T(8,128)S(1)} %collect.1.after_ref.own_ref), channel_id=1, source_target_pairs={{0,12},{1,13},{2,14},{3,15},{4,8},{5,9},{6,10},{7,11},{8,4},{9,5},... | collective-permute-start | bytes 196616 | tf_op jit(solution)/shard_map/ppermute | solution.py:388
  11.1 4.8 %collective-permute-start.3 = (f32[128,128]{1,0:T(8,128)S(1)}, f32[128,128]{1,0:T(8,128)S(1)}, u32[]{:S(2)}, u32[]{:S(2)}) collective-permute-start(f32[128,128]{1,0:T(8,128)S(1)} %collect.1.after_ref.own_ref), channel_id=1, source_target_pairs={{0,1},{1,0},{2,3},{3,2},{4,5},{5,4},{6,7},{7,6},{8,9},{9,8},{10,11... | collective-permute-start | bytes 196616 | tf_op jit(solution)/shard_map/ppermute | solution.py:388
  21.8 7.9 %collective-permute-start.9 = (bf16[400,128]{1,0:T(8,128)(2,1)S(1)}, bf16[400,128]{1,0:T(8,128)(2,1)S(1)}, u32[]{:S(2)}, u32[]{:S(2)}) collective-permute-start(bf16[400,128]{1,0:T(8,128)(2,1)S(1)} %chip_sum.2.after_ref.own_ref), channel_id=1, source_target_pairs={{0,64},{16,80},{32,96},{48,112},{64,0},{80,16},{96,32},{112,48},{1... | collective-permute-start | bytes 307208 | tf_op jit(solution)/shard_map/ppermute | solution.py:375
  25.5 5.6 %collective-permute-start.8 = (bf16[400,128]{1,0:T(8,128)(2,1)S(1)}, bf16[400,128]{1,0:T(8,128)(2,1)S(1)}, u32[]{:S(2)}, u32[]{:S(2)}) collective-permute-start(bf16[400,128]{1,0:T(8,128)(2,1)S(1)} %chip_sum.2.after_ref.own_ref), channel_id=1, source_target_pairs={{0,96},{16,48},{32,64},{48,16},{64,32},{80,112},{96,0},{112,80},{1... | collective-permute-start | bytes 307208 | tf_op jit(solution)/shard_map/ppermute | solution.py:375
  26.2 5.8 %collective-permute-start.7 = (bf16[400,128]{1,0:T(8,128)(2,1)S(1)}, bf16[400,128]{1,0:T(8,128)(2,1)S(1)}, u32[]{:S(2)}, u32[]{:S(2)}) collective-permute-start(bf16[400,128]{1,0:T(8,128)(2,1)S(1)} %chip_sum.2.after_ref.own_ref), channel_id=1, source_target_pairs={{0,32},{16,112},{32,0},{48,80},{64,96},{80,48},{96,64},{112,16},{1... | collective-permute-start | bytes 307208 | tf_op jit(solution)/shard_map/ppermute | solution.py:375
  36.5 6.3 %collective-permute-start.13 = (bf16[528,128]{1,0:T(8,128)(2,1)S(1)}, bf16[528,128]{1,0:T(8,128)(2,1)S(1)}, u32[]{:S(2)}, u32[]{:S(2)}) collective-permute-start(bf16[528,128]{1,0:T(8,128)(2,1)S(1)} %forward.2.own_ref), channel_id=1, source_target_pairs={{0,7},{1,6},{2,5},{3,4},{4,3},{5,2},{6,1},{7,0},{8,15},{9,14},{10,... | collective-permute-start | bytes 405512 | tf_op jit(solution)/shard_map/ppermute | solution.py:381
  39.8 5.4 %collective-permute-start.12 = (bf16[528,128]{1,0:T(8,128)(2,1)S(1)}, bf16[528,128]{1,0:T(8,128)(2,1)S(1)}, u32[]{:S(2)}, u32[]{:S(2)}) collective-permute-start(bf16[528,128]{1,0:T(8,128)(2,1)S(1)} %forward.2.own_ref), channel_id=1, source_target_pairs={{0,4},{1,5},{2,6},{3,7},{4,0},{5,1},{6,2},{7,3},{8,12},{9,13},{10,... | collective-permute-start | bytes 405512 | tf_op jit(solution)/shard_map/ppermute | solution.py:381
  40.8 4.4 %collective-permute-start.11 = (bf16[528,128]{1,0:T(8,128)(2,1)S(1)}, bf16[528,128]{1,0:T(8,128)(2,1)S(1)}, u32[]{:S(2)}, u32[]{:S(2)}) collective-permute-start(bf16[528,128]{1,0:T(8,128)(2,1)S(1)} %forward.2.own_ref), channel_id=1, source_target_pairs={{0,3},{1,2},{2,1},{3,0},{4,7},{5,6},{6,5},{7,4},{8,11},{9,10},{10,... | collective-permute-start | bytes 405512 | tf_op jit(solution)/shard_map/ppermute | solution.py:381
  45.3 6.0 %collective-permute-start.16 = (bf16[528,128]{1,0:T(8,128)(2,1)S(1)}, bf16[528,128]{1,0:T(8,128)(2,1)S(1)}, u32[]{:S(2)}, u32[]{:S(2)}) collective-permute-start(bf16[528,128]{1,0:T(8,128)(2,1)S(1)} %row_sum.2.own_ref), channel_id=1, source_target_pairs={{0,13},{1,12},{2,15},{3,14},{4,9},{5,8},{6,11},{7,10},{8,5},{9,4},... | collective-permute-start | bytes 405512 | tf_op jit(solution)/shard_map/ppermute | solution.py:381
  45.4 7.3 %collective-permute-start.15 = (bf16[528,128]{1,0:T(8,128)(2,1)S(1)}, bf16[528,128]{1,0:T(8,128)(2,1)S(1)}, u32[]{:S(2)}, u32[]{:S(2)}) collective-permute-start(bf16[528,128]{1,0:T(8,128)(2,1)S(1)} %row_sum.2.own_ref), channel_id=1, source_target_pairs={{0,12},{1,13},{2,14},{3,15},{4,8},{5,9},{6,10},{7,11},{8,4},{9,5},... | collective-permute-start | bytes 405512 | tf_op jit(solution)/shard_map/ppermute | solution.py:381
  48.5 5.4 %collective-permute-start.14 = (bf16[528,128]{1,0:T(8,128)(2,1)S(1)}, bf16[528,128]{1,0:T(8,128)(2,1)S(1)}, u32[]{:S(2)}, u32[]{:S(2)}) collective-permute-start(bf16[528,128]{1,0:T(8,128)(2,1)S(1)} %row_sum.2.own_ref), channel_id=1, source_target_pairs={{0,1},{1,0},{2,3},{3,2},{4,5},{5,4},{6,7},{7,6},{8,9},{9,8},{10,11... | collective-permute-start | bytes 405512 | tf_op jit(solution)/shard_map/ppermute | solution.py:381
  59.1 5.7 %collective-permute-start.20 = (bf16[400,128]{1,0:T(8,128)(2,1)S(1)}, bf16[400,128]{1,0:T(8,128)(2,1)S(1)}, u32[]{:S(2)}, u32[]{:S(2)}) collective-permute-start(bf16[400,128]{1,0:T(8,128)(2,1)S(1)} %chip_sum.3.own_ref), channel_id=1, source_target_pairs={{0,64},{16,80},{32,96},{48,112},{64,0},{80,16},{96,32},{112,48},{1... | collective-permute-start | bytes 307208 | tf_op jit(solution)/shard_map/ppermute | solution.py:375
  61.0 5.5 %collective-permute-start.19 = (bf16[400,128]{1,0:T(8,128)(2,1)S(1)}, bf16[400,128]{1,0:T(8,128)(2,1)S(1)}, u32[]{:S(2)}, u32[]{:S(2)}) collective-permute-start(bf16[400,128]{1,0:T(8,128)(2,1)S(1)} %chip_sum.3.own_ref), channel_id=1, source_target_pairs={{0,96},{16,48},{32,64},{48,16},{64,32},{80,112},{96,0},{112,80},{1... | collective-permute-start | bytes 307208 | tf_op jit(solution)/shard_map/ppermute | solution.py:375
  61.7 6.3 %collective-permute-start.18 = (bf16[400,128]{1,0:T(8,128)(2,1)S(1)}, bf16[400,128]{1,0:T(8,128)(2,1)S(1)}, u32[]{:S(2)}, u32[]{:S(2)}) collective-permute-start(bf16[400,128]{1,0:T(8,128)(2,1)S(1)} %chip_sum.3.own_ref), channel_id=1, source_target_pairs={{0,32},{16,112},{32,0},{48,80},{64,96},{80,48},{96,64},{112,16},{1... | collective-permute-start | bytes 307208 | tf_op jit(solution)/shard_map/ppermute | solution.py:375
  72.3 6.3 %collective-permute-start.24 = (bf16[528,128]{1,0:T(8,128)(2,1)S(1)}, bf16[528,128]{1,0:T(8,128)(2,1)S(1)}, u32[]{:S(2)}, u32[]{:S(2)}) collective-permute-start(bf16[528,128]{1,0:T(8,128)(2,1)S(1)} %forward.3.own_ref), channel_id=1, source_target_pairs={{0,7},{1,6},{2,5},{3,4},{4,3},{5,2},{6,1},{7,0},{8,15},{9,14},{10,... | collective-permute-start | bytes 405512 | tf_op jit(solution)/shard_map/ppermute | solution.py:381
  75.5 5.4 %collective-permute-start.23 = (bf16[528,128]{1,0:T(8,128)(2,1)S(1)}, bf16[528,128]{1,0:T(8,128)(2,1)S(1)}, u32[]{:S(2)}, u32[]{:S(2)}) collective-permute-start(bf16[528,128]{1,0:T(8,128)(2,1)S(1)} %forward.3.own_ref), channel_id=1, source_target_pairs={{0,4},{1,5},{2,6},{3,7},{4,0},{5,1},{6,2},{7,3},{8,12},{9,13},{10,... | collective-permute-start | bytes 405512 | tf_op jit(solution)/shard_map/ppermute | solution.py:381
  76.4 4.4 %collective-permute-start.22 = (bf16[528,128]{1,0:T(8,128)(2,1)S(1)}, bf16[528,128]{1,0:T(8,128)(2,1)S(1)}, u32[]{:S(2)}, u32[]{:S(2)}) collective-permute-start(bf16[528,128]{1,0:T(8,128)(2,1)S(1)} %forward.3.own_ref), channel_id=1, source_target_pairs={{0,3},{1,2},{2,1},{3,0},{4,7},{5,6},{6,5},{7,4},{8,11},{9,10},{10,... | collective-permute-start | bytes 405512 | tf_op jit(solution)/shard_map/ppermute | solution.py:381
  80.9 6.3 %collective-permute-start.27 = (bf16[528,128]{1,0:T(8,128)(2,1)S(1)}, bf16[528,128]{1,0:T(8,128)(2,1)S(1)}, u32[]{:S(2)}, u32[]{:S(2)}) collective-permute-start(bf16[528,128]{1,0:T(8,128)(2,1)S(1)} %row_sum.3.own_ref), channel_id=1, source_target_pairs={{0,13},{1,12},{2,15},{3,14},{4,9},{5,8},{6,11},{7,10},{8,5},{9,4},... | collective-permute-start | bytes 405512 | tf_op jit(solution)/shard_map/ppermute | solution.py:381
  81.0 6.3 %collective-permute-start.26 = (bf16[528,128]{1,0:T(8,128)(2,1)S(1)}, bf16[528,128]{1,0:T(8,128)(2,1)S(1)}, u32[]{:S(2)}, u32[]{:S(2)}) collective-permute-start(bf16[528,128]{1,0:T(8,128)(2,1)S(1)} %row_sum.3.own_ref), channel_id=1, source_target_pairs={{0,12},{1,13},{2,14},{3,15},{4,8},{5,9},{6,10},{7,11},{8,4},{9,5},... | collective-permute-start | bytes 405512 | tf_op jit(solution)/shard_map/ppermute | solution.py:381
  82.6 6.1 %collective-permute-start.25 = (bf16[528,128]{1,0:T(8,128)(2,1)S(1)}, bf16[528,128]{1,0:T(8,128)(2,1)S(1)}, u32[]{:S(2)}, u32[]{:S(2)}) collective-permute-start(bf16[528,128]{1,0:T(8,128)(2,1)S(1)} %row_sum.3.own_ref), channel_id=1, source_target_pairs={{0,1},{1,0},{2,3},{3,2},{4,5},{5,4},{6,7},{7,6},{8,9},{9,8},{10,11... | collective-permute-start | bytes 405512 | tf_op jit(solution)/shard_map/ppermute | solution.py:381
  (8 other events, 21.9 us)

commit v4 on v3

--- a/solution.py
+++ b/solution.py
@@ -72,13 +72,24 @@
     return jnp.where((jnp.broadcast_to(index, (size, slots)) == row) & (lane < live), 1.0, 0.0).astype(BF16)
 
 
-def scatter(products, hot, live):
-    slot = lax.broadcasted_iota(jnp.int32, products.shape, 0)
-    products = jnp.where(slot < live, products, 0.0)
-    high = products.astype(BF16)
-    low = (products - high.astype(F32)).astype(BF16)
-    both = jnp.dot(hot, jnp.concatenate([high, low], 1), preferred_element_type=F32)
-    return both[:, :BS] + both[:, BS:]
+def gather(pick_ref, source, picked_ref):
+    for start in reversed(range(0, picked_ref.shape[0], BS)):
+        piece = jnp.dot(pick_ref[start : start + BS, :], source, preferred_element_type=F32)
+        picked_ref[start : start + BS, :] = piece.astype(BF16)
+
+
+def scatter(products_ref, hot_ref, live):
+    slots = products_ref.shape[0]
+    total = 0.0
+    for start in range(0, slots, 2 * BS):
+        piece = slice(start, min(start + 2 * BS, slots))
+        products = products_ref[piece, :]
+        slot = lax.broadcasted_iota(jnp.int32, products.shape, 0) + start
+        products = jnp.where(slot < live, products, 0.0)
+        high = products.astype(BF16)
+        low = (products - high.astype(F32)).astype(BF16)
+        total += jnp.dot(hot_ref[:, piece], jnp.concatenate([high, low], 1), preferred_element_type=F32)
+    return total[:, :BS] + total[:, BS:]
 
 
 def spread(picked):
@@ -88,19 +99,38 @@
 
 
 def multiply(blocks_refs, picked_ref, products_ref):
-    base = 0
-    for ref in blocks_refs:
-        for start in range(0, ref.shape[0], GROUP):
-            slots = slice(base + start, base + start + GROUP)
-            tile = ref[start : start + GROUP].reshape(GROUP * BS, BS)
-            products_ref[slots, :] = jnp.dot(spread(picked_ref[slots, :]), tile, preferred_element_type=F32)
-        base += ref.shape[0]
-
-
-def adjoint_tail(live, data, pick, hot, blocks_refs, keep_ref, send_ref, picked_ref, products_ref):
-    picked_ref[...] = jnp.dot(pick, data.astype(BF16), preferred_element_type=F32).astype(BF16)
+    def block(slot, size):
+        for ref in blocks_refs:
+            if slot < ref.shape[0]:
+                return ref[slot : slot + size]
+            slot -= ref.shape[0]
+
+    slots = picked_ref.shape[0]
+    singles = slots // 4
+    groups = (slots - singles) // GROUP
+    first = groups * GROUP
+    turned = []
+    for start in range(first, slots, BS):
+        rows = picked_ref[start : min(start + BS, slots), :].astype(F32)
+        if rows.shape[0] < BS:
+            rows = jnp.concatenate([rows, jnp.zeros((BS - rows.shape[0], BS), F32)], 0)
+        turned.append(jnp.transpose(rows))
+    for group in range(groups):
+        for single in range(singles * group // groups, singles * (group + 1) // groups):
+            weights = jnp.broadcast_to(turned[single // BS][:, single % BS : single % BS + 1], (BS, BS))
+            product = block(first + single, 1)[0].astype(F32) * weights
+            products_ref[first + single : first + single + 1, :] = jnp.sum(product, axis=0, keepdims=True)
+        start = group * GROUP
+        tile = block(start, GROUP).reshape(GROUP * BS, BS)
+        products_ref[start : start + GROUP, :] = jnp.dot(
+            spread(picked_ref[start : start + GROUP, :]), tile, preferred_element_type=F32
+        )
+
+
+def adjoint_tail(live, data, pick_ref, hot_ref, blocks_refs, keep_ref, send_ref, picked_ref, products_ref):
+    gather(pick_ref, data.astype(BF16), picked_ref)
     multiply(blocks_refs, picked_ref, products_ref)
-    partial = scatter(products_ref[...], hot, live)
+    partial = scatter(products_ref, hot_ref, live)
     keep_ref[...] = partial[:HALF]
     send_ref[:HALF, :] = partial[HALF:].astype(BF16)
     send_ref[HALF:, :] = split_rows(square_sum(data))
@@ -131,12 +161,10 @@
             at = pl.multiple_of((place_ref[0] ^ step ^ hop) * SHARE, SHARE)
             data_ref[pl.ds(at, SHARE), :] = ref[piece * SHARE : (piece + 1) * SHARE, :]
     live = live_ref[0, 0]
-    pick = picker(rows_ref[...], RB)
-    hot = adder(cols_ref[...], CB, live)
-    pick_ref[...] = pick
-    hot_ref[...] = hot
+    pick_ref[...] = picker(rows_ref[...], RB)
+    hot_ref[...] = adder(cols_ref[...], CB, live)
     blocks_refs = (first_ref, second_ref)
-    adjoint_tail(live, data_ref[...], pick, hot, blocks_refs, keep_ref, send_ref, picked_ref, products_ref)
+    adjoint_tail(live, data_ref[...], pick_ref, hot_ref, blocks_refs, keep_ref, send_ref, picked_ref, products_ref)
 
 
 def forward_sum(own_ref, one_ref, two_ref, three_ref):
@@ -149,7 +177,7 @@
     alpha2 = joined_rows(whole[RB:])
     alpha = jnp.sqrt(alpha2)
     beta = jnp.sqrt(beta2_ref[0:1, :])
-    return whole[:RB] / alpha - alpha * (data_ref[...] / beta), alpha2
+    return whole[:RB] * (1.0 / alpha) - data_ref[...] * (alpha / beta), alpha2
 
 
 def second_adjoint(
@@ -176,7 +204,7 @@
     alpha2_ref[...] = jnp.broadcast_to(alpha2, alpha2_ref.shape)
     blocks_refs = (first_ref, second_ref)
     adjoint_tail(
-        live_ref[0, 0], data, pick_ref[...], hot_ref[...], blocks_refs, keep_ref, send_ref, picked_ref, products_ref
+        live_ref[0, 0], data, pick_ref, hot_ref, blocks_refs, keep_ref, send_ref, picked_ref, products_ref
     )
 
 
@@ -199,7 +227,7 @@
 
 def first_model(own_ref, one_ref, two_ref, three_ref, turned_ref, model_ref, send_ref, beta2_ref):
     total, beta2 = model_sum(own_ref, one_ref, two_ref, three_ref)
-    model_out(total / jnp.sqrt(beta2), beta2, model_ref, send_ref, beta2_ref)
+    model_out(total * (1.0 / jnp.sqrt(beta2)), beta2, model_ref, send_ref, beta2_ref)
 
 
 def second_model(
@@ -207,15 +235,15 @@
 ):
     total, beta2 = model_sum(own_ref, one_ref, two_ref, three_ref)
     beta = jnp.sqrt(beta2)
-    last = last_ref[...] / jnp.sqrt(alpha2_ref[0:1, :])
-    model_out(total / beta - beta * last, beta2, model_ref, send_ref, beta2_ref)
+    alpha = jnp.sqrt(alpha2_ref[0:1, :])
+    model_out(total * (1.0 / beta) - last_ref[...] * (beta / alpha), beta2, model_ref, send_ref, beta2_ref)
 
 
 def forward(live_ref, own_ref, got_ref, pick_ref, hot_ref, blocks_ref, out_ref, picked_ref, products_ref):
     model = jnp.concatenate([own_ref[:HALF, :], got_ref[:HALF, :]], 0)
-    picked_ref[...] = jnp.dot(pick_ref[...], model, preferred_element_type=F32).astype(BF16)
+    gather(pick_ref, model, picked_ref)
     multiply((blocks_ref,), picked_ref, products_ref)
-    out_ref[:RB, :] = scatter(products_ref[...], hot_ref[...], live_ref[0, 0]).astype(BF16)
+    out_ref[:RB, :] = scatter(products_ref, hot_ref, live_ref[0, 0]).astype(BF16)
     out_ref[RB:, :] = split_rows(joined_rows(own_ref[HALF:, :]) + joined_rows(got_ref[HALF:, :]))
 
 
@@ -320,7 +348,7 @@
 
 
 def load_second(after_ref, blocks_ref, tile_ref, sems):
-    large = read(blocks_ref, tile_ref, sems, tile_ref.shape[0])
+    large = read(blocks_ref, tile_ref, sems, blocks_ref.shape[0] - tile_ref.shape[0])
     for copy in large:
         copy.start()
     for copy in large:
@@ -330,10 +358,11 @@
 def transpose(live_ref, after_ref, rows_ref, cols_ref, first_ref, second_ref, out_ref, pick_ref, hot_ref):
     pick_ref[...] = picker(cols_ref[...], CB)
     hot_ref[...] = adder(rows_ref[...], RB, live_ref[0, 0])
-    half = first_ref.shape[0]
-    for slot in range(half):
-        out_ref[slot] = jnp.transpose(first_ref[slot])
-        out_ref[half + slot] = jnp.transpose(second_ref[slot])
+    base = 0
+    for ref in (first_ref, second_ref):
+        for slot in range(ref.shape[0]):
+            out_ref[base + slot] = jnp.transpose(ref[slot])
+        base += ref.shape[0]
 
 
 def collect(own_ref, one_ref, two_ref, three_ref, after_ref, out_ref):
@@ -395,7 +424,9 @@
     inputs = [
         pltpu.with_memory_space_constraint(x, pltpu.HBM) for x in (rhs, block_rows[0], block_cols[0], blocks[0, 0])
     ]
-    tile_shape = pltpu.VMEM((slots // 2, BS, BS), BF16)
+    early = slots * 3 // 8
+    first_shape = pltpu.VMEM((early, BS, BS), BF16)
+    second_shape = pltpu.VMEM((slots - early, BS, BS), BF16)
     params = pltpu.CompilerParams(vmem_limit_bytes=16 * 2**20)
     cost = pl.CostEstimate(flops=0, bytes_accessed=slots * BS * BS * 2, transcendentals=0)
     data, rows, cols, first = pl.pallas_call(
@@ -404,7 +435,7 @@
             jax.ShapeDtypeStruct(rhs.shape, F32),
             jax.ShapeDtypeStruct((1, slots), jnp.int32),
             jax.ShapeDtypeStruct((1, slots), jnp.int32),
-            tile_shape,
+            first_shape,
         ],
         in_specs=[SCALAR] * 4 + [lies] * 4,
         out_specs=[VECTOR] * 4,
@@ -421,7 +452,7 @@
     (quarter,) = call(collect, [(4 * SHARE, F32)], [data, *over_places(rhs, NEAR), first])
     second = pl.pallas_call(
         load_second,
-        out_shape=tile_shape,
+        out_shape=second_shape,
         in_specs=[VECTOR, lies],
         out_specs=VECTOR,
         scratch_shapes=[pltpu.SemaphoreType.DMA((LOADS,))],

time: 97.9 us -> 97.1 us (level)
  starting transfers between devices: 42.8 us -> 44.3 us
  Pallas kernels: 20.9 us -> 19.5 us
    ppermute x5, starting transfers between devices: 6.86 us -> 8.62 us  [over_core(): return lax.ppermute(x, 'dp', [(i, i ^ 1) for i in range(8)])]
    pallas_call x14, Pallas kernels: 11.7 us -> 10.3 us  [call(): pl.pallas_call(kernel, out_shape=[jax.ShapeDtypeStruct((rows, *(width or...]
where the time goes in v4:
time: 97.1 us; the launch traced here: 97 us
  starting transfers between devices  44.3 us (46%)
  waiting for transfers between devices  32.4 us (33%)
  Pallas kernels  19.5 us (20%)
    ppermute x12, waiting for transfers between devices, over_square(): lax.ppermute(x, ('dp', 'mp'), [(i * 16 + j, i * 16 + (j ^ step[i & 1])) f...  16.8 us
    ppermute x12, starting transfers between devices, over_square(): lax.ppermute(x, ('dp', 'mp'), [(i * 16 + j, i * 16 + (j ^ step[i & 1])) f...  15.9 us
    ppermute x9, starting transfers between devices, over_chips(): lax.ppermute(x, 'dp', [(i, (i >> 1 ^ step[i & 1]) * 2 + (i & 1)) for i in...  11 us
    ppermute x9, waiting for transfers between devices, over_chips(): lax.ppermute(x, 'dp', [(i, (i >> 1 ^ step[i & 1]) * 2 + (i & 1)) for i in...  10.5 us
    pallas_call x14, Pallas kernels, call(): pl.pallas_call(kernel, out_shape=[jax.ShapeDtypeStruct((rows, *(width or...  10.3 us
    ppermute x6, starting transfers between devices, over_places(): lax.ppermute(x, 'mp', [(j, j ^ step) for j in range(16)])  8.72 us
    ppermute x5, starting transfers between devices, over_core(): return lax.ppermute(x, 'dp', [(i, i ^ 1) for i in range(8)])  8.62 us
    ppermute x5, waiting for transfers between devices, over_core(): return lax.ppermute(x, 'dp', [(i, i ^ 1) for i in range(8)])  4.62 us
  transfers between devices with their start and end apart: 32, of which 24 were waited for; matrix products, arithmetic and copies ran while one was open for 0% of the time, Pallas kernels for 9%

profile of v4, /device:TPU:1, one launch (start us, length us, event | category | flops | bytes accessed | tf_op | source)
XLA Modules:
  0.0 97.0 jit_solution(18069764721147008634)
XLA Ops:
  0.0 3.6 %collective-permute-start = (f32[32,128]{1,0:T(8,128)}, f32[32,128]{1,0:T(8,128)S(1)}, u32[]{:S(2)}, u32[]{:S(2)}) collective-permute-start(f32[32,128]{1,0:T(8,128)} %data_ref.1), channel_id=1, source_target_pairs={{0,3},{1,2},{2,1},{3,0},{4,7},{5,6},{6,5},{7,4},{8,11},{9,10},{10,... | collective-permute-start | bytes 49160 | tf_op jit(solution)/shard_map/ppermute | solution.py:417
  5.4 2.4 %load_first.1 = (f32[32,128]{1,0:T(8,128)S(1)}, s32[1,384]{1,0:T(1,128)S(1)}, s32[1,384]{1,0:T(1,128)S(1)}, bf16[144,128,128]{2,1,0:T(8,128)(2,1)S(1)}) custom-call(s32[1]{0:T(128)} %bitcast.2.core_ref, s32[1]{0:T(128)} %bitcast.chip_ref, s32[1]{0:T(128)} %bitcast.1.place_ref, s32[1,1]{1,0:T(1,128)S(6)} %copy.6.live_ref, f32[32,128]{1,0:T(8,128)} %data_ref.1, ...), custom_call_target="tpu_custom_call" | custom-call | bytes 12582912 | tf_op jit(solution)/shard_map/load_first/pallas_call | solution.py:432
  12.4 3.3 %load_second.1.second_ref = bf16[240,128,128]{2,1,0:T(8,128)(2,1)S(1)} custom-call(f32[128,128]{1,0:T(8,128)S(1)} %collect.1.after_ref.own_ref, bf16[384,128,128]{2,1,0:T(8,128)(2,1)} %bitcast.7), custom_call_target="tpu_custom_call" | custom-call | bytes 12582912 | tf_op jit(solution)/shard_map/load_second/pallas_call | solution.py:453
  15.8 2.2 %first_adjoint.1 = (f32[512,128]{1,0:T(8,128)S(1)}, bf16[384,512]{1,0:T(8,128)(2,1)S(1)}, bf16[768,384]{1,0:T(8,128)(2,1)S(1)}, f32[384,128]{1,0:T(8,128)S(1)}, bf16[400,128]{1,0:T(8,128)(2,1)S(1)}) custom-call(s32[1,1]{1,0:T(1,128)S(6)} %copy.6.live_ref, s32[1]{0:T(128)} %bitcast.1.place_ref, f32[128,128]{1,0:T(8,128)S(1)} %collect.1.after_ref.own_ref, ...), custom_call_target="tpu_custom_call" | custom-call | tf_op jit(solution)/shard_map/first_adjoint/pallas_call | solution.py:380
  18.0 3.0 %collective-permute-start.6 = (bf16[400,128]{1,0:T(8,128)(2,1)S(1)}, bf16[400,128]{1,0:T(8,128)(2,1)S(1)}, u32[]{:S(2)}, u32[]{:S(2)}) collective-permute-start(bf16[400,128]{1,0:T(8,128)(2,1)S(1)} %get-tuple-element.34.send_ref), channel_id=1, source_target_pairs={{0,16},{16,0},{32,48},{48,32},{64,80},{80,64},{96,112},{112,96},{1... | collective-permute-start | bytes 307208 | tf_op jit(solution)/shard_map/ppermute | solution.py:399
  22.0 3.7 %collective-permute-start.9 = (bf16[400,128]{1,0:T(8,128)(2,1)S(1)}, bf16[400,128]{1,0:T(8,128)(2,1)S(1)}, u32[]{:S(2)}, u32[]{:S(2)}) collective-permute-start(bf16[400,128]{1,0:T(8,128)(2,1)S(1)} %chip_sum.2.after_ref.own_ref), channel_id=1, source_target_pairs={{0,64},{16,80},{32,96},{48,112},{64,0},{80,16},{96,32},{112,48},{1... | collective-permute-start | bytes 307208 | tf_op jit(solution)/shard_map/ppermute | solution.py:404
  26.4 3.4 %transpose.1 = (bf16[384,128,128]{2,1,0:T(8,128)(2,1)S(1)}, bf16[384,768]{1,0:T(8,128)(2,1)S(1)}, bf16[512,384]{1,0:T(8,128)(2,1)S(1)}) custom-call(s32[1,1]{1,0:T(1,128)S(6)} %copy.6.live_ref, bf16[400,128]{1,0:T(8,128)(2,1)S(1)} %chip_sum.2.after_ref.own_ref, s32[1,384]{1,0:T(1,128)S(1)} %get-tuple-element.31.rows_ref, ...), custom_call_target="tpu_custom_call" | custom-call | bytes 12582912 | tf_op jit(solution)/shard_map/transpose/pallas_call | solution.py:481
  34.1 2.1 %forward.2.own_ref = bf16[528,128]{1,0:T(8,128)(2,1)S(1)} custom-call(s32[1,1]{1,0:T(1,128)S(6)} %copy.6.live_ref, bf16[400,128]{1,0:T(8,128)(2,1)S(1)} %get-tuple-element.36.own_ref, bf16[400,128]{1,0:T(8,128)(2,1)S(1)} %collective-permute-done.10.got_ref, bf16[384,768]{1,0:T(8,128)(2,1)S(1)} %get-tuple-element.37.pick_ref, ...), custom_call_target="tpu_custom_call" | custom-call | tf_op jit(solution)/shard_map/forward/pallas_call | solution.py:380
  36.2 2.9 %collective-permute-start.13 = (bf16[528,128]{1,0:T(8,128)(2,1)S(1)}, bf16[528,128]{1,0:T(8,128)(2,1)S(1)}, u32[]{:S(2)}, u32[]{:S(2)}) collective-permute-start(bf16[528,128]{1,0:T(8,128)(2,1)S(1)} %forward.2.own_ref), channel_id=1, source_target_pairs={{0,7},{1,6},{2,5},{3,4},{4,3},{5,2},{6,1},{7,0},{8,15},{9,14},{10,... | collective-permute-start | bytes 405512 | tf_op jit(solution)/shard_map/ppermute | solution.py:410
  40.2 2.4 %collective-permute-done.13.three_ref = bf16[528,128]{1,0:T(8,128)(2,1)S(1)} collective-permute-done((bf16[528,128]{1,0:T(8,128)(2,1)S(1)}, bf16[528,128]{1,0:T(8,128)(2,1)S(1)}, u32[]{:S(2)}, u32[]{:S(2)}) %collective-permute-start.13) | collective-permute-done | bytes 135200 | tf_op jit(solution)/shard_map/ppermute | solution.py:410
  42.6 1.9 %collective-permute-done.12.two_ref = bf16[528,128]{1,0:T(8,128)(2,1)S(1)} collective-permute-done((bf16[528,128]{1,0:T(8,128)(2,1)S(1)}, bf16[528,128]{1,0:T(8,128)(2,1)S(1)}, u32[]{:S(2)}, u32[]{:S(2)}) %collective-permute-start.12) | collective-permute-done | bytes 135200 | tf_op jit(solution)/shard_map/ppermute | solution.py:410
  44.9 2.7 %collective-permute-start.15 = (bf16[528,128]{1,0:T(8,128)(2,1)S(1)}, bf16[528,128]{1,0:T(8,128)(2,1)S(1)}, u32[]{:S(2)}, u32[]{:S(2)}) collective-permute-start(bf16[528,128]{1,0:T(8,128)(2,1)S(1)} %row_sum.2.own_ref), channel_id=1, source_target_pairs={{0,12},{1,13},{2,14},{3,15},{4,8},{5,9},{6,10},{7,11},{8,4},{9,5},... | collective-permute-start | bytes 405512 | tf_op jit(solution)/shard_map/ppermute | solution.py:410
  48.7 2.1 %collective-permute-done.16.three_ref = bf16[528,128]{1,0:T(8,128)(2,1)S(1)} collective-permute-done((bf16[528,128]{1,0:T(8,128)(2,1)S(1)}, bf16[528,128]{1,0:T(8,128)(2,1)S(1)}, u32[]{:S(2)}, u32[]{:S(2)}) %collective-permute-start.16) | collective-permute-done | bytes 135200 | tf_op jit(solution)/shard_map/ppermute | solution.py:410
  52.9 2.2 %second_adjoint.1 = (f32[512,128]{1,0:T(8,128)S(1)}, f32[8,128]{1,0:T(8,128)S(1)}, f32[384,128]{1,0:T(8,128)S(1)}, bf16[400,128]{1,0:T(8,128)(2,1)S(1)}) custom-call(s32[1,1]{1,0:T(1,128)S(6)} %copy.6.live_ref, bf16[528,128]{1,0:T(8,128)(2,1)S(1)} %row_sum.2.own_ref, bf16[528,128]{1,0:T(8,128)(2,1)S(1)} %collective-permute-done.14.one_ref, ...), custom_call_target="tpu_custom_call" | custom-call | tf_op jit(solution)/shard_map/second_adjoint/pallas_call | solution.py:380
  55.1 2.4 %collective-permute-start.17 = (bf16[400,128]{1,0:T(8,128)(2,1)S(1)}, bf16[400,128]{1,0:T(8,128)(2,1)S(1)}, u32[]{:S(2)}, u32[]{:S(2)}) collective-permute-start(bf16[400,128]{1,0:T(8,128)(2,1)S(1)} %get-tuple-element.44.send_ref), channel_id=1, source_target_pairs={{0,16},{16,0},{32,48},{48,32},{64,80},{80,64},{96,112},{112,96},{1... | collective-permute-start | bytes 307208 | tf_op jit(solution)/shard_map/ppermute | solution.py:399
  58.5 1.8 %collective-permute-start.20 = (bf16[400,128]{1,0:T(8,128)(2,1)S(1)}, bf16[400,128]{1,0:T(8,128)(2,1)S(1)}, u32[]{:S(2)}, u32[]{:S(2)}) collective-permute-start(bf16[400,128]{1,0:T(8,128)(2,1)S(1)} %chip_sum.3.own_ref), channel_id=1, source_target_pairs={{0,64},{16,80},{32,96},{48,112},{64,0},{80,16},{96,32},{112,48},{1... | collective-permute-start | bytes 307208 | tf_op jit(solution)/shard_map/ppermute | solution.py:404
  61.8 2.4 %collective-permute-done.20.three_ref = bf16[400,128]{1,0:T(8,128)(2,1)S(1)} collective-permute-done((bf16[400,128]{1,0:T(8,128)(2,1)S(1)}, bf16[400,128]{1,0:T(8,128)(2,1)S(1)}, u32[]{:S(2)}, u32[]{:S(2)}) %collective-permute-start.20) | collective-permute-done | bytes 102432 | tf_op jit(solution)/shard_map/ppermute | solution.py:404
  69.2 2.1 %forward.3.own_ref = bf16[528,128]{1,0:T(8,128)(2,1)S(1)} custom-call(s32[1,1]{1,0:T(1,128)S(6)} %copy.6.live_ref, bf16[400,128]{1,0:T(8,128)(2,1)S(1)} %get-tuple-element.47.own_ref, bf16[400,128]{1,0:T(8,128)(2,1)S(1)} %collective-permute-done.21.got_ref, bf16[384,768]{1,0:T(8,128)(2,1)S(1)} %get-tuple-element.37.pick_ref, ...), custom_call_target="tpu_custom_call" | custom-call | tf_op jit(solution)/shard_map/forward/pallas_call | solution.py:380
  71.3 2.9 %collective-permute-start.24 = (bf16[528,128]{1,0:T(8,128)(2,1)S(1)}, bf16[528,128]{1,0:T(8,128)(2,1)S(1)}, u32[]{:S(2)}, u32[]{:S(2)}) collective-permute-start(bf16[528,128]{1,0:T(8,128)(2,1)S(1)} %forward.3.own_ref), channel_id=1, source_target_pairs={{0,7},{1,6},{2,5},{3,4},{4,3},{5,2},{6,1},{7,0},{8,15},{9,14},{10,... | collective-permute-start | bytes 405512 | tf_op jit(solution)/shard_map/ppermute | solution.py:410
  75.2 2.4 %collective-permute-done.24.three_ref = bf16[528,128]{1,0:T(8,128)(2,1)S(1)} collective-permute-done((bf16[528,128]{1,0:T(8,128)(2,1)S(1)}, bf16[528,128]{1,0:T(8,128)(2,1)S(1)}, u32[]{:S(2)}, u32[]{:S(2)}) %collective-permute-start.24) | collective-permute-done | bytes 135200 | tf_op jit(solution)/shard_map/ppermute | solution.py:410
  77.6 2.0 %collective-permute-done.23.two_ref = bf16[528,128]{1,0:T(8,128)(2,1)S(1)} collective-permute-done((bf16[528,128]{1,0:T(8,128)(2,1)S(1)}, bf16[528,128]{1,0:T(8,128)(2,1)S(1)}, u32[]{:S(2)}, u32[]{:S(2)}) %collective-permute-start.23) | collective-permute-done | bytes 135200 | tf_op jit(solution)/shard_map/ppermute | solution.py:410
  79.8 2.3 %collective-permute-start.26 = (bf16[528,128]{1,0:T(8,128)(2,1)S(1)}, bf16[528,128]{1,0:T(8,128)(2,1)S(1)}, u32[]{:S(2)}, u32[]{:S(2)}) collective-permute-start(bf16[528,128]{1,0:T(8,128)(2,1)S(1)} %row_sum.3.own_ref), channel_id=1, source_target_pairs={{0,12},{1,13},{2,14},{3,15},{4,8},{5,9},{6,10},{7,11},{8,4},{9,5},... | collective-permute-start | bytes 405512 | tf_op jit(solution)/shard_map/ppermute | solution.py:410
  83.6 2.1 %collective-permute-done.27.three_ref = bf16[528,128]{1,0:T(8,128)(2,1)S(1)} collective-permute-done((bf16[528,128]{1,0:T(8,128)(2,1)S(1)}, bf16[528,128]{1,0:T(8,128)(2,1)S(1)}, u32[]{:S(2)}, u32[]{:S(2)}) %collective-permute-start.27) | collective-permute-done | bytes 135200 | tf_op jit(solution)/shard_map/ppermute | solution.py:410
  87.8 1.9 %collective-permute-start.28 = (f32[8,128]{1,0:T(8,128)S(1)}, f32[8,128]{1,0:T(8,128)S(1)}, u32[]{:S(2)}, u32[]{:S(2)}) collective-permute-start(f32[8,128]{1,0:T(8,128)S(1)} %get-tuple-element.50.own_ref), channel_id=1, source_target_pairs={{0,16},{16,0},{32,48},{48,32},{64,80},{80,64},{96,112},{112,96},{1... | collective-permute-start | bytes 12296 | tf_op jit(solution)/shard_map/ppermute | solution.py:399
  (57 shorter events, 35.8 us)
Async XLA Ops:
  0.0 7.9 %collective-permute-start = (f32[32,128]{1,0:T(8,128)}, f32[32,128]{1,0:T(8,128)S(1)}, u32[]{:S(2)}, u32[]{:S(2)}) collective-permute-start(f32[32,128]{1,0:T(8,128)} %data_ref.1), channel_id=1, source_target_pairs={{0,3},{1,2},{2,1},{3,0},{4,7},{5,6},{6,5},{7,4},{8,11},{9,10},{10,... | collective-permute-start | bytes 49160 | tf_op jit(solution)/shard_map/ppermute | solution.py:417
  3.6 4.9 %collective-permute-start.2 = (f32[32,128]{1,0:T(8,128)}, f32[32,128]{1,0:T(8,128)S(1)}, u32[]{:S(2)}, u32[]{:S(2)}) collective-permute-start(f32[32,128]{1,0:T(8,128)} %data_ref.1), channel_id=1, source_target_pairs={{0,7},{1,6},{2,5},{3,4},{4,3},{5,2},{6,1},{7,0},{8,15},{9,14},{10,... | collective-permute-start | bytes 49160 | tf_op jit(solution)/shard_map/ppermute | solution.py:417
  4.5 4.0 %collective-permute-start.1 = (f32[32,128]{1,0:T(8,128)}, f32[32,128]{1,0:T(8,128)S(1)}, u32[]{:S(2)}, u32[]{:S(2)}) collective-permute-start(f32[32,128]{1,0:T(8,128)} %data_ref.1), channel_id=1, source_target_pairs={{0,4},{1,5},{2,6},{3,7},{4,0},{5,1},{6,2},{7,3},{8,12},{9,13},{10,... | collective-permute-start | bytes 49160 | tf_op jit(solution)/shard_map/ppermute | solution.py:417
  8.5 7.3 %collective-permute-start.5 = (f32[128,128]{1,0:T(8,128)S(1)}, f32[128,128]{1,0:T(8,128)S(1)}, u32[]{:S(2)}, u32[]{:S(2)}) collective-permute-start(f32[128,128]{1,0:T(8,128)S(1)} %collect.1.after_ref.own_ref), channel_id=1, source_target_pairs={{0,13},{1,12},{2,15},{3,14},{4,9},{5,8},{6,11},{7,10},{8,5},{9,4},... | collective-permute-start | bytes 196616 | tf_op jit(solution)/shard_map/ppermute | solution.py:417
  10.2 5.6 %collective-permute-start.4 = (f32[128,128]{1,0:T(8,128)S(1)}, f32[128,128]{1,0:T(8,128)S(1)}, u32[]{:S(2)}, u32[]{:S(2)}) collective-permute-start(f32[128,128]{1,0:T(8,128)S(1)} %collect.1.after_ref.own_ref), channel_id=1, source_target_pairs={{0,12},{1,13},{2,14},{3,15},{4,8},{5,9},{6,10},{7,11},{8,4},{9,5},... | collective-permute-start | bytes 196616 | tf_op jit(solution)/shard_map/ppermute | solution.py:417
  11.1 4.6 %collective-permute-start.3 = (f32[128,128]{1,0:T(8,128)S(1)}, f32[128,128]{1,0:T(8,128)S(1)}, u32[]{:S(2)}, u32[]{:S(2)}) collective-permute-start(f32[128,128]{1,0:T(8,128)S(1)} %collect.1.after_ref.own_ref), channel_id=1, source_target_pairs={{0,1},{1,0},{2,3},{3,2},{4,5},{5,4},{6,7},{7,6},{8,9},{9,8},{10,11... | collective-permute-start | bytes 196616 | tf_op jit(solution)/shard_map/ppermute | solution.py:417
  22.0 7.9 %collective-permute-start.9 = (bf16[400,128]{1,0:T(8,128)(2,1)S(1)}, bf16[400,128]{1,0:T(8,128)(2,1)S(1)}, u32[]{:S(2)}, u32[]{:S(2)}) collective-permute-start(bf16[400,128]{1,0:T(8,128)(2,1)S(1)} %chip_sum.2.after_ref.own_ref), channel_id=1, source_target_pairs={{0,64},{16,80},{32,96},{48,112},{64,0},{80,16},{96,32},{112,48},{1... | collective-permute-start | bytes 307208 | tf_op jit(solution)/shard_map/ppermute | solution.py:404
  25.7 5.6 %collective-permute-start.8 = (bf16[400,128]{1,0:T(8,128)(2,1)S(1)}, bf16[400,128]{1,0:T(8,128)(2,1)S(1)}, u32[]{:S(2)}, u32[]{:S(2)}) collective-permute-start(bf16[400,128]{1,0:T(8,128)(2,1)S(1)} %chip_sum.2.after_ref.own_ref), channel_id=1, source_target_pairs={{0,96},{16,48},{32,64},{48,16},{64,32},{80,112},{96,0},{112,80},{1... | collective-permute-start | bytes 307208 | tf_op jit(solution)/shard_map/ppermute | solution.py:404
  26.4 5.8 %collective-permute-start.7 = (bf16[400,128]{1,0:T(8,128)(2,1)S(1)}, bf16[400,128]{1,0:T(8,128)(2,1)S(1)}, u32[]{:S(2)}, u32[]{:S(2)}) collective-permute-start(bf16[400,128]{1,0:T(8,128)(2,1)S(1)} %chip_sum.2.after_ref.own_ref), channel_id=1, source_target_pairs={{0,32},{16,112},{32,0},{48,80},{64,96},{80,48},{96,64},{112,16},{1... | collective-permute-start | bytes 307208 | tf_op jit(solution)/shard_map/ppermute | solution.py:404
  36.2 6.3 %collective-permute-start.13 = (bf16[528,128]{1,0:T(8,128)(2,1)S(1)}, bf16[528,128]{1,0:T(8,128)(2,1)S(1)}, u32[]{:S(2)}, u32[]{:S(2)}) collective-permute-start(bf16[528,128]{1,0:T(8,128)(2,1)S(1)} %forward.2.own_ref), channel_id=1, source_target_pairs={{0,7},{1,6},{2,5},{3,4},{4,3},{5,2},{6,1},{7,0},{8,15},{9,14},{10,... | collective-permute-start | bytes 405512 | tf_op jit(solution)/shard_map/ppermute | solution.py:410
  39.1 5.4 %collective-permute-start.12 = (bf16[528,128]{1,0:T(8,128)(2,1)S(1)}, bf16[528,128]{1,0:T(8,128)(2,1)S(1)}, u32[]{:S(2)}, u32[]{:S(2)}) collective-permute-start(bf16[528,128]{1,0:T(8,128)(2,1)S(1)} %forward.2.own_ref), channel_id=1, source_target_pairs={{0,4},{1,5},{2,6},{3,7},{4,0},{5,1},{6,2},{7,3},{8,12},{9,13},{10,... | collective-permute-start | bytes 405512 | tf_op jit(solution)/shard_map/ppermute | solution.py:410
  40.1 4.4 %collective-permute-start.11 = (bf16[528,128]{1,0:T(8,128)(2,1)S(1)}, bf16[528,128]{1,0:T(8,128)(2,1)S(1)}, u32[]{:S(2)}, u32[]{:S(2)}) collective-permute-start(bf16[528,128]{1,0:T(8,128)(2,1)S(1)} %forward.2.own_ref), channel_id=1, source_target_pairs={{0,3},{1,2},{2,1},{3,0},{4,7},{5,6},{6,5},{7,4},{8,11},{9,10},{10,... | collective-permute-start | bytes 405512 | tf_op jit(solution)/shard_map/ppermute | solution.py:410
  44.6 6.2 %collective-permute-start.16 = (bf16[528,128]{1,0:T(8,128)(2,1)S(1)}, bf16[528,128]{1,0:T(8,128)(2,1)S(1)}, u32[]{:S(2)}, u32[]{:S(2)}) collective-permute-start(bf16[528,128]{1,0:T(8,128)(2,1)S(1)} %row_sum.2.own_ref), channel_id=1, source_target_pairs={{0,13},{1,12},{2,15},{3,14},{4,9},{5,8},{6,11},{7,10},{8,5},{9,4},... | collective-permute-start | bytes 405512 | tf_op jit(solution)/shard_map/ppermute | solution.py:410
  44.9 6.5 %collective-permute-start.15 = (bf16[528,128]{1,0:T(8,128)(2,1)S(1)}, bf16[528,128]{1,0:T(8,128)(2,1)S(1)}, u32[]{:S(2)}, u32[]{:S(2)}) collective-permute-start(bf16[528,128]{1,0:T(8,128)(2,1)S(1)} %row_sum.2.own_ref), channel_id=1, source_target_pairs={{0,12},{1,13},{2,14},{3,15},{4,8},{5,9},{6,10},{7,11},{8,4},{9,5},... | collective-permute-start | bytes 405512 | tf_op jit(solution)/shard_map/ppermute | solution.py:410
  47.5 5.4 %collective-permute-start.14 = (bf16[528,128]{1,0:T(8,128)(2,1)S(1)}, bf16[528,128]{1,0:T(8,128)(2,1)S(1)}, u32[]{:S(2)}, u32[]{:S(2)}) collective-permute-start(bf16[528,128]{1,0:T(8,128)(2,1)S(1)} %row_sum.2.own_ref), channel_id=1, source_target_pairs={{0,1},{1,0},{2,3},{3,2},{4,5},{5,4},{6,7},{7,6},{8,9},{9,8},{10,11... | collective-permute-start | bytes 405512 | tf_op jit(solution)/shard_map/ppermute | solution.py:410
  58.5 5.7 %collective-permute-start.20 = (bf16[400,128]{1,0:T(8,128)(2,1)S(1)}, bf16[400,128]{1,0:T(8,128)(2,1)S(1)}, u32[]{:S(2)}, u32[]{:S(2)}) collective-permute-start(bf16[400,128]{1,0:T(8,128)(2,1)S(1)} %chip_sum.3.own_ref), channel_id=1, source_target_pairs={{0,64},{16,80},{32,96},{48,112},{64,0},{80,16},{96,32},{112,48},{1... | collective-permute-start | bytes 307208 | tf_op jit(solution)/shard_map/ppermute | solution.py:404
  60.3 5.5 %collective-permute-start.19 = (bf16[400,128]{1,0:T(8,128)(2,1)S(1)}, bf16[400,128]{1,0:T(8,128)(2,1)S(1)}, u32[]{:S(2)}, u32[]{:S(2)}) collective-permute-start(bf16[400,128]{1,0:T(8,128)(2,1)S(1)} %chip_sum.3.own_ref), channel_id=1, source_target_pairs={{0,96},{16,48},{32,64},{48,16},{64,32},{80,112},{96,0},{112,80},{1... | collective-permute-start | bytes 307208 | tf_op jit(solution)/shard_map/ppermute | solution.py:404
  61.0 6.3 %collective-permute-start.18 = (bf16[400,128]{1,0:T(8,128)(2,1)S(1)}, bf16[400,128]{1,0:T(8,128)(2,1)S(1)}, u32[]{:S(2)}, u32[]{:S(2)}) collective-permute-start(bf16[400,128]{1,0:T(8,128)(2,1)S(1)} %chip_sum.3.own_ref), channel_id=1, source_target_pairs={{0,32},{16,112},{32,0},{48,80},{64,96},{80,48},{96,64},{112,16},{1... | collective-permute-start | bytes 307208 | tf_op jit(solution)/shard_map/ppermute | solution.py:404
  71.3 6.3 %collective-permute-start.24 = (bf16[528,128]{1,0:T(8,128)(2,1)S(1)}, bf16[528,128]{1,0:T(8,128)(2,1)S(1)}, u32[]{:S(2)}, u32[]{:S(2)}) collective-permute-start(bf16[528,128]{1,0:T(8,128)(2,1)S(1)} %forward.3.own_ref), channel_id=1, source_target_pairs={{0,7},{1,6},{2,5},{3,4},{4,3},{5,2},{6,1},{7,0},{8,15},{9,14},{10,... | collective-permute-start | bytes 405512 | tf_op jit(solution)/shard_map/ppermute | solution.py:410
  74.2 5.4 %collective-permute-start.23 = (bf16[528,128]{1,0:T(8,128)(2,1)S(1)}, bf16[528,128]{1,0:T(8,128)(2,1)S(1)}, u32[]{:S(2)}, u32[]{:S(2)}) collective-permute-start(bf16[528,128]{1,0:T(8,128)(2,1)S(1)} %forward.3.own_ref), channel_id=1, source_target_pairs={{0,4},{1,5},{2,6},{3,7},{4,0},{5,1},{6,2},{7,3},{8,12},{9,13},{10,... | collective-permute-start | bytes 405512 | tf_op jit(solution)/shard_map/ppermute | solution.py:410
  75.2 4.4 %collective-permute-start.22 = (bf16[528,128]{1,0:T(8,128)(2,1)S(1)}, bf16[528,128]{1,0:T(8,128)(2,1)S(1)}, u32[]{:S(2)}, u32[]{:S(2)}) collective-permute-start(bf16[528,128]{1,0:T(8,128)(2,1)S(1)} %forward.3.own_ref), channel_id=1, source_target_pairs={{0,3},{1,2},{2,1},{3,0},{4,7},{5,6},{6,5},{7,4},{8,11},{9,10},{10,... | collective-permute-start | bytes 405512 | tf_op jit(solution)/shard_map/ppermute | solution.py:410
  79.7 6.0 %collective-permute-start.27 = (bf16[528,128]{1,0:T(8,128)(2,1)S(1)}, bf16[528,128]{1,0:T(8,128)(2,1)S(1)}, u32[]{:S(2)}, u32[]{:S(2)}) collective-permute-start(bf16[528,128]{1,0:T(8,128)(2,1)S(1)} %row_sum.3.own_ref), channel_id=1, source_target_pairs={{0,13},{1,12},{2,15},{3,14},{4,9},{5,8},{6,11},{7,10},{8,5},{9,4},... | collective-permute-start | bytes 405512 | tf_op jit(solution)/shard_map/ppermute | solution.py:410
  79.8 6.5 %collective-permute-start.26 = (bf16[528,128]{1,0:T(8,128)(2,1)S(1)}, bf16[528,128]{1,0:T(8,128)(2,1)S(1)}, u32[]{:S(2)}, u32[]{:S(2)}) collective-permute-start(bf16[528,128]{1,0:T(8,128)(2,1)S(1)} %row_sum.3.own_ref), channel_id=1, source_target_pairs={{0,12},{1,13},{2,14},{3,15},{4,8},{5,9},{6,10},{7,11},{8,4},{9,5},... | collective-permute-start | bytes 405512 | tf_op jit(solution)/shard_map/ppermute | solution.py:410
  82.1 5.4 %collective-permute-start.25 = (bf16[528,128]{1,0:T(8,128)(2,1)S(1)}, bf16[528,128]{1,0:T(8,128)(2,1)S(1)}, u32[]{:S(2)}, u32[]{:S(2)}) collective-permute-start(bf16[528,128]{1,0:T(8,128)(2,1)S(1)} %row_sum.3.own_ref), channel_id=1, source_target_pairs={{0,1},{1,0},{2,3},{3,2},{4,5},{5,4},{6,7},{7,6},{8,9},{9,8},{10,11... | collective-permute-start | bytes 405512 | tf_op jit(solution)/shard_map/ppermute | solution.py:410
  (8 other events, 23.6 us)

commit v5 on v4

--- a/solution.py
+++ b/solution.py
@@ -53,12 +53,13 @@
     return jnp.concatenate(pieces, 0)
 
 
-def picker(index, size):
+def picker(index, size, live):
     at = column(index)
     lane = lax.broadcasted_iota(jnp.int32, at.shape, 1)
+    slot = lax.broadcasted_iota(jnp.int32, at.shape, 0)
     return jnp.concatenate(
         [
-            jnp.where(at == (lane + start).astype(F32), 1.0, 0.0).astype(BF16)
+            jnp.where((at == (lane + start).astype(F32)) & (slot < live), 1.0, 0.0).astype(BF16)
             for start in range(0, size, BS)
         ],
         1,
@@ -73,19 +74,17 @@
 
 
 def gather(pick_ref, source, picked_ref):
-    for start in reversed(range(0, picked_ref.shape[0], BS)):
+    for start in range(0, picked_ref.shape[0], BS):
         piece = jnp.dot(pick_ref[start : start + BS, :], source, preferred_element_type=F32)
         picked_ref[start : start + BS, :] = piece.astype(BF16)
 
 
-def scatter(products_ref, hot_ref, live):
+def scatter(products_ref, hot_ref):
     slots = products_ref.shape[0]
     total = 0.0
     for start in range(0, slots, 2 * BS):
         piece = slice(start, min(start + 2 * BS, slots))
         products = products_ref[piece, :]
-        slot = lax.broadcasted_iota(jnp.int32, products.shape, 0) + start
-        products = jnp.where(slot < live, products, 0.0)
         high = products.astype(BF16)
         low = (products - high.astype(F32)).astype(BF16)
         total += jnp.dot(hot_ref[:, piece], jnp.concatenate([high, low], 1), preferred_element_type=F32)
@@ -108,29 +107,28 @@
     slots = picked_ref.shape[0]
     singles = slots // 4
     groups = (slots - singles) // GROUP
-    first = groups * GROUP
     turned = []
-    for start in range(first, slots, BS):
-        rows = picked_ref[start : min(start + BS, slots), :].astype(F32)
+    for start in range(0, singles, BS):
+        rows = picked_ref[start : min(start + BS, singles), :].astype(F32)
         if rows.shape[0] < BS:
             rows = jnp.concatenate([rows, jnp.zeros((BS - rows.shape[0], BS), F32)], 0)
         turned.append(jnp.transpose(rows))
     for group in range(groups):
+        start = singles + group * GROUP
         for single in range(singles * group // groups, singles * (group + 1) // groups):
             weights = jnp.broadcast_to(turned[single // BS][:, single % BS : single % BS + 1], (BS, BS))
-            product = block(first + single, 1)[0].astype(F32) * weights
-            products_ref[first + single : first + single + 1, :] = jnp.sum(product, axis=0, keepdims=True)
-        start = group * GROUP
+            product = block(single, 1)[0].astype(F32) * weights
+            products_ref[single : single + 1, :] = jnp.sum(product, axis=0, keepdims=True)
         tile = block(start, GROUP).reshape(GROUP * BS, BS)
         products_ref[start : start + GROUP, :] = jnp.dot(
             spread(picked_ref[start : start + GROUP, :]), tile, preferred_element_type=F32
         )
 
 
-def adjoint_tail(live, data, pick_ref, hot_ref, blocks_refs, keep_ref, send_ref, picked_ref, products_ref):
+def adjoint_tail(data, pick_ref, hot_ref, blocks_refs, keep_ref, send_ref, picked_ref, products_ref):
     gather(pick_ref, data.astype(BF16), picked_ref)
     multiply(blocks_refs, picked_ref, products_ref)
-    partial = scatter(products_ref, hot_ref, live)
+    partial = scatter(products_ref, hot_ref)
     keep_ref[...] = partial[:HALF]
     send_ref[:HALF, :] = partial[HALF:].astype(BF16)
     send_ref[HALF:, :] = split_rows(square_sum(data))
@@ -138,7 +136,6 @@
 
 def first_adjoint(
     live_ref,
-    place_ref,
     own_ref,
     one_ref,
     two_ref,
@@ -156,15 +153,16 @@
     products_ref,
 ):
     near, far = square(*NEAR), square(*FAR)
+    place = lax.axis_index("mp")
     for step, ref in zip((0, *far), (own_ref, one_ref, two_ref, three_ref)):
         for piece, hop in enumerate((0, *near)):
-            at = pl.multiple_of((place_ref[0] ^ step ^ hop) * SHARE, SHARE)
+            at = pl.multiple_of((place ^ step ^ hop) * SHARE, SHARE)
             data_ref[pl.ds(at, SHARE), :] = ref[piece * SHARE : (piece + 1) * SHARE, :]
     live = live_ref[0, 0]
-    pick_ref[...] = picker(rows_ref[...], RB)
+    pick_ref[...] = picker(rows_ref[...], RB, live)
     hot_ref[...] = adder(cols_ref[...], CB, live)
     blocks_refs = (first_ref, second_ref)
-    adjoint_tail(live, data_ref[...], pick_ref, hot_ref, blocks_refs, keep_ref, send_ref, picked_ref, products_ref)
+    adjoint_tail(data_ref[...], pick_ref, hot_ref, blocks_refs, keep_ref, send_ref, picked_ref, products_ref)
 
 
 def forward_sum(own_ref, one_ref, two_ref, three_ref):
@@ -181,7 +179,6 @@
 
 
 def second_adjoint(
-    live_ref,
     own_ref,
     one_ref,
     two_ref,
@@ -204,7 +201,7 @@
     alpha2_ref[...] = jnp.broadcast_to(alpha2, alpha2_ref.shape)
     blocks_refs = (first_ref, second_ref)
     adjoint_tail(
-        live_ref[0, 0], data, pick_ref, hot_ref, blocks_refs, keep_ref, send_ref, picked_ref, products_ref
+        data, pick_ref, hot_ref, blocks_refs, keep_ref, send_ref, picked_ref, products_ref
     )
 
 
@@ -239,11 +236,11 @@
     model_out(total * (1.0 / beta) - last_ref[...] * (beta / alpha), beta2, model_ref, send_ref, beta2_ref)
 
 
-def forward(live_ref, own_ref, got_ref, pick_ref, hot_ref, blocks_ref, out_ref, picked_ref, products_ref):
+def forward(own_ref, got_ref, pick_ref, hot_ref, blocks_ref, out_ref, picked_ref, products_ref):
     model = jnp.concatenate([own_ref[:HALF, :], got_ref[:HALF, :]], 0)
     gather(pick_ref, model, picked_ref)
     multiply((blocks_ref,), picked_ref, products_ref)
-    out_ref[:RB, :] = scatter(products_ref, hot_ref, live_ref[0, 0]).astype(BF16)
+    out_ref[:RB, :] = scatter(products_ref, hot_ref).astype(BF16)
     out_ref[RB:, :] = split_rows(joined_rows(own_ref[HALF:, :]) + joined_rows(got_ref[HALF:, :]))
 
 
@@ -264,7 +261,6 @@
 
 
 def finish(
-    chip_ref,
     own_ref,
     one_ref,
     two_ref,
@@ -282,7 +278,7 @@
     beta1 = jnp.sqrt(beta1_ref[0:1, :])
     alpha1 = jnp.sqrt(alpha1_ref[0:1, :])
     beta2 = jnp.sqrt(forward_sum(own_ref, one_ref, two_ref, three_ref)[0:1, :])
-    chunk = pl.ds(pl.multiple_of(chip_ref[0] * CHUNK, CHUNK), CHUNK)
+    chunk = pl.ds(pl.multiple_of((lax.axis_index("dp") >> 1) * CHUNK, CHUNK), CHUNK)
     model0 = model0_ref[chunk, :] / alpha0
     model1 = model1_ref[chunk, :] / alpha1
     rho1 = jnp.sqrt(alpha0 * alpha0 + beta1 * beta1)
@@ -312,9 +308,6 @@
 
 
 def load_first(
-    core_ref,
-    chip_ref,
-    place_ref,
     live_ref,
     data_ref,
     rows_ref,
@@ -341,7 +334,7 @@
     chunk = jnp.zeros_like(cols)
     for edge in range(CHUNK, CB, CHUNK):
         chunk += jnp.where(cols >= edge, 1, 0)
-    half = jnp.where((chunk & 1) == core_ref[0], 0, HALF)
+    half = jnp.where((chunk & 1) == (lax.axis_index("dp") & 1), 0, HALF)
     cols_out[...] = half + (chunk >> 1) * CHUNK + cols - chunk * CHUNK
     for copy in small[1:] + large:
         copy.wait()
@@ -356,7 +349,7 @@
 
 
 def transpose(live_ref, after_ref, rows_ref, cols_ref, first_ref, second_ref, out_ref, pick_ref, hot_ref):
-    pick_ref[...] = picker(cols_ref[...], CB)
+    pick_ref[...] = picker(cols_ref[...], CB, live_ref[0, 0])
     hot_ref[...] = adder(rows_ref[...], RB, live_ref[0, 0])
     base = 0
     for ref in (first_ref, second_ref):
@@ -390,10 +383,6 @@
 
 def body(rhs, blocks, block_rows, block_cols, counts):
     slots = blocks.shape[2]
-    group = lax.axis_index("dp")
-    core = (group & 1)[None]
-    chip = (group >> 1)[None]
-    place = lax.axis_index("mp")[None]
 
     def over_core(x):
         return lax.ppermute(x, "dp", [(i, i ^ 1) for i in range(8)])
@@ -437,7 +426,7 @@
             jax.ShapeDtypeStruct((1, slots), jnp.int32),
             first_shape,
         ],
-        in_specs=[SCALAR] * 4 + [lies] * 4,
+        in_specs=[SCALAR] + [lies] * 4,
         out_specs=[VECTOR] * 4,
         scratch_shapes=[
             pltpu.VMEM((1, slots), jnp.int32),
@@ -447,7 +436,7 @@
         compiler_params=params,
         cost_estimate=cost,
         name="load_first",
-    )(core, chip, place, counts, *inputs)
+    )(counts, *inputs)
     first = pltpu.with_memory_space_constraint(first, pltpu.VMEM)
     (quarter,) = call(collect, [(4 * SHARE, F32)], [data, *over_places(rhs, NEAR), first])
     second = pl.pallas_call(
@@ -463,7 +452,7 @@
     second = pltpu.with_memory_space_constraint(second, pltpu.VMEM)
 
     def forward_whole(own):
-        (part,) = call(forward, [(RB + EXTRA, BF16)], [own, over_core(own), pick_cols, add_rows, turned], [counts], slots)
+        (part,) = call(forward, [(RB + EXTRA, BF16)], [own, over_core(own), pick_cols, add_rows, turned], (), slots)
         (part,) = call(row_sum, [(RB + EXTRA, BF16)], [part, *over_square(part, NEAR)])
         return [part, *over_square(part, FAR)]
 
@@ -474,7 +463,7 @@
         first_adjoint,
         [(RB, F32), (slots, BF16, RB), (CB, BF16, slots), (HALF, F32), message],
         [quarter, *over_places(quarter, FAR), rows, cols, first, second],
-        [counts, place],
+        [counts],
         slots,
     )
     (part,) = call(chip_sum, [message], [keep, send, over_core(send)])
@@ -497,7 +486,7 @@
         second_adjoint,
         [(RB, F32), scalar, (HALF, F32), message],
         [*forward_whole(own), data0, beta0, pick_rows, add_cols, first, second],
-        [counts],
+        (),
         slots,
     )
     (part,) = call(chip_sum, [message], [keep, send, over_core(send)])
@@ -508,7 +497,6 @@
         finish,
         [(CHUNK, F32)],
         [total, *over_chips(total), beta0, alpha0, beta1, alpha1, model0, model1],
-        [chip],
     )
     return out
 

time: 97.1 us -> 97 us (level)
  no operation moved by 1% of the time
where the time goes in v5:
time: 97 us; the launch traced here: 96.9 us
  starting transfers between devices  44.2 us (46%)
  waiting for transfers between devices  32.5 us (34%)
  Pallas kernels  19.4 us (20%)
    ppermute x12, waiting for transfers between devices, over_square(): lax.ppermute(x, ('dp', 'mp'), [(i * 16 + j, i * 16 + (j ^ step[i & 1])) f...  16.8 us
    ppermute x12, starting transfers between devices, over_square(): lax.ppermute(x, ('dp', 'mp'), [(i * 16 + j, i * 16 + (j ^ step[i & 1])) f...  15.9 us
    ppermute x9, starting transfers between devices, over_chips(): lax.ppermute(x, 'dp', [(i, (i >> 1 ^ step[i & 1]) * 2 + (i & 1)) for i in...  11 us
    ppermute x9, waiting for transfers between devices, over_chips(): lax.ppermute(x, 'dp', [(i, (i >> 1 ^ step[i & 1]) * 2 + (i & 1)) for i in...  10.5 us
    pallas_call x14, Pallas kernels, call(): pl.pallas_call(kernel, out_shape=[jax.ShapeDtypeStruct((rows, *(width or...  10.2 us
    ppermute x6, starting transfers between devices, over_places(): lax.ppermute(x, 'mp', [(j, j ^ step) for j in range(16)])  8.72 us
    ppermute x5, starting transfers between devices, over_core(): return lax.ppermute(x, 'dp', [(i, i ^ 1) for i in range(8)])  8.62 us
    ppermute x5, waiting for transfers between devices, over_core(): return lax.ppermute(x, 'dp', [(i, i ^ 1) for i in range(8)])  4.62 us
  transfers between devices with their start and end apart: 32, of which 24 were waited for; matrix products, arithmetic and copies ran while one was open for 0% of the time, Pallas kernels for 9%

profile of v5, /device:TPU:1, one launch (start us, length us, event | category | flops | bytes accessed | tf_op | source)
XLA Modules:
  0.0 96.9 jit_solution(7805830237492262929)
XLA Ops:
  0.0 3.6 %collective-permute-start = (f32[32,128]{1,0:T(8,128)}, f32[32,128]{1,0:T(8,128)S(1)}, u32[]{:S(2)}, u32[]{:S(2)}) collective-permute-start(f32[32,128]{1,0:T(8,128)} %data_ref.1), channel_id=1, source_target_pairs={{0,3},{1,2},{2,1},{3,0},{4,7},{5,6},{6,5},{7,4},{8,11},{9,10},{10,... | collective-permute-start | bytes 49160 | tf_op jit(solution)/shard_map/ppermute | solution.py:406
  5.4 2.4 %load_first.1 = (f32[32,128]{1,0:T(8,128)S(1)}, s32[1,384]{1,0:T(1,128)S(1)}, s32[1,384]{1,0:T(1,128)S(1)}, bf16[144,128,128]{2,1,0:T(8,128)(2,1)S(1)}) custom-call(s32[1,1]{1,0:T(1,128)S(6)} %copy.6.live_ref, f32[32,128]{1,0:T(8,128)} %data_ref.1, s32[1,384]{1,0:T(1,128)} %bitcast.5, s32[1,384]{1,0:T(1,128)} %bitcast.6, bf16[384,128,128]{2,1,0:T(8,128)(2,1)} %bitcast.3), custom_call_target="tpu_custom_call" | custom-call | bytes 12582912 | tf_op jit(solution)/shard_map/load_first/pallas_call | solution.py:421
  12.4 3.3 %load_second.1.second_ref = bf16[240,128,128]{2,1,0:T(8,128)(2,1)S(1)} custom-call(f32[128,128]{1,0:T(8,128)S(1)} %collect.1.after_ref.own_ref, bf16[384,128,128]{2,1,0:T(8,128)(2,1)} %bitcast.4), custom_call_target="tpu_custom_call" | custom-call | bytes 12582912 | tf_op jit(solution)/shard_map/load_second/pallas_call | solution.py:442
  15.8 2.2 %first_adjoint.1 = (f32[512,128]{1,0:T(8,128)S(1)}, bf16[384,512]{1,0:T(8,128)(2,1)S(1)}, bf16[768,384]{1,0:T(8,128)(2,1)S(1)}, f32[384,128]{1,0:T(8,128)S(1)}, bf16[400,128]{1,0:T(8,128)(2,1)S(1)}) custom-call(s32[1,1]{1,0:T(1,128)S(6)} %copy.6.live_ref, f32[128,128]{1,0:T(8,128)S(1)} %collect.1.after_ref.own_ref, ...), custom_call_target="tpu_custom_call" | custom-call | tf_op jit(solution)/shard_map/first_adjoint/pallas_call | solution.py:373
  18.0 3.0 %collective-permute-start.6 = (bf16[400,128]{1,0:T(8,128)(2,1)S(1)}, bf16[400,128]{1,0:T(8,128)(2,1)S(1)}, u32[]{:S(2)}, u32[]{:S(2)}) collective-permute-start(bf16[400,128]{1,0:T(8,128)(2,1)S(1)} %get-tuple-element.34.send_ref), channel_id=1, source_target_pairs={{0,16},{16,0},{32,48},{48,32},{64,80},{80,64},{96,112},{112,96},{1... | collective-permute-start | bytes 307208 | tf_op jit(solution)/shard_map/ppermute | solution.py:388
  22.0 3.7 %collective-permute-start.9 = (bf16[400,128]{1,0:T(8,128)(2,1)S(1)}, bf16[400,128]{1,0:T(8,128)(2,1)S(1)}, u32[]{:S(2)}, u32[]{:S(2)}) collective-permute-start(bf16[400,128]{1,0:T(8,128)(2,1)S(1)} %chip_sum.2.after_ref.own_ref), channel_id=1, source_target_pairs={{0,64},{16,80},{32,96},{48,112},{64,0},{80,16},{96,32},{112,48},{1... | collective-permute-start | bytes 307208 | tf_op jit(solution)/shard_map/ppermute | solution.py:393
  26.4 3.4 %transpose.1 = (bf16[384,128,128]{2,1,0:T(8,128)(2,1)S(1)}, bf16[384,768]{1,0:T(8,128)(2,1)S(1)}, bf16[512,384]{1,0:T(8,128)(2,1)S(1)}) custom-call(s32[1,1]{1,0:T(1,128)S(6)} %copy.6.live_ref, bf16[400,128]{1,0:T(8,128)(2,1)S(1)} %chip_sum.2.after_ref.own_ref, s32[1,384]{1,0:T(1,128)S(1)} %get-tuple-element.31.rows_ref, ...), custom_call_target="tpu_custom_call" | custom-call | bytes 12582912 | tf_op jit(solution)/shard_map/transpose/pallas_call | solution.py:470
  34.1 2.1 %forward.2.own_ref = bf16[528,128]{1,0:T(8,128)(2,1)S(1)} custom-call(bf16[400,128]{1,0:T(8,128)(2,1)S(1)} %get-tuple-element.36.own_ref, bf16[400,128]{1,0:T(8,128)(2,1)S(1)} %collective-permute-done.10.got_ref, bf16[384,768]{1,0:T(8,128)(2,1)S(1)} %get-tuple-element.37.pick_ref, bf16[512,384]{1,0:T(8,128)(2,1)S(1)} %get-tuple-element.38.hot_ref, ...), custom_call_target="tpu_custom_call" | custom-call | tf_op jit(solution)/shard_map/forward/pallas_call | solution.py:373
  36.2 2.9 %collective-permute-start.13 = (bf16[528,128]{1,0:T(8,128)(2,1)S(1)}, bf16[528,128]{1,0:T(8,128)(2,1)S(1)}, u32[]{:S(2)}, u32[]{:S(2)}) collective-permute-start(bf16[528,128]{1,0:T(8,128)(2,1)S(1)} %forward.2.own_ref), channel_id=1, source_target_pairs={{0,7},{1,6},{2,5},{3,4},{4,3},{5,2},{6,1},{7,0},{8,15},{9,14},{10,... | collective-permute-start | bytes 405512 | tf_op jit(solution)/shard_map/ppermute | solution.py:399
  40.1 2.4 %collective-permute-done.13.three_ref = bf16[528,128]{1,0:T(8,128)(2,1)S(1)} collective-permute-done((bf16[528,128]{1,0:T(8,128)(2,1)S(1)}, bf16[528,128]{1,0:T(8,128)(2,1)S(1)}, u32[]{:S(2)}, u32[]{:S(2)}) %collective-permute-start.13) | collective-permute-done | bytes 135200 | tf_op jit(solution)/shard_map/ppermute | solution.py:399
  42.5 1.9 %collective-permute-done.12.two_ref = bf16[528,128]{1,0:T(8,128)(2,1)S(1)} collective-permute-done((bf16[528,128]{1,0:T(8,128)(2,1)S(1)}, bf16[528,128]{1,0:T(8,128)(2,1)S(1)}, u32[]{:S(2)}, u32[]{:S(2)}) %collective-permute-start.12) | collective-permute-done | bytes 135200 | tf_op jit(solution)/shard_map/ppermute | solution.py:399
  44.8 2.7 %collective-permute-start.15 = (bf16[528,128]{1,0:T(8,128)(2,1)S(1)}, bf16[528,128]{1,0:T(8,128)(2,1)S(1)}, u32[]{:S(2)}, u32[]{:S(2)}) collective-permute-start(bf16[528,128]{1,0:T(8,128)(2,1)S(1)} %row_sum.2.own_ref), channel_id=1, source_target_pairs={{0,12},{1,13},{2,14},{3,15},{4,8},{5,9},{6,10},{7,11},{8,4},{9,5},... | collective-permute-start | bytes 405512 | tf_op jit(solution)/shard_map/ppermute | solution.py:399
  48.6 2.1 %collective-permute-done.16.three_ref = bf16[528,128]{1,0:T(8,128)(2,1)S(1)} collective-permute-done((bf16[528,128]{1,0:T(8,128)(2,1)S(1)}, bf16[528,128]{1,0:T(8,128)(2,1)S(1)}, u32[]{:S(2)}, u32[]{:S(2)}) %collective-permute-start.16) | collective-permute-done | bytes 135200 | tf_op jit(solution)/shard_map/ppermute | solution.py:399
  52.8 2.2 %second_adjoint.1 = (f32[512,128]{1,0:T(8,128)S(1)}, f32[8,128]{1,0:T(8,128)S(1)}, f32[384,128]{1,0:T(8,128)S(1)}, bf16[400,128]{1,0:T(8,128)(2,1)S(1)}) custom-call(bf16[528,128]{1,0:T(8,128)(2,1)S(1)} %row_sum.2.own_ref, bf16[528,128]{1,0:T(8,128)(2,1)S(1)} %collective-permute-done.14.one_ref, bf16[528,128]{1,0:T(8,128)(2,1)S(1)} %collective-permute-done.15.two_ref, ...), custom_call_target="tpu_custom_call" | custom-call | tf_op jit(solution)/shard_map/second_adjoint/pallas_call | solution.py:373
  55.0 2.4 %collective-permute-start.17 = (bf16[400,128]{1,0:T(8,128)(2,1)S(1)}, bf16[400,128]{1,0:T(8,128)(2,1)S(1)}, u32[]{:S(2)}, u32[]{:S(2)}) collective-permute-start(bf16[400,128]{1,0:T(8,128)(2,1)S(1)} %get-tuple-element.44.send_ref), channel_id=1, source_target_pairs={{0,16},{16,0},{32,48},{48,32},{64,80},{80,64},{96,112},{112,96},{1... | collective-permute-start | bytes 307208 | tf_op jit(solution)/shard_map/ppermute | solution.py:388
  58.4 1.8 %collective-permute-start.20 = (bf16[400,128]{1,0:T(8,128)(2,1)S(1)}, bf16[400,128]{1,0:T(8,128)(2,1)S(1)}, u32[]{:S(2)}, u32[]{:S(2)}) collective-permute-start(bf16[400,128]{1,0:T(8,128)(2,1)S(1)} %chip_sum.3.own_ref), channel_id=1, source_target_pairs={{0,64},{16,80},{32,96},{48,112},{64,0},{80,16},{96,32},{112,48},{1... | collective-permute-start | bytes 307208 | tf_op jit(solution)/shard_map/ppermute | solution.py:393
  61.8 2.4 %collective-permute-done.20.three_ref = bf16[400,128]{1,0:T(8,128)(2,1)S(1)} collective-permute-done((bf16[400,128]{1,0:T(8,128)(2,1)S(1)}, bf16[400,128]{1,0:T(8,128)(2,1)S(1)}, u32[]{:S(2)}, u32[]{:S(2)}) %collective-permute-start.20) | collective-permute-done | bytes 102432 | tf_op jit(solution)/shard_map/ppermute | solution.py:393
  69.1 2.1 %forward.3.own_ref = bf16[528,128]{1,0:T(8,128)(2,1)S(1)} custom-call(bf16[400,128]{1,0:T(8,128)(2,1)S(1)} %get-tuple-element.47.own_ref, bf16[400,128]{1,0:T(8,128)(2,1)S(1)} %collective-permute-done.21.got_ref, bf16[384,768]{1,0:T(8,128)(2,1)S(1)} %get-tuple-element.37.pick_ref, bf16[512,384]{1,0:T(8,128)(2,1)S(1)} %get-tuple-element.38.hot_ref, ...), custom_call_target="tpu_custom_call" | custom-call | tf_op jit(solution)/shard_map/forward/pallas_call | solution.py:373
  71.2 2.9 %collective-permute-start.24 = (bf16[528,128]{1,0:T(8,128)(2,1)S(1)}, bf16[528,128]{1,0:T(8,128)(2,1)S(1)}, u32[]{:S(2)}, u32[]{:S(2)}) collective-permute-start(bf16[528,128]{1,0:T(8,128)(2,1)S(1)} %forward.3.own_ref), channel_id=1, source_target_pairs={{0,7},{1,6},{2,5},{3,4},{4,3},{5,2},{6,1},{7,0},{8,15},{9,14},{10,... | collective-permute-start | bytes 405512 | tf_op jit(solution)/shard_map/ppermute | solution.py:399
  75.1 2.4 %collective-permute-done.24.three_ref = bf16[528,128]{1,0:T(8,128)(2,1)S(1)} collective-permute-done((bf16[528,128]{1,0:T(8,128)(2,1)S(1)}, bf16[528,128]{1,0:T(8,128)(2,1)S(1)}, u32[]{:S(2)}, u32[]{:S(2)}) %collective-permute-start.24) | collective-permute-done | bytes 135200 | tf_op jit(solution)/shard_map/ppermute | solution.py:399
  77.5 2.0 %collective-permute-done.23.two_ref = bf16[528,128]{1,0:T(8,128)(2,1)S(1)} collective-permute-done((bf16[528,128]{1,0:T(8,128)(2,1)S(1)}, bf16[528,128]{1,0:T(8,128)(2,1)S(1)}, u32[]{:S(2)}, u32[]{:S(2)}) %collective-permute-start.23) | collective-permute-done | bytes 135200 | tf_op jit(solution)/shard_map/ppermute | solution.py:399
  79.7 2.3 %collective-permute-start.26 = (bf16[528,128]{1,0:T(8,128)(2,1)S(1)}, bf16[528,128]{1,0:T(8,128)(2,1)S(1)}, u32[]{:S(2)}, u32[]{:S(2)}) collective-permute-start(bf16[528,128]{1,0:T(8,128)(2,1)S(1)} %row_sum.3.own_ref), channel_id=1, source_target_pairs={{0,12},{1,13},{2,14},{3,15},{4,8},{5,9},{6,10},{7,11},{8,4},{9,5},... | collective-permute-start | bytes 405512 | tf_op jit(solution)/shard_map/ppermute | solution.py:399
  83.5 2.1 %collective-permute-done.27.three_ref = bf16[528,128]{1,0:T(8,128)(2,1)S(1)} collective-permute-done((bf16[528,128]{1,0:T(8,128)(2,1)S(1)}, bf16[528,128]{1,0:T(8,128)(2,1)S(1)}, u32[]{:S(2)}, u32[]{:S(2)}) %collective-permute-start.27) | collective-permute-done | bytes 135200 | tf_op jit(solution)/shard_map/ppermute | solution.py:399
  87.7 1.9 %collective-permute-start.28 = (f32[8,128]{1,0:T(8,128)S(1)}, f32[8,128]{1,0:T(8,128)S(1)}, u32[]{:S(2)}, u32[]{:S(2)}) collective-permute-start(f32[8,128]{1,0:T(8,128)S(1)} %get-tuple-element.50.own_ref), channel_id=1, source_target_pairs={{0,16},{16,0},{32,48},{48,32},{64,80},{80,64},{96,112},{112,96},{1... | collective-permute-start | bytes 12296 | tf_op jit(solution)/shard_map/ppermute | solution.py:388
  (57 shorter events, 35.9 us)
Async XLA Ops:
  0.0 7.9 %collective-permute-start = (f32[32,128]{1,0:T(8,128)}, f32[32,128]{1,0:T(8,128)S(1)}, u32[]{:S(2)}, u32[]{:S(2)}) collective-permute-start(f32[32,128]{1,0:T(8,128)} %data_ref.1), channel_id=1, source_target_pairs={{0,3},{1,2},{2,1},{3,0},{4,7},{5,6},{6,5},{7,4},{8,11},{9,10},{10,... | collective-permute-start | bytes 49160 | tf_op jit(solution)/shard_map/ppermute | solution.py:406
  3.6 4.9 %collective-permute-start.2 = (f32[32,128]{1,0:T(8,128)}, f32[32,128]{1,0:T(8,128)S(1)}, u32[]{:S(2)}, u32[]{:S(2)}) collective-permute-start(f32[32,128]{1,0:T(8,128)} %data_ref.1), channel_id=1, source_target_pairs={{0,7},{1,6},{2,5},{3,4},{4,3},{5,2},{6,1},{7,0},{8,15},{9,14},{10,... | collective-permute-start | bytes 49160 | tf_op jit(solution)/shard_map/ppermute | solution.py:406
  4.5 4.0 %collective-permute-start.1 = (f32[32,128]{1,0:T(8,128)}, f32[32,128]{1,0:T(8,128)S(1)}, u32[]{:S(2)}, u32[]{:S(2)}) collective-permute-start(f32[32,128]{1,0:T(8,128)} %data_ref.1), channel_id=1, source_target_pairs={{0,4},{1,5},{2,6},{3,7},{4,0},{5,1},{6,2},{7,3},{8,12},{9,13},{10,... | collective-permute-start | bytes 49160 | tf_op jit(solution)/shard_map/ppermute | solution.py:406
  8.5 7.3 %collective-permute-start.5 = (f32[128,128]{1,0:T(8,128)S(1)}, f32[128,128]{1,0:T(8,128)S(1)}, u32[]{:S(2)}, u32[]{:S(2)}) collective-permute-start(f32[128,128]{1,0:T(8,128)S(1)} %collect.1.after_ref.own_ref), channel_id=1, source_target_pairs={{0,13},{1,12},{2,15},{3,14},{4,9},{5,8},{6,11},{7,10},{8,5},{9,4},... | collective-permute-start | bytes 196616 | tf_op jit(solution)/shard_map/ppermute | solution.py:406
  10.2 5.6 %collective-permute-start.4 = (f32[128,128]{1,0:T(8,128)S(1)}, f32[128,128]{1,0:T(8,128)S(1)}, u32[]{:S(2)}, u32[]{:S(2)}) collective-permute-start(f32[128,128]{1,0:T(8,128)S(1)} %collect.1.after_ref.own_ref), channel_id=1, source_target_pairs={{0,12},{1,13},{2,14},{3,15},{4,8},{5,9},{6,10},{7,11},{8,4},{9,5},... | collective-permute-start | bytes 196616 | tf_op jit(solution)/shard_map/ppermute | solution.py:406
  11.1 4.6 %collective-permute-start.3 = (f32[128,128]{1,0:T(8,128)S(1)}, f32[128,128]{1,0:T(8,128)S(1)}, u32[]{:S(2)}, u32[]{:S(2)}) collective-permute-start(f32[128,128]{1,0:T(8,128)S(1)} %collect.1.after_ref.own_ref), channel_id=1, source_target_pairs={{0,1},{1,0},{2,3},{3,2},{4,5},{5,4},{6,7},{7,6},{8,9},{9,8},{10,11... | collective-permute-start | bytes 196616 | tf_op jit(solution)/shard_map/ppermute | solution.py:406
  22.0 7.8 %collective-permute-start.9 = (bf16[400,128]{1,0:T(8,128)(2,1)S(1)}, bf16[400,128]{1,0:T(8,128)(2,1)S(1)}, u32[]{:S(2)}, u32[]{:S(2)}) collective-permute-start(bf16[400,128]{1,0:T(8,128)(2,1)S(1)} %chip_sum.2.after_ref.own_ref), channel_id=1, source_target_pairs={{0,64},{16,80},{32,96},{48,112},{64,0},{80,16},{96,32},{112,48},{1... | collective-permute-start | bytes 307208 | tf_op jit(solution)/shard_map/ppermute | solution.py:393
  25.7 5.6 %collective-permute-start.8 = (bf16[400,128]{1,0:T(8,128)(2,1)S(1)}, bf16[400,128]{1,0:T(8,128)(2,1)S(1)}, u32[]{:S(2)}, u32[]{:S(2)}) collective-permute-start(bf16[400,128]{1,0:T(8,128)(2,1)S(1)} %chip_sum.2.after_ref.own_ref), channel_id=1, source_target_pairs={{0,96},{16,48},{32,64},{48,16},{64,32},{80,112},{96,0},{112,80},{1... | collective-permute-start | bytes 307208 | tf_op jit(solution)/shard_map/ppermute | solution.py:393
  26.4 5.8 %collective-permute-start.7 = (bf16[400,128]{1,0:T(8,128)(2,1)S(1)}, bf16[400,128]{1,0:T(8,128)(2,1)S(1)}, u32[]{:S(2)}, u32[]{:S(2)}) collective-permute-start(bf16[400,128]{1,0:T(8,128)(2,1)S(1)} %chip_sum.2.after_ref.own_ref), channel_id=1, source_target_pairs={{0,32},{16,112},{32,0},{48,80},{64,96},{80,48},{96,64},{112,16},{1... | collective-permute-start | bytes 307208 | tf_op jit(solution)/shard_map/ppermute | solution.py:393
  36.2 6.3 %collective-permute-start.13 = (bf16[528,128]{1,0:T(8,128)(2,1)S(1)}, bf16[528,128]{1,0:T(8,128)(2,1)S(1)}, u32[]{:S(2)}, u32[]{:S(2)}) collective-permute-start(bf16[528,128]{1,0:T(8,128)(2,1)S(1)} %forward.2.own_ref), channel_id=1, source_target_pairs={{0,7},{1,6},{2,5},{3,4},{4,3},{5,2},{6,1},{7,0},{8,15},{9,14},{10,... | collective-permute-start | bytes 405512 | tf_op jit(solution)/shard_map/ppermute | solution.py:399
  39.1 5.4 %collective-permute-start.12 = (bf16[528,128]{1,0:T(8,128)(2,1)S(1)}, bf16[528,128]{1,0:T(8,128)(2,1)S(1)}, u32[]{:S(2)}, u32[]{:S(2)}) collective-permute-start(bf16[528,128]{1,0:T(8,128)(2,1)S(1)} %forward.2.own_ref), channel_id=1, source_target_pairs={{0,4},{1,5},{2,6},{3,7},{4,0},{5,1},{6,2},{7,3},{8,12},{9,13},{10,... | collective-permute-start | bytes 405512 | tf_op jit(solution)/shard_map/ppermute | solution.py:399
  40.0 4.4 %collective-permute-start.11 = (bf16[528,128]{1,0:T(8,128)(2,1)S(1)}, bf16[528,128]{1,0:T(8,128)(2,1)S(1)}, u32[]{:S(2)}, u32[]{:S(2)}) collective-permute-start(bf16[528,128]{1,0:T(8,128)(2,1)S(1)} %forward.2.own_ref), channel_id=1, source_target_pairs={{0,3},{1,2},{2,1},{3,0},{4,7},{5,6},{6,5},{7,4},{8,11},{9,10},{10,... | collective-permute-start | bytes 405512 | tf_op jit(solution)/shard_map/ppermute | solution.py:399
  44.5 6.2 %collective-permute-start.16 = (bf16[528,128]{1,0:T(8,128)(2,1)S(1)}, bf16[528,128]{1,0:T(8,128)(2,1)S(1)}, u32[]{:S(2)}, u32[]{:S(2)}) collective-permute-start(bf16[528,128]{1,0:T(8,128)(2,1)S(1)} %row_sum.2.own_ref), channel_id=1, source_target_pairs={{0,13},{1,12},{2,15},{3,14},{4,9},{5,8},{6,11},{7,10},{8,5},{9,4},... | collective-permute-start | bytes 405512 | tf_op jit(solution)/shard_map/ppermute | solution.py:399
  44.8 6.5 %collective-permute-start.15 = (bf16[528,128]{1,0:T(8,128)(2,1)S(1)}, bf16[528,128]{1,0:T(8,128)(2,1)S(1)}, u32[]{:S(2)}, u32[]{:S(2)}) collective-permute-start(bf16[528,128]{1,0:T(8,128)(2,1)S(1)} %row_sum.2.own_ref), channel_id=1, source_target_pairs={{0,12},{1,13},{2,14},{3,15},{4,8},{5,9},{6,10},{7,11},{8,4},{9,5},... | collective-permute-start | bytes 405512 | tf_op jit(solution)/shard_map/ppermute | solution.py:399
  47.5 5.4 %collective-permute-start.14 = (bf16[528,128]{1,0:T(8,128)(2,1)S(1)}, bf16[528,128]{1,0:T(8,128)(2,1)S(1)}, u32[]{:S(2)}, u32[]{:S(2)}) collective-permute-start(bf16[528,128]{1,0:T(8,128)(2,1)S(1)} %row_sum.2.own_ref), channel_id=1, source_target_pairs={{0,1},{1,0},{2,3},{3,2},{4,5},{5,4},{6,7},{7,6},{8,9},{9,8},{10,11... | collective-permute-start | bytes 405512 | tf_op jit(solution)/shard_map/ppermute | solution.py:399
  58.4 5.7 %collective-permute-start.20 = (bf16[400,128]{1,0:T(8,128)(2,1)S(1)}, bf16[400,128]{1,0:T(8,128)(2,1)S(1)}, u32[]{:S(2)}, u32[]{:S(2)}) collective-permute-start(bf16[400,128]{1,0:T(8,128)(2,1)S(1)} %chip_sum.3.own_ref), channel_id=1, source_target_pairs={{0,64},{16,80},{32,96},{48,112},{64,0},{80,16},{96,32},{112,48},{1... | collective-permute-start | bytes 307208 | tf_op jit(solution)/shard_map/ppermute | solution.py:393
  60.3 5.5 %collective-permute-start.19 = (bf16[400,128]{1,0:T(8,128)(2,1)S(1)}, bf16[400,128]{1,0:T(8,128)(2,1)S(1)}, u32[]{:S(2)}, u32[]{:S(2)}) collective-permute-start(bf16[400,128]{1,0:T(8,128)(2,1)S(1)} %chip_sum.3.own_ref), channel_id=1, source_target_pairs={{0,96},{16,48},{32,64},{48,16},{64,32},{80,112},{96,0},{112,80},{1... | collective-permute-start | bytes 307208 | tf_op jit(solution)/shard_map/ppermute | solution.py:393
  61.0 6.3 %collective-permute-start.18 = (bf16[400,128]{1,0:T(8,128)(2,1)S(1)}, bf16[400,128]{1,0:T(8,128)(2,1)S(1)}, u32[]{:S(2)}, u32[]{:S(2)}) collective-permute-start(bf16[400,128]{1,0:T(8,128)(2,1)S(1)} %chip_sum.3.own_ref), channel_id=1, source_target_pairs={{0,32},{16,112},{32,0},{48,80},{64,96},{80,48},{96,64},{112,16},{1... | collective-permute-start | bytes 307208 | tf_op jit(solution)/shard_map/ppermute | solution.py:393
  71.2 6.3 %collective-permute-start.24 = (bf16[528,128]{1,0:T(8,128)(2,1)S(1)}, bf16[528,128]{1,0:T(8,128)(2,1)S(1)}, u32[]{:S(2)}, u32[]{:S(2)}) collective-permute-start(bf16[528,128]{1,0:T(8,128)(2,1)S(1)} %forward.3.own_ref), channel_id=1, source_target_pairs={{0,7},{1,6},{2,5},{3,4},{4,3},{5,2},{6,1},{7,0},{8,15},{9,14},{10,... | collective-permute-start | bytes 405512 | tf_op jit(solution)/shard_map/ppermute | solution.py:399
  74.1 5.4 %collective-permute-start.23 = (bf16[528,128]{1,0:T(8,128)(2,1)S(1)}, bf16[528,128]{1,0:T(8,128)(2,1)S(1)}, u32[]{:S(2)}, u32[]{:S(2)}) collective-permute-start(bf16[528,128]{1,0:T(8,128)(2,1)S(1)} %forward.3.own_ref), channel_id=1, source_target_pairs={{0,4},{1,5},{2,6},{3,7},{4,0},{5,1},{6,2},{7,3},{8,12},{9,13},{10,... | collective-permute-start | bytes 405512 | tf_op jit(solution)/shard_map/ppermute | solution.py:399
  75.1 4.4 %collective-permute-start.22 = (bf16[528,128]{1,0:T(8,128)(2,1)S(1)}, bf16[528,128]{1,0:T(8,128)(2,1)S(1)}, u32[]{:S(2)}, u32[]{:S(2)}) collective-permute-start(bf16[528,128]{1,0:T(8,128)(2,1)S(1)} %forward.3.own_ref), channel_id=1, source_target_pairs={{0,3},{1,2},{2,1},{3,0},{4,7},{5,6},{6,5},{7,4},{8,11},{9,10},{10,... | collective-permute-start | bytes 405512 | tf_op jit(solution)/shard_map/ppermute | solution.py:399
  79.6 6.0 %collective-permute-start.27 = (bf16[528,128]{1,0:T(8,128)(2,1)S(1)}, bf16[528,128]{1,0:T(8,128)(2,1)S(1)}, u32[]{:S(2)}, u32[]{:S(2)}) collective-permute-start(bf16[528,128]{1,0:T(8,128)(2,1)S(1)} %row_sum.3.own_ref), channel_id=1, source_target_pairs={{0,13},{1,12},{2,15},{3,14},{4,9},{5,8},{6,11},{7,10},{8,5},{9,4},... | collective-permute-start | bytes 405512 | tf_op jit(solution)/shard_map/ppermute | solution.py:399
  79.7 6.5 %collective-permute-start.26 = (bf16[528,128]{1,0:T(8,128)(2,1)S(1)}, bf16[528,128]{1,0:T(8,128)(2,1)S(1)}, u32[]{:S(2)}, u32[]{:S(2)}) collective-permute-start(bf16[528,128]{1,0:T(8,128)(2,1)S(1)} %row_sum.3.own_ref), channel_id=1, source_target_pairs={{0,12},{1,13},{2,14},{3,15},{4,8},{5,9},{6,10},{7,11},{8,4},{9,5},... | collective-permute-start | bytes 405512 | tf_op jit(solution)/shard_map/ppermute | solution.py:399
  82.0 5.4 %collective-permute-start.25 = (bf16[528,128]{1,0:T(8,128)(2,1)S(1)}, bf16[528,128]{1,0:T(8,128)(2,1)S(1)}, u32[]{:S(2)}, u32[]{:S(2)}) collective-permute-start(bf16[528,128]{1,0:T(8,128)(2,1)S(1)} %row_sum.3.own_ref), channel_id=1, source_target_pairs={{0,1},{1,0},{2,3},{3,2},{4,5},{5,4},{6,7},{7,6},{8,9},{9,8},{10,11... | collective-permute-start | bytes 405512 | tf_op jit(solution)/shard_map/ppermute | solution.py:399
  (8 other events, 23.6 us)

commit v6 on v5

--- a/solution.py
+++ b/solution.py
@@ -125,12 +125,10 @@
         )
 
 
-def adjoint_tail(data, pick_ref, hot_ref, blocks_refs, keep_ref, send_ref, picked_ref, products_ref):
+def adjoint_tail(data, pick_ref, hot_ref, blocks_refs, products_ref, send_ref, picked_ref):
     gather(pick_ref, data.astype(BF16), picked_ref)
     multiply(blocks_refs, picked_ref, products_ref)
-    partial = scatter(products_ref, hot_ref)
-    keep_ref[...] = partial[:HALF]
-    send_ref[:HALF, :] = partial[HALF:].astype(BF16)
+    send_ref[:HALF, :] = scatter(products_ref, hot_ref.at[HALF:, :]).astype(BF16)
     send_ref[HALF:, :] = split_rows(square_sum(data))
 
 
@@ -147,10 +145,9 @@
     data_ref,
     pick_ref,
     hot_ref,
-    keep_ref,
+    products_ref,
     send_ref,
     picked_ref,
-    products_ref,
 ):
     near, far = square(*NEAR), square(*FAR)
     place = lax.axis_index("mp")
@@ -162,7 +159,7 @@
     pick_ref[...] = picker(rows_ref[...], RB, live)
     hot_ref[...] = adder(cols_ref[...], CB, live)
     blocks_refs = (first_ref, second_ref)
-    adjoint_tail(data_ref[...], pick_ref, hot_ref, blocks_refs, keep_ref, send_ref, picked_ref, products_ref)
+    adjoint_tail(data_ref[...], pick_ref, hot_ref, blocks_refs, products_ref, send_ref, picked_ref)
 
 
 def forward_sum(own_ref, one_ref, two_ref, three_ref):
@@ -191,18 +188,21 @@
     second_ref,
     next_ref,
     alpha2_ref,
-    keep_ref,
+    products_ref,
     send_ref,
     picked_ref,
-    products_ref,
 ):
     data, alpha2 = next_data(own_ref, one_ref, two_ref, three_ref, data_ref, beta2_ref)
     next_ref[...] = data
     alpha2_ref[...] = jnp.broadcast_to(alpha2, alpha2_ref.shape)
     blocks_refs = (first_ref, second_ref)
     adjoint_tail(
-        data, pick_ref, hot_ref, blocks_refs, keep_ref, send_ref, picked_ref, products_ref
-    )
+        data, pick_ref, hot_ref, blocks_refs, products_ref, send_ref, picked_ref
+    )
+
+
+def add_own(products_ref, hot_ref, keep_ref):
+    keep_ref[...] = scatter(products_ref, hot_ref.at[:HALF, :])
 
 
 def chip_sum(keep_ref, send_ref, got_ref, out_ref):
@@ -368,8 +368,8 @@
 VECTOR = pl.BlockSpec(memory_space=pltpu.VMEM)
 
 
-def call(kernel, outs, vectors, scalars=(), slots=0):
-    scratch = [pltpu.VMEM((slots, BS), BF16), pltpu.VMEM((slots, BS), F32)] if slots else []
+def call(kernel, outs, vectors, scalars=(), slots=0, held=(), work=0):
+    scratch = [pltpu.VMEM((slots, BS), dtype) for dtype in held]
     return pl.pallas_call(
         kernel,
         out_shape=[jax.ShapeDtypeStruct((rows, *(width or (BS,))), dtype) for rows, dtype, *width in outs],
@@ -377,6 +377,7 @@
         out_specs=[VECTOR] * len(outs),
         scratch_shapes=scratch,
         compiler_params=pltpu.CompilerParams(vmem_limit_bytes=16 * 2**20),
+        cost_estimate=pl.CostEstimate(flops=0, bytes_accessed=work, transcendentals=0) if work else None,
         name=kernel.__name__,
     )(*scalars, *vectors)
 
@@ -452,21 +453,24 @@
     second = pltpu.with_memory_space_constraint(second, pltpu.VMEM)
 
     def forward_whole(own):
-        (part,) = call(forward, [(RB + EXTRA, BF16)], [own, over_core(own), pick_cols, add_rows, turned], (), slots)
+        (part,) = call(forward, [(RB + EXTRA, BF16)], [own, over_core(own), pick_cols, add_rows, turned], (), slots, (BF16, F32))
         (part,) = call(row_sum, [(RB + EXTRA, BF16)], [part, *over_square(part, NEAR)])
         return [part, *over_square(part, FAR)]
 
     def chips_whole(part):
         return [part, *over_chips(part)]
 
-    data0, pick_rows, add_cols, keep, send = call(
+    data0, pick_rows, add_cols, products, send = call(
         first_adjoint,
-        [(RB, F32), (slots, BF16, RB), (CB, BF16, slots), (HALF, F32), message],
+        [(RB, F32), (slots, BF16, RB), (CB, BF16, slots), (slots, F32), message],
         [quarter, *over_places(quarter, FAR), rows, cols, first, second],
         [counts],
         slots,
-    )
-    (part,) = call(chip_sum, [message], [keep, send, over_core(send)])
+        (BF16,),
+    )
+    got = over_core(send)
+    (keep,) = call(add_own, [(HALF, F32)], [products, add_cols], work=CB * slots * 2)
+    (part,) = call(chip_sum, [message], [keep, send, got])
     turned, pick_cols, add_rows = pl.pallas_call(
         transpose,
         out_shape=[
@@ -482,14 +486,17 @@
     )(counts, part, rows, cols, first, second)
     turned = pltpu.with_memory_space_constraint(turned, pltpu.VMEM)
     model0, own, beta0 = call(first_model, model_outs, [*chips_whole(part), turned])
-    data1, alpha0, keep, send = call(
+    data1, alpha0, products, send = call(
         second_adjoint,
-        [(RB, F32), scalar, (HALF, F32), message],
+        [(RB, F32), scalar, (slots, F32), message],
         [*forward_whole(own), data0, beta0, pick_rows, add_cols, first, second],
         (),
         slots,
-    )
-    (part,) = call(chip_sum, [message], [keep, send, over_core(send)])
+        (BF16,),
+    )
+    got = over_core(send)
+    (keep,) = call(add_own, [(HALF, F32)], [products, add_cols], work=CB * slots * 2)
+    (part,) = call(chip_sum, [message], [keep, send, got])
     model1, own, beta1 = call(second_model, model_outs, [*chips_whole(part), model0, alpha0])
     alpha1, total = call(last_data, [scalar, scalar], [*forward_whole(own), data1, beta1])
     (total,) = call(add, [scalar], [total, over_core(total)])

time: 97 us -> 96.8 us (level)
    pallas_call x14 -> x16, Pallas kernels: 10.2 us -> 10.5 us  [call(): pl.pallas_call(kernel, out_shape=[jax.ShapeDtypeStruct((rows, *(width or...]
  transfers between devices with their start and end apart: 32 -> 32, of which waited for: 24 -> 24; matrix products, arithmetic and copies ran while one was open for 0% -> 0% of each run, Pallas kernels for 9% -> 10%
where the time goes in v6:
time: 96.8 us; the launch traced here: 96.7 us
  starting transfers between devices  44.2 us (46%)
  waiting for transfers between devices  32 us (33%)
  Pallas kernels  19.7 us (20%)
    ppermute x12, waiting for transfers between devices, over_square(): lax.ppermute(x, ('dp', 'mp'), [(i * 16 + j, i * 16 + (j ^ step[i & 1])) f...  16.8 us
    ppermute x12, starting transfers between devices, over_square(): lax.ppermute(x, ('dp', 'mp'), [(i * 16 + j, i * 16 + (j ^ step[i & 1])) f...  15.9 us
    ppermute x9, starting transfers between devices, over_chips(): lax.ppermute(x, 'dp', [(i, (i >> 1 ^ step[i & 1]) * 2 + (i & 1)) for i in...  11 us
    ppermute x9, waiting for transfers between devices, over_chips(): lax.ppermute(x, 'dp', [(i, (i >> 1 ^ step[i & 1]) * 2 + (i & 1)) for i in...  10.5 us
    pallas_call x16, Pallas kernels, call(): pl.pallas_call(kernel, out_shape=[jax.ShapeDtypeStruct((rows, *(width or...  10.5 us
    ppermute x6, starting transfers between devices, over_places(): lax.ppermute(x, 'mp', [(j, j ^ step) for j in range(16)])  8.72 us
    ppermute x5, starting transfers between devices, over_core(): return lax.ppermute(x, 'dp', [(i, i ^ 1) for i in range(8)])  8.61 us
    ppermute x5, waiting for transfers between devices, over_core(): return lax.ppermute(x, 'dp', [(i, i ^ 1) for i in range(8)])  4.11 us
  transfers between devices with their start and end apart: 32, of which 24 were waited for; matrix products, arithmetic and copies ran while one was open for 0% of the time, Pallas kernels for 10%

profile of v6, /device:TPU:1, one launch (start us, length us, event | category | flops | bytes accessed | tf_op | source)
XLA Modules:
  0.0 96.7 jit_solution(3739362621941702559)
XLA Ops:
  0.0 3.6 %collective-permute-start = (f32[32,128]{1,0:T(8,128)}, f32[32,128]{1,0:T(8,128)S(1)}, u32[]{:S(2)}, u32[]{:S(2)}) collective-permute-start(f32[32,128]{1,0:T(8,128)} %data_ref.1), channel_id=1, source_target_pairs={{0,3},{1,2},{2,1},{3,0},{4,7},{5,6},{6,5},{7,4},{8,11},{9,10},{10,... | collective-permute-start | bytes 49160 | tf_op jit(solution)/shard_map/ppermute | solution.py:407
  5.4 2.4 %load_first.1 = (f32[32,128]{1,0:T(8,128)S(1)}, s32[1,384]{1,0:T(1,128)S(1)}, s32[1,384]{1,0:T(1,128)S(1)}, bf16[144,128,128]{2,1,0:T(8,128)(2,1)S(1)}) custom-call(s32[1,1]{1,0:T(1,128)S(6)} %copy.6.live_ref, f32[32,128]{1,0:T(8,128)} %data_ref.1, s32[1,384]{1,0:T(1,128)} %bitcast.5, s32[1,384]{1,0:T(1,128)} %bitcast.6, bf16[384,128,128]{2,1,0:T(8,128)(2,1)} %bitcast.3), custom_call_target="tpu_custom_call" | custom-call | bytes 12582912 | tf_op jit(solution)/shard_map/load_first/pallas_call | solution.py:422
  12.4 3.3 %load_second.1.second_ref = bf16[240,128,128]{2,1,0:T(8,128)(2,1)S(1)} custom-call(f32[128,128]{1,0:T(8,128)S(1)} %collect.1.after_ref.own_ref, bf16[384,128,128]{2,1,0:T(8,128)(2,1)} %bitcast.4), custom_call_target="tpu_custom_call" | custom-call | bytes 12582912 | tf_op jit(solution)/shard_map/load_second/pallas_call | solution.py:443
  15.8 2.1 %first_adjoint.1 = (f32[512,128]{1,0:T(8,128)S(1)}, bf16[384,512]{1,0:T(8,128)(2,1)S(1)}, bf16[768,384]{1,0:T(8,128)(2,1)S(1)}, f32[384,128]{1,0:T(8,128)S(1)}, bf16[400,128]{1,0:T(8,128)(2,1)S(1)}) custom-call(s32[1,1]{1,0:T(1,128)S(6)} %copy.6.live_ref, f32[128,128]{1,0:T(8,128)S(1)} %collect.1.after_ref.own_ref, ...), custom_call_target="tpu_custom_call" | custom-call | tf_op jit(solution)/shard_map/first_adjoint/pallas_call | solution.py:373
  17.9 3.0 %collective-permute-start.6 = (bf16[400,128]{1,0:T(8,128)(2,1)S(1)}, bf16[400,128]{1,0:T(8,128)(2,1)S(1)}, u32[]{:S(2)}, u32[]{:S(2)}) collective-permute-start(bf16[400,128]{1,0:T(8,128)(2,1)S(1)} %get-tuple-element.35.send_ref), channel_id=1, source_target_pairs={{0,16},{16,0},{32,48},{48,32},{64,80},{80,64},{96,112},{112,96},{1... | collective-permute-start | bytes 307208 | tf_op jit(solution)/shard_map/ppermute | solution.py:389
  21.9 3.7 %collective-permute-start.9 = (bf16[400,128]{1,0:T(8,128)(2,1)S(1)}, bf16[400,128]{1,0:T(8,128)(2,1)S(1)}, u32[]{:S(2)}, u32[]{:S(2)}) collective-permute-start(bf16[400,128]{1,0:T(8,128)(2,1)S(1)} %chip_sum.2.after_ref.own_ref), channel_id=1, source_target_pairs={{0,64},{16,80},{32,96},{48,112},{64,0},{80,16},{96,32},{112,48},{1... | collective-permute-start | bytes 307208 | tf_op jit(solution)/shard_map/ppermute | solution.py:394
  26.3 3.4 %transpose.1 = (bf16[384,128,128]{2,1,0:T(8,128)(2,1)S(1)}, bf16[384,768]{1,0:T(8,128)(2,1)S(1)}, bf16[512,384]{1,0:T(8,128)(2,1)S(1)}) custom-call(s32[1,1]{1,0:T(1,128)S(6)} %copy.6.live_ref, bf16[400,128]{1,0:T(8,128)(2,1)S(1)} %chip_sum.2.after_ref.own_ref, s32[1,384]{1,0:T(1,128)S(1)} %get-tuple-element.31.rows_ref, ...), custom_call_target="tpu_custom_call" | custom-call | bytes 12582912 | tf_op jit(solution)/shard_map/transpose/pallas_call | solution.py:474
  34.0 2.1 %forward.2.own_ref = bf16[528,128]{1,0:T(8,128)(2,1)S(1)} custom-call(bf16[400,128]{1,0:T(8,128)(2,1)S(1)} %get-tuple-element.37.own_ref, bf16[400,128]{1,0:T(8,128)(2,1)S(1)} %collective-permute-done.10.got_ref, bf16[384,768]{1,0:T(8,128)(2,1)S(1)} %get-tuple-element.38.pick_ref, bf16[512,384]{1,0:T(8,128)(2,1)S(1)} %get-tuple-element.39.hot_ref, ...), custom_call_target="tpu_custom_call" | custom-call | tf_op jit(solution)/shard_map/forward/pallas_call | solution.py:373
  36.0 2.9 %collective-permute-start.13 = (bf16[528,128]{1,0:T(8,128)(2,1)S(1)}, bf16[528,128]{1,0:T(8,128)(2,1)S(1)}, u32[]{:S(2)}, u32[]{:S(2)}) collective-permute-start(bf16[528,128]{1,0:T(8,128)(2,1)S(1)} %forward.2.own_ref), channel_id=1, source_target_pairs={{0,7},{1,6},{2,5},{3,4},{4,3},{5,2},{6,1},{7,0},{8,15},{9,14},{10,... | collective-permute-start | bytes 405512 | tf_op jit(solution)/shard_map/ppermute | solution.py:400
  40.0 2.4 %collective-permute-done.13.three_ref = bf16[528,128]{1,0:T(8,128)(2,1)S(1)} collective-permute-done((bf16[528,128]{1,0:T(8,128)(2,1)S(1)}, bf16[528,128]{1,0:T(8,128)(2,1)S(1)}, u32[]{:S(2)}, u32[]{:S(2)}) %collective-permute-start.13) | collective-permute-done | bytes 135200 | tf_op jit(solution)/shard_map/ppermute | solution.py:400
  42.4 1.9 %collective-permute-done.12.two_ref = bf16[528,128]{1,0:T(8,128)(2,1)S(1)} collective-permute-done((bf16[528,128]{1,0:T(8,128)(2,1)S(1)}, bf16[528,128]{1,0:T(8,128)(2,1)S(1)}, u32[]{:S(2)}, u32[]{:S(2)}) %collective-permute-start.12) | collective-permute-done | bytes 135200 | tf_op jit(solution)/shard_map/ppermute | solution.py:400
  44.7 2.7 %collective-permute-start.15 = (bf16[528,128]{1,0:T(8,128)(2,1)S(1)}, bf16[528,128]{1,0:T(8,128)(2,1)S(1)}, u32[]{:S(2)}, u32[]{:S(2)}) collective-permute-start(bf16[528,128]{1,0:T(8,128)(2,1)S(1)} %row_sum.2.own_ref), channel_id=1, source_target_pairs={{0,12},{1,13},{2,14},{3,15},{4,8},{5,9},{6,10},{7,11},{8,4},{9,5},... | collective-permute-start | bytes 405512 | tf_op jit(solution)/shard_map/ppermute | solution.py:400
  48.5 2.1 %collective-permute-done.16.three_ref = bf16[528,128]{1,0:T(8,128)(2,1)S(1)} collective-permute-done((bf16[528,128]{1,0:T(8,128)(2,1)S(1)}, bf16[528,128]{1,0:T(8,128)(2,1)S(1)}, u32[]{:S(2)}, u32[]{:S(2)}) %collective-permute-start.16) | collective-permute-done | bytes 135200 | tf_op jit(solution)/shard_map/ppermute | solution.py:400
  52.7 2.1 %second_adjoint.1 = (f32[512,128]{1,0:T(8,128)S(1)}, f32[8,128]{1,0:T(8,128)S(1)}, f32[384,128]{1,0:T(8,128)S(1)}, bf16[400,128]{1,0:T(8,128)(2,1)S(1)}) custom-call(bf16[528,128]{1,0:T(8,128)(2,1)S(1)} %row_sum.2.own_ref, bf16[528,128]{1,0:T(8,128)(2,1)S(1)} %collective-permute-done.14.one_ref, bf16[528,128]{1,0:T(8,128)(2,1)S(1)} %collective-permute-done.15.two_ref, ...), custom_call_target="tpu_custom_call" | custom-call | tf_op jit(solution)/shard_map/second_adjoint/pallas_call | solution.py:373
  54.8 2.4 %collective-permute-start.17 = (bf16[400,128]{1,0:T(8,128)(2,1)S(1)}, bf16[400,128]{1,0:T(8,128)(2,1)S(1)}, u32[]{:S(2)}, u32[]{:S(2)}) collective-permute-start(bf16[400,128]{1,0:T(8,128)(2,1)S(1)} %get-tuple-element.44.send_ref), channel_id=1, source_target_pairs={{0,16},{16,0},{32,48},{48,32},{64,80},{80,64},{96,112},{112,96},{1... | collective-permute-start | bytes 307208 | tf_op jit(solution)/shard_map/ppermute | solution.py:389
  58.2 1.8 %collective-permute-start.20 = (bf16[400,128]{1,0:T(8,128)(2,1)S(1)}, bf16[400,128]{1,0:T(8,128)(2,1)S(1)}, u32[]{:S(2)}, u32[]{:S(2)}) collective-permute-start(bf16[400,128]{1,0:T(8,128)(2,1)S(1)} %chip_sum.3.own_ref), channel_id=1, source_target_pairs={{0,64},{16,80},{32,96},{48,112},{64,0},{80,16},{96,32},{112,48},{1... | collective-permute-start | bytes 307208 | tf_op jit(solution)/shard_map/ppermute | solution.py:394
  61.6 2.4 %collective-permute-done.20.three_ref = bf16[400,128]{1,0:T(8,128)(2,1)S(1)} collective-permute-done((bf16[400,128]{1,0:T(8,128)(2,1)S(1)}, bf16[400,128]{1,0:T(8,128)(2,1)S(1)}, u32[]{:S(2)}, u32[]{:S(2)}) %collective-permute-start.20) | collective-permute-done | bytes 102432 | tf_op jit(solution)/shard_map/ppermute | solution.py:394
  68.9 2.1 %forward.3.own_ref = bf16[528,128]{1,0:T(8,128)(2,1)S(1)} custom-call(bf16[400,128]{1,0:T(8,128)(2,1)S(1)} %get-tuple-element.47.own_ref, bf16[400,128]{1,0:T(8,128)(2,1)S(1)} %collective-permute-done.21.got_ref, bf16[384,768]{1,0:T(8,128)(2,1)S(1)} %get-tuple-element.38.pick_ref, bf16[512,384]{1,0:T(8,128)(2,1)S(1)} %get-tuple-element.39.hot_ref, ...), custom_call_target="tpu_custom_call" | custom-call | tf_op jit(solution)/shard_map/forward/pallas_call | solution.py:373
  71.0 2.9 %collective-permute-start.24 = (bf16[528,128]{1,0:T(8,128)(2,1)S(1)}, bf16[528,128]{1,0:T(8,128)(2,1)S(1)}, u32[]{:S(2)}, u32[]{:S(2)}) collective-permute-start(bf16[528,128]{1,0:T(8,128)(2,1)S(1)} %forward.3.own_ref), channel_id=1, source_target_pairs={{0,7},{1,6},{2,5},{3,4},{4,3},{5,2},{6,1},{7,0},{8,15},{9,14},{10,... | collective-permute-start | bytes 405512 | tf_op jit(solution)/shard_map/ppermute | solution.py:400
  74.9 2.4 %collective-permute-done.24.three_ref = bf16[528,128]{1,0:T(8,128)(2,1)S(1)} collective-permute-done((bf16[528,128]{1,0:T(8,128)(2,1)S(1)}, bf16[528,128]{1,0:T(8,128)(2,1)S(1)}, u32[]{:S(2)}, u32[]{:S(2)}) %collective-permute-start.24) | collective-permute-done | bytes 135200 | tf_op jit(solution)/shard_map/ppermute | solution.py:400
  77.3 2.0 %collective-permute-done.23.two_ref = bf16[528,128]{1,0:T(8,128)(2,1)S(1)} collective-permute-done((bf16[528,128]{1,0:T(8,128)(2,1)S(1)}, bf16[528,128]{1,0:T(8,128)(2,1)S(1)}, u32[]{:S(2)}, u32[]{:S(2)}) %collective-permute-start.23) | collective-permute-done | bytes 135200 | tf_op jit(solution)/shard_map/ppermute | solution.py:400
  79.5 2.3 %collective-permute-start.26 = (bf16[528,128]{1,0:T(8,128)(2,1)S(1)}, bf16[528,128]{1,0:T(8,128)(2,1)S(1)}, u32[]{:S(2)}, u32[]{:S(2)}) collective-permute-start(bf16[528,128]{1,0:T(8,128)(2,1)S(1)} %row_sum.3.own_ref), channel_id=1, source_target_pairs={{0,12},{1,13},{2,14},{3,15},{4,8},{5,9},{6,10},{7,11},{8,4},{9,5},... | collective-permute-start | bytes 405512 | tf_op jit(solution)/shard_map/ppermute | solution.py:400
  83.3 2.1 %collective-permute-done.27.three_ref = bf16[528,128]{1,0:T(8,128)(2,1)S(1)} collective-permute-done((bf16[528,128]{1,0:T(8,128)(2,1)S(1)}, bf16[528,128]{1,0:T(8,128)(2,1)S(1)}, u32[]{:S(2)}, u32[]{:S(2)}) %collective-permute-start.27) | collective-permute-done | bytes 135200 | tf_op jit(solution)/shard_map/ppermute | solution.py:400
  87.5 1.9 %collective-permute-start.28 = (f32[8,128]{1,0:T(8,128)S(1)}, f32[8,128]{1,0:T(8,128)S(1)}, u32[]{:S(2)}, u32[]{:S(2)}) collective-permute-start(f32[8,128]{1,0:T(8,128)S(1)} %get-tuple-element.50.own_ref), channel_id=1, source_target_pairs={{0,16},{16,0},{32,48},{48,32},{64,80},{80,64},{96,112},{112,96},{1... | collective-permute-start | bytes 12296 | tf_op jit(solution)/shard_map/ppermute | solution.py:389
  (59 shorter events, 35.9 us)
Async XLA Ops:
  0.0 7.9 %collective-permute-start = (f32[32,128]{1,0:T(8,128)}, f32[32,128]{1,0:T(8,128)S(1)}, u32[]{:S(2)}, u32[]{:S(2)}) collective-permute-start(f32[32,128]{1,0:T(8,128)} %data_ref.1), channel_id=1, source_target_pairs={{0,3},{1,2},{2,1},{3,0},{4,7},{5,6},{6,5},{7,4},{8,11},{9,10},{10,... | collective-permute-start | bytes 49160 | tf_op jit(solution)/shard_map/ppermute | solution.py:407
  3.6 4.9 %collective-permute-start.2 = (f32[32,128]{1,0:T(8,128)}, f32[32,128]{1,0:T(8,128)S(1)}, u32[]{:S(2)}, u32[]{:S(2)}) collective-permute-start(f32[32,128]{1,0:T(8,128)} %data_ref.1), channel_id=1, source_target_pairs={{0,7},{1,6},{2,5},{3,4},{4,3},{5,2},{6,1},{7,0},{8,15},{9,14},{10,... | collective-permute-start | bytes 49160 | tf_op jit(solution)/shard_map/ppermute | solution.py:407
  4.5 4.0 %collective-permute-start.1 = (f32[32,128]{1,0:T(8,128)}, f32[32,128]{1,0:T(8,128)S(1)}, u32[]{:S(2)}, u32[]{:S(2)}) collective-permute-start(f32[32,128]{1,0:T(8,128)} %data_ref.1), channel_id=1, source_target_pairs={{0,4},{1,5},{2,6},{3,7},{4,0},{5,1},{6,2},{7,3},{8,12},{9,13},{10,... | collective-permute-start | bytes 49160 | tf_op jit(solution)/shard_map/ppermute | solution.py:407
  8.5 7.3 %collective-permute-start.5 = (f32[128,128]{1,0:T(8,128)S(1)}, f32[128,128]{1,0:T(8,128)S(1)}, u32[]{:S(2)}, u32[]{:S(2)}) collective-permute-start(f32[128,128]{1,0:T(8,128)S(1)} %collect.1.after_ref.own_ref), channel_id=1, source_target_pairs={{0,13},{1,12},{2,15},{3,14},{4,9},{5,8},{6,11},{7,10},{8,5},{9,4},... | collective-permute-start | bytes 196616 | tf_op jit(solution)/shard_map/ppermute | solution.py:407
  10.2 5.6 %collective-permute-start.4 = (f32[128,128]{1,0:T(8,128)S(1)}, f32[128,128]{1,0:T(8,128)S(1)}, u32[]{:S(2)}, u32[]{:S(2)}) collective-permute-start(f32[128,128]{1,0:T(8,128)S(1)} %collect.1.after_ref.own_ref), channel_id=1, source_target_pairs={{0,12},{1,13},{2,14},{3,15},{4,8},{5,9},{6,10},{7,11},{8,4},{9,5},... | collective-permute-start | bytes 196616 | tf_op jit(solution)/shard_map/ppermute | solution.py:407
  11.1 4.6 %collective-permute-start.3 = (f32[128,128]{1,0:T(8,128)S(1)}, f32[128,128]{1,0:T(8,128)S(1)}, u32[]{:S(2)}, u32[]{:S(2)}) collective-permute-start(f32[128,128]{1,0:T(8,128)S(1)} %collect.1.after_ref.own_ref), channel_id=1, source_target_pairs={{0,1},{1,0},{2,3},{3,2},{4,5},{5,4},{6,7},{7,6},{8,9},{9,8},{10,11... | collective-permute-start | bytes 196616 | tf_op jit(solution)/shard_map/ppermute | solution.py:407
  21.9 7.8 %collective-permute-start.9 = (bf16[400,128]{1,0:T(8,128)(2,1)S(1)}, bf16[400,128]{1,0:T(8,128)(2,1)S(1)}, u32[]{:S(2)}, u32[]{:S(2)}) collective-permute-start(bf16[400,128]{1,0:T(8,128)(2,1)S(1)} %chip_sum.2.after_ref.own_ref), channel_id=1, source_target_pairs={{0,64},{16,80},{32,96},{48,112},{64,0},{80,16},{96,32},{112,48},{1... | collective-permute-start | bytes 307208 | tf_op jit(solution)/shard_map/ppermute | solution.py:394
  25.5 5.6 %collective-permute-start.8 = (bf16[400,128]{1,0:T(8,128)(2,1)S(1)}, bf16[400,128]{1,0:T(8,128)(2,1)S(1)}, u32[]{:S(2)}, u32[]{:S(2)}) collective-permute-start(bf16[400,128]{1,0:T(8,128)(2,1)S(1)} %chip_sum.2.after_ref.own_ref), channel_id=1, source_target_pairs={{0,96},{16,48},{32,64},{48,16},{64,32},{80,112},{96,0},{112,80},{1... | collective-permute-start | bytes 307208 | tf_op jit(solution)/shard_map/ppermute | solution.py:394
  26.3 5.8 %collective-permute-start.7 = (bf16[400,128]{1,0:T(8,128)(2,1)S(1)}, bf16[400,128]{1,0:T(8,128)(2,1)S(1)}, u32[]{:S(2)}, u32[]{:S(2)}) collective-permute-start(bf16[400,128]{1,0:T(8,128)(2,1)S(1)} %chip_sum.2.after_ref.own_ref), channel_id=1, source_target_pairs={{0,32},{16,112},{32,0},{48,80},{64,96},{80,48},{96,64},{112,16},{1... | collective-permute-start | bytes 307208 | tf_op jit(solution)/shard_map/ppermute | solution.py:394
  36.0 6.3 %collective-permute-start.13 = (bf16[528,128]{1,0:T(8,128)(2,1)S(1)}, bf16[528,128]{1,0:T(8,128)(2,1)S(1)}, u32[]{:S(2)}, u32[]{:S(2)}) collective-permute-start(bf16[528,128]{1,0:T(8,128)(2,1)S(1)} %forward.2.own_ref), channel_id=1, source_target_pairs={{0,7},{1,6},{2,5},{3,4},{4,3},{5,2},{6,1},{7,0},{8,15},{9,14},{10,... | collective-permute-start | bytes 405512 | tf_op jit(solution)/shard_map/ppermute | solution.py:400
  38.9 5.4 %collective-permute-start.12 = (bf16[528,128]{1,0:T(8,128)(2,1)S(1)}, bf16[528,128]{1,0:T(8,128)(2,1)S(1)}, u32[]{:S(2)}, u32[]{:S(2)}) collective-permute-start(bf16[528,128]{1,0:T(8,128)(2,1)S(1)} %forward.2.own_ref), channel_id=1, source_target_pairs={{0,4},{1,5},{2,6},{3,7},{4,0},{5,1},{6,2},{7,3},{8,12},{9,13},{10,... | collective-permute-start | bytes 405512 | tf_op jit(solution)/shard_map/ppermute | solution.py:400
  39.9 4.4 %collective-permute-start.11 = (bf16[528,128]{1,0:T(8,128)(2,1)S(1)}, bf16[528,128]{1,0:T(8,128)(2,1)S(1)}, u32[]{:S(2)}, u32[]{:S(2)}) collective-permute-start(bf16[528,128]{1,0:T(8,128)(2,1)S(1)} %forward.2.own_ref), channel_id=1, source_target_pairs={{0,3},{1,2},{2,1},{3,0},{4,7},{5,6},{6,5},{7,4},{8,11},{9,10},{10,... | collective-permute-start | bytes 405512 | tf_op jit(solution)/shard_map/ppermute | solution.py:400
  44.4 6.2 %collective-permute-start.16 = (bf16[528,128]{1,0:T(8,128)(2,1)S(1)}, bf16[528,128]{1,0:T(8,128)(2,1)S(1)}, u32[]{:S(2)}, u32[]{:S(2)}) collective-permute-start(bf16[528,128]{1,0:T(8,128)(2,1)S(1)} %row_sum.2.own_ref), channel_id=1, source_target_pairs={{0,13},{1,12},{2,15},{3,14},{4,9},{5,8},{6,11},{7,10},{8,5},{9,4},... | collective-permute-start | bytes 405512 | tf_op jit(solution)/shard_map/ppermute | solution.py:400
  44.7 6.5 %collective-permute-start.15 = (bf16[528,128]{1,0:T(8,128)(2,1)S(1)}, bf16[528,128]{1,0:T(8,128)(2,1)S(1)}, u32[]{:S(2)}, u32[]{:S(2)}) collective-permute-start(bf16[528,128]{1,0:T(8,128)(2,1)S(1)} %row_sum.2.own_ref), channel_id=1, source_target_pairs={{0,12},{1,13},{2,14},{3,15},{4,8},{5,9},{6,10},{7,11},{8,4},{9,5},... | collective-permute-start | bytes 405512 | tf_op jit(solution)/shard_map/ppermute | solution.py:400
  47.3 5.4 %collective-permute-start.14 = (bf16[528,128]{1,0:T(8,128)(2,1)S(1)}, bf16[528,128]{1,0:T(8,128)(2,1)S(1)}, u32[]{:S(2)}, u32[]{:S(2)}) collective-permute-start(bf16[528,128]{1,0:T(8,128)(2,1)S(1)} %row_sum.2.own_ref), channel_id=1, source_target_pairs={{0,1},{1,0},{2,3},{3,2},{4,5},{5,4},{6,7},{7,6},{8,9},{9,8},{10,11... | collective-permute-start | bytes 405512 | tf_op jit(solution)/shard_map/ppermute | solution.py:400
  58.2 5.7 %collective-permute-start.20 = (bf16[400,128]{1,0:T(8,128)(2,1)S(1)}, bf16[400,128]{1,0:T(8,128)(2,1)S(1)}, u32[]{:S(2)}, u32[]{:S(2)}) collective-permute-start(bf16[400,128]{1,0:T(8,128)(2,1)S(1)} %chip_sum.3.own_ref), channel_id=1, source_target_pairs={{0,64},{16,80},{32,96},{48,112},{64,0},{80,16},{96,32},{112,48},{1... | collective-permute-start | bytes 307208 | tf_op jit(solution)/shard_map/ppermute | solution.py:394
  60.1 5.5 %collective-permute-start.19 = (bf16[400,128]{1,0:T(8,128)(2,1)S(1)}, bf16[400,128]{1,0:T(8,128)(2,1)S(1)}, u32[]{:S(2)}, u32[]{:S(2)}) collective-permute-start(bf16[400,128]{1,0:T(8,128)(2,1)S(1)} %chip_sum.3.own_ref), channel_id=1, source_target_pairs={{0,96},{16,48},{32,64},{48,16},{64,32},{80,112},{96,0},{112,80},{1... | collective-permute-start | bytes 307208 | tf_op jit(solution)/shard_map/ppermute | solution.py:394
  60.8 6.3 %collective-permute-start.18 = (bf16[400,128]{1,0:T(8,128)(2,1)S(1)}, bf16[400,128]{1,0:T(8,128)(2,1)S(1)}, u32[]{:S(2)}, u32[]{:S(2)}) collective-permute-start(bf16[400,128]{1,0:T(8,128)(2,1)S(1)} %chip_sum.3.own_ref), channel_id=1, source_target_pairs={{0,32},{16,112},{32,0},{48,80},{64,96},{80,48},{96,64},{112,16},{1... | collective-permute-start | bytes 307208 | tf_op jit(solution)/shard_map/ppermute | solution.py:394
  71.0 6.3 %collective-permute-start.24 = (bf16[528,128]{1,0:T(8,128)(2,1)S(1)}, bf16[528,128]{1,0:T(8,128)(2,1)S(1)}, u32[]{:S(2)}, u32[]{:S(2)}) collective-permute-start(bf16[528,128]{1,0:T(8,128)(2,1)S(1)} %forward.3.own_ref), channel_id=1, source_target_pairs={{0,7},{1,6},{2,5},{3,4},{4,3},{5,2},{6,1},{7,0},{8,15},{9,14},{10,... | collective-permute-start | bytes 405512 | tf_op jit(solution)/shard_map/ppermute | solution.py:400
  73.9 5.4 %collective-permute-start.23 = (bf16[528,128]{1,0:T(8,128)(2,1)S(1)}, bf16[528,128]{1,0:T(8,128)(2,1)S(1)}, u32[]{:S(2)}, u32[]{:S(2)}) collective-permute-start(bf16[528,128]{1,0:T(8,128)(2,1)S(1)} %forward.3.own_ref), channel_id=1, source_target_pairs={{0,4},{1,5},{2,6},{3,7},{4,0},{5,1},{6,2},{7,3},{8,12},{9,13},{10,... | collective-permute-start | bytes 405512 | tf_op jit(solution)/shard_map/ppermute | solution.py:400
  74.9 4.4 %collective-permute-start.22 = (bf16[528,128]{1,0:T(8,128)(2,1)S(1)}, bf16[528,128]{1,0:T(8,128)(2,1)S(1)}, u32[]{:S(2)}, u32[]{:S(2)}) collective-permute-start(bf16[528,128]{1,0:T(8,128)(2,1)S(1)} %forward.3.own_ref), channel_id=1, source_target_pairs={{0,3},{1,2},{2,1},{3,0},{4,7},{5,6},{6,5},{7,4},{8,11},{9,10},{10,... | collective-permute-start | bytes 405512 | tf_op jit(solution)/shard_map/ppermute | solution.py:400
  79.4 6.0 %collective-permute-start.27 = (bf16[528,128]{1,0:T(8,128)(2,1)S(1)}, bf16[528,128]{1,0:T(8,128)(2,1)S(1)}, u32[]{:S(2)}, u32[]{:S(2)}) collective-permute-start(bf16[528,128]{1,0:T(8,128)(2,1)S(1)} %row_sum.3.own_ref), channel_id=1, source_target_pairs={{0,13},{1,12},{2,15},{3,14},{4,9},{5,8},{6,11},{7,10},{8,5},{9,4},... | collective-permute-start | bytes 405512 | tf_op jit(solution)/shard_map/ppermute | solution.py:400
  79.5 6.5 %collective-permute-start.26 = (bf16[528,128]{1,0:T(8,128)(2,1)S(1)}, bf16[528,128]{1,0:T(8,128)(2,1)S(1)}, u32[]{:S(2)}, u32[]{:S(2)}) collective-permute-start(bf16[528,128]{1,0:T(8,128)(2,1)S(1)} %row_sum.3.own_ref), channel_id=1, source_target_pairs={{0,12},{1,13},{2,14},{3,15},{4,8},{5,9},{6,10},{7,11},{8,4},{9,5},... | collective-permute-start | bytes 405512 | tf_op jit(solution)/shard_map/ppermute | solution.py:400
  81.8 5.4 %collective-permute-start.25 = (bf16[528,128]{1,0:T(8,128)(2,1)S(1)}, bf16[528,128]{1,0:T(8,128)(2,1)S(1)}, u32[]{:S(2)}, u32[]{:S(2)}) collective-permute-start(bf16[528,128]{1,0:T(8,128)(2,1)S(1)} %row_sum.3.own_ref), channel_id=1, source_target_pairs={{0,1},{1,0},{2,3},{3,2},{4,5},{5,4},{6,7},{7,6},{8,9},{9,8},{10,11... | collective-permute-start | bytes 405512 | tf_op jit(solution)/shard_map/ppermute | solution.py:400
  (8 other events, 23.6 us)

commit v7 on v6

--- a/solution.py
+++ b/solution.py
@@ -73,10 +73,13 @@
     return jnp.where((jnp.broadcast_to(index, (size, slots)) == row) & (lane < live), 1.0, 0.0).astype(BF16)
 
 
-def gather(pick_ref, source, picked_ref):
+def gather(pick_ref, source, picked_ref, also_ref=None):
     for start in range(0, picked_ref.shape[0], BS):
-        piece = jnp.dot(pick_ref[start : start + BS, :], source, preferred_element_type=F32)
-        picked_ref[start : start + BS, :] = piece.astype(BF16)
+        rows = slice(start, start + BS)
+        piece = jnp.dot(pick_ref[rows, :], source, preferred_element_type=F32)
+        if also_ref is not None:
+            piece += also_ref[rows, :].astype(F32)
+        picked_ref[rows, :] = piece.astype(BF16)
 
 
 def scatter(products_ref, hot_ref):
@@ -236,9 +239,12 @@
     model_out(total * (1.0 / beta) - last_ref[...] * (beta / alpha), beta2, model_ref, send_ref, beta2_ref)
 
 
-def forward(own_ref, got_ref, pick_ref, hot_ref, blocks_ref, out_ref, picked_ref, products_ref):
-    model = jnp.concatenate([own_ref[:HALF, :], got_ref[:HALF, :]], 0)
-    gather(pick_ref, model, picked_ref)
+def pick_own(own_ref, pick_ref, out_ref):
+    gather(pick_ref.at[:, :HALF], own_ref[:HALF, :], out_ref)
+
+
+def forward(own_ref, got_ref, mine_ref, pick_ref, hot_ref, blocks_ref, out_ref, picked_ref, products_ref):
+    gather(pick_ref.at[:, HALF:], got_ref[:HALF, :], picked_ref, mine_ref)
     multiply((blocks_ref,), picked_ref, products_ref)
     out_ref[:RB, :] = scatter(products_ref, hot_ref).astype(BF16)
     out_ref[RB:, :] = split_rows(joined_rows(own_ref[HALF:, :]) + joined_rows(got_ref[HALF:, :]))
@@ -453,7 +459,10 @@
     second = pltpu.with_memory_space_constraint(second, pltpu.VMEM)
 
     def forward_whole(own):
-        (part,) = call(forward, [(RB + EXTRA, BF16)], [own, over_core(own), pick_cols, add_rows, turned], (), slots, (BF16, F32))
+        got = over_core(own)
+        (mine,) = call(pick_own, [(slots, BF16)], [own, pick_cols], work=CB * slots * 2)
+        inputs = [own, got, mine, pick_cols, add_rows, turned]
+        (part,) = call(forward, [(RB + EXTRA, BF16)], inputs, (), slots, (BF16, F32))
         (part,) = call(row_sum, [(RB + EXTRA, BF16)], [part, *over_square(part, NEAR)])
         return [part, *over_square(part, FAR)]
 

time: 96.8 us -> 96.6 us (level)
    pallas_call x16 -> x18, Pallas kernels: 10.5 us -> 10.8 us  [call(): pl.pallas_call(kernel, out_shape=[jax.ShapeDtypeStruct((rows, *(width or...]
where the time goes in v7:
time: 96.6 us; the launch traced here: 96.5 us
  starting transfers between devices  44.2 us (46%)
  waiting for transfers between devices  31.5 us (33%)
  Pallas kernels  19.9 us (21%)
    ppermute x12, waiting for transfers between devices, over_square(): lax.ppermute(x, ('dp', 'mp'), [(i * 16 + j, i * 16 + (j ^ step[i & 1])) f...  16.8 us
    ppermute x12, starting transfers between devices, over_square(): lax.ppermute(x, ('dp', 'mp'), [(i * 16 + j, i * 16 + (j ^ step[i & 1])) f...  15.9 us
    ppermute x9, starting transfers between devices, over_chips(): lax.ppermute(x, 'dp', [(i, (i >> 1 ^ step[i & 1]) * 2 + (i & 1)) for i in...  11 us
    pallas_call x18, Pallas kernels, call(): pl.pallas_call(kernel, out_shape=[jax.ShapeDtypeStruct((rows, *(width or...  10.8 us
    ppermute x9, waiting for transfers between devices, over_chips(): lax.ppermute(x, 'dp', [(i, (i >> 1 ^ step[i & 1]) * 2 + (i & 1)) for i in...  10.5 us
    ppermute x6, starting transfers between devices, over_places(): lax.ppermute(x, 'mp', [(j, j ^ step) for j in range(16)])  8.72 us
    ppermute x5, starting transfers between devices, over_core(): return lax.ppermute(x, 'dp', [(i, i ^ 1) for i in range(8)])  8.62 us
    ppermute x5, waiting for transfers between devices, over_core(): return lax.ppermute(x, 'dp', [(i, i ^ 1) for i in range(8)])  3.63 us
  transfers between devices with their start and end apart: 32, of which 24 were waited for; matrix products, arithmetic and copies ran while one was open for 0% of the time, Pallas kernels for 10%

profile of v7, /device:TPU:1, one launch (start us, length us, event | category | flops | bytes accessed | tf_op | source)
XLA Modules:
  0.0 96.5 jit_solution(2903533792350096512)
XLA Ops:
  0.0 3.6 %collective-permute-start = (f32[32,128]{1,0:T(8,128)}, f32[32,128]{1,0:T(8,128)S(1)}, u32[]{:S(2)}, u32[]{:S(2)}) collective-permute-start(f32[32,128]{1,0:T(8,128)} %data_ref.1), channel_id=1, source_target_pairs={{0,3},{1,2},{2,1},{3,0},{4,7},{5,6},{6,5},{7,4},{8,11},{9,10},{10,... | collective-permute-start | bytes 49160 | tf_op jit(solution)/shard_map/ppermute | solution.py:413
  5.4 2.4 %load_first.1 = (f32[32,128]{1,0:T(8,128)S(1)}, s32[1,384]{1,0:T(1,128)S(1)}, s32[1,384]{1,0:T(1,128)S(1)}, bf16[144,128,128]{2,1,0:T(8,128)(2,1)S(1)}) custom-call(s32[1,1]{1,0:T(1,128)S(6)} %copy.6.live_ref, f32[32,128]{1,0:T(8,128)} %data_ref.1, s32[1,384]{1,0:T(1,128)} %bitcast.5, s32[1,384]{1,0:T(1,128)} %bitcast.6, bf16[384,128,128]{2,1,0:T(8,128)(2,1)} %bitcast.3), custom_call_target="tpu_custom_call" | custom-call | bytes 12582912 | tf_op jit(solution)/shard_map/load_first/pallas_call | solution.py:428
  12.4 3.3 %load_second.1.second_ref = bf16[240,128,128]{2,1,0:T(8,128)(2,1)S(1)} custom-call(f32[128,128]{1,0:T(8,128)S(1)} %collect.1.after_ref.own_ref, bf16[384,128,128]{2,1,0:T(8,128)(2,1)} %bitcast.4), custom_call_target="tpu_custom_call" | custom-call | bytes 12582912 | tf_op jit(solution)/shard_map/load_second/pallas_call | solution.py:449
  15.8 2.1 %first_adjoint.1 = (f32[512,128]{1,0:T(8,128)S(1)}, bf16[384,512]{1,0:T(8,128)(2,1)S(1)}, bf16[768,384]{1,0:T(8,128)(2,1)S(1)}, f32[384,128]{1,0:T(8,128)S(1)}, bf16[400,128]{1,0:T(8,128)(2,1)S(1)}) custom-call(s32[1,1]{1,0:T(1,128)S(6)} %copy.6.live_ref, f32[128,128]{1,0:T(8,128)S(1)} %collect.1.after_ref.own_ref, ...), custom_call_target="tpu_custom_call" | custom-call | tf_op jit(solution)/shard_map/first_adjoint/pallas_call | solution.py:379
  17.8 3.0 %collective-permute-start.6 = (bf16[400,128]{1,0:T(8,128)(2,1)S(1)}, bf16[400,128]{1,0:T(8,128)(2,1)S(1)}, u32[]{:S(2)}, u32[]{:S(2)}) collective-permute-start(bf16[400,128]{1,0:T(8,128)(2,1)S(1)} %get-tuple-element.35.send_ref), channel_id=1, source_target_pairs={{0,16},{16,0},{32,48},{48,32},{64,80},{80,64},{96,112},{112,96},{1... | collective-permute-start | bytes 307208 | tf_op jit(solution)/shard_map/ppermute | solution.py:395
  21.9 3.7 %collective-permute-start.9 = (bf16[400,128]{1,0:T(8,128)(2,1)S(1)}, bf16[400,128]{1,0:T(8,128)(2,1)S(1)}, u32[]{:S(2)}, u32[]{:S(2)}) collective-permute-start(bf16[400,128]{1,0:T(8,128)(2,1)S(1)} %chip_sum.2.after_ref.own_ref), channel_id=1, source_target_pairs={{0,64},{16,80},{32,96},{48,112},{64,0},{80,16},{96,32},{112,48},{1... | collective-permute-start | bytes 307208 | tf_op jit(solution)/shard_map/ppermute | solution.py:400
  26.3 3.4 %transpose.1 = (bf16[384,128,128]{2,1,0:T(8,128)(2,1)S(1)}, bf16[384,768]{1,0:T(8,128)(2,1)S(1)}, bf16[512,384]{1,0:T(8,128)(2,1)S(1)}) custom-call(s32[1,1]{1,0:T(1,128)S(6)} %copy.6.live_ref, bf16[400,128]{1,0:T(8,128)(2,1)S(1)} %chip_sum.2.after_ref.own_ref, s32[1,384]{1,0:T(1,128)S(1)} %get-tuple-element.31.rows_ref, ...), custom_call_target="tpu_custom_call" | custom-call | bytes 12582912 | tf_op jit(solution)/shard_map/transpose/pallas_call | solution.py:483
  34.0 2.0 %forward.2.own_ref = bf16[528,128]{1,0:T(8,128)(2,1)S(1)} custom-call(bf16[400,128]{1,0:T(8,128)(2,1)S(1)} %get-tuple-element.37.own_ref, bf16[400,128]{1,0:T(8,128)(2,1)S(1)} %collective-permute-done.10.got_ref, bf16[384,128]{1,0:T(8,128)(2,1)S(1)} %pick_own.2.mine_ref, bf16[384,768]{1,0:T(8,128)(2,1)S(1)} %get-tuple-element.38.pick_ref, ...), custom_call_target="tpu_custom_call" | custom-call | tf_op jit(solution)/shard_map/forward/pallas_call | solution.py:379
  35.9 2.9 %collective-permute-start.13 = (bf16[528,128]{1,0:T(8,128)(2,1)S(1)}, bf16[528,128]{1,0:T(8,128)(2,1)S(1)}, u32[]{:S(2)}, u32[]{:S(2)}) collective-permute-start(bf16[528,128]{1,0:T(8,128)(2,1)S(1)} %forward.2.own_ref), channel_id=1, source_target_pairs={{0,7},{1,6},{2,5},{3,4},{4,3},{5,2},{6,1},{7,0},{8,15},{9,14},{10,... | collective-permute-start | bytes 405512 | tf_op jit(solution)/shard_map/ppermute | solution.py:406
  39.9 2.4 %collective-permute-done.13.three_ref = bf16[528,128]{1,0:T(8,128)(2,1)S(1)} collective-permute-done((bf16[528,128]{1,0:T(8,128)(2,1)S(1)}, bf16[528,128]{1,0:T(8,128)(2,1)S(1)}, u32[]{:S(2)}, u32[]{:S(2)}) %collective-permute-start.13) | collective-permute-done | bytes 135200 | tf_op jit(solution)/shard_map/ppermute | solution.py:406
  42.3 1.9 %collective-permute-done.12.two_ref = bf16[528,128]{1,0:T(8,128)(2,1)S(1)} collective-permute-done((bf16[528,128]{1,0:T(8,128)(2,1)S(1)}, bf16[528,128]{1,0:T(8,128)(2,1)S(1)}, u32[]{:S(2)}, u32[]{:S(2)}) %collective-permute-start.12) | collective-permute-done | bytes 135200 | tf_op jit(solution)/shard_map/ppermute | solution.py:406
  44.6 2.7 %collective-permute-start.15 = (bf16[528,128]{1,0:T(8,128)(2,1)S(1)}, bf16[528,128]{1,0:T(8,128)(2,1)S(1)}, u32[]{:S(2)}, u32[]{:S(2)}) collective-permute-start(bf16[528,128]{1,0:T(8,128)(2,1)S(1)} %row_sum.2.own_ref), channel_id=1, source_target_pairs={{0,12},{1,13},{2,14},{3,15},{4,8},{5,9},{6,10},{7,11},{8,4},{9,5},... | collective-permute-start | bytes 405512 | tf_op jit(solution)/shard_map/ppermute | solution.py:406
  48.4 2.1 %collective-permute-done.16.three_ref = bf16[528,128]{1,0:T(8,128)(2,1)S(1)} collective-permute-done((bf16[528,128]{1,0:T(8,128)(2,1)S(1)}, bf16[528,128]{1,0:T(8,128)(2,1)S(1)}, u32[]{:S(2)}, u32[]{:S(2)}) %collective-permute-start.16) | collective-permute-done | bytes 135200 | tf_op jit(solution)/shard_map/ppermute | solution.py:406
  52.6 2.1 %second_adjoint.1 = (f32[512,128]{1,0:T(8,128)S(1)}, f32[8,128]{1,0:T(8,128)S(1)}, f32[384,128]{1,0:T(8,128)S(1)}, bf16[400,128]{1,0:T(8,128)(2,1)S(1)}) custom-call(bf16[528,128]{1,0:T(8,128)(2,1)S(1)} %row_sum.2.own_ref, bf16[528,128]{1,0:T(8,128)(2,1)S(1)} %collective-permute-done.14.one_ref, bf16[528,128]{1,0:T(8,128)(2,1)S(1)} %collective-permute-done.15.two_ref, ...), custom_call_target="tpu_custom_call" | custom-call | tf_op jit(solution)/shard_map/second_adjoint/pallas_call | solution.py:379
  54.7 2.4 %collective-permute-start.17 = (bf16[400,128]{1,0:T(8,128)(2,1)S(1)}, bf16[400,128]{1,0:T(8,128)(2,1)S(1)}, u32[]{:S(2)}, u32[]{:S(2)}) collective-permute-start(bf16[400,128]{1,0:T(8,128)(2,1)S(1)} %get-tuple-element.44.send_ref), channel_id=1, source_target_pairs={{0,16},{16,0},{32,48},{48,32},{64,80},{80,64},{96,112},{112,96},{1... | collective-permute-start | bytes 307208 | tf_op jit(solution)/shard_map/ppermute | solution.py:395
  58.1 1.8 %collective-permute-start.20 = (bf16[400,128]{1,0:T(8,128)(2,1)S(1)}, bf16[400,128]{1,0:T(8,128)(2,1)S(1)}, u32[]{:S(2)}, u32[]{:S(2)}) collective-permute-start(bf16[400,128]{1,0:T(8,128)(2,1)S(1)} %chip_sum.3.own_ref), channel_id=1, source_target_pairs={{0,64},{16,80},{32,96},{48,112},{64,0},{80,16},{96,32},{112,48},{1... | collective-permute-start | bytes 307208 | tf_op jit(solution)/shard_map/ppermute | solution.py:400
  61.5 2.4 %collective-permute-done.20.three_ref = bf16[400,128]{1,0:T(8,128)(2,1)S(1)} collective-permute-done((bf16[400,128]{1,0:T(8,128)(2,1)S(1)}, bf16[400,128]{1,0:T(8,128)(2,1)S(1)}, u32[]{:S(2)}, u32[]{:S(2)}) %collective-permute-start.20) | collective-permute-done | bytes 102432 | tf_op jit(solution)/shard_map/ppermute | solution.py:400
  68.8 2.0 %forward.3.own_ref = bf16[528,128]{1,0:T(8,128)(2,1)S(1)} custom-call(bf16[400,128]{1,0:T(8,128)(2,1)S(1)} %get-tuple-element.47.own_ref, bf16[400,128]{1,0:T(8,128)(2,1)S(1)} %collective-permute-done.21.got_ref, bf16[384,128]{1,0:T(8,128)(2,1)S(1)} %pick_own.3.mine_ref, bf16[384,768]{1,0:T(8,128)(2,1)S(1)} %get-tuple-element.38.pick_ref, ...), custom_call_target="tpu_custom_call" | custom-call | tf_op jit(solution)/shard_map/forward/pallas_call | solution.py:379
  70.8 2.9 %collective-permute-start.24 = (bf16[528,128]{1,0:T(8,128)(2,1)S(1)}, bf16[528,128]{1,0:T(8,128)(2,1)S(1)}, u32[]{:S(2)}, u32[]{:S(2)}) collective-permute-start(bf16[528,128]{1,0:T(8,128)(2,1)S(1)} %forward.3.own_ref), channel_id=1, source_target_pairs={{0,7},{1,6},{2,5},{3,4},{4,3},{5,2},{6,1},{7,0},{8,15},{9,14},{10,... | collective-permute-start | bytes 405512 | tf_op jit(solution)/shard_map/ppermute | solution.py:406
  74.7 2.4 %collective-permute-done.24.three_ref = bf16[528,128]{1,0:T(8,128)(2,1)S(1)} collective-permute-done((bf16[528,128]{1,0:T(8,128)(2,1)S(1)}, bf16[528,128]{1,0:T(8,128)(2,1)S(1)}, u32[]{:S(2)}, u32[]{:S(2)}) %collective-permute-start.24) | collective-permute-done | bytes 135200 | tf_op jit(solution)/shard_map/ppermute | solution.py:406
  77.1 2.0 %collective-permute-done.23.two_ref = bf16[528,128]{1,0:T(8,128)(2,1)S(1)} collective-permute-done((bf16[528,128]{1,0:T(8,128)(2,1)S(1)}, bf16[528,128]{1,0:T(8,128)(2,1)S(1)}, u32[]{:S(2)}, u32[]{:S(2)}) %collective-permute-start.23) | collective-permute-done | bytes 135200 | tf_op jit(solution)/shard_map/ppermute | solution.py:406
  79.3 2.3 %collective-permute-start.26 = (bf16[528,128]{1,0:T(8,128)(2,1)S(1)}, bf16[528,128]{1,0:T(8,128)(2,1)S(1)}, u32[]{:S(2)}, u32[]{:S(2)}) collective-permute-start(bf16[528,128]{1,0:T(8,128)(2,1)S(1)} %row_sum.3.own_ref), channel_id=1, source_target_pairs={{0,12},{1,13},{2,14},{3,15},{4,8},{5,9},{6,10},{7,11},{8,4},{9,5},... | collective-permute-start | bytes 405512 | tf_op jit(solution)/shard_map/ppermute | solution.py:406
  83.1 2.1 %collective-permute-done.27.three_ref = bf16[528,128]{1,0:T(8,128)(2,1)S(1)} collective-permute-done((bf16[528,128]{1,0:T(8,128)(2,1)S(1)}, bf16[528,128]{1,0:T(8,128)(2,1)S(1)}, u32[]{:S(2)}, u32[]{:S(2)}) %collective-permute-start.27) | collective-permute-done | bytes 135200 | tf_op jit(solution)/shard_map/ppermute | solution.py:406
  87.3 1.9 %collective-permute-start.28 = (f32[8,128]{1,0:T(8,128)S(1)}, f32[8,128]{1,0:T(8,128)S(1)}, u32[]{:S(2)}, u32[]{:S(2)}) collective-permute-start(f32[8,128]{1,0:T(8,128)S(1)} %get-tuple-element.50.own_ref), channel_id=1, source_target_pairs={{0,16},{16,0},{32,48},{48,32},{64,80},{80,64},{96,112},{112,96},{1... | collective-permute-start | bytes 12296 | tf_op jit(solution)/shard_map/ppermute | solution.py:395
  (61 shorter events, 35.9 us)
Async XLA Ops:
  0.0 7.9 %collective-permute-start = (f32[32,128]{1,0:T(8,128)}, f32[32,128]{1,0:T(8,128)S(1)}, u32[]{:S(2)}, u32[]{:S(2)}) collective-permute-start(f32[32,128]{1,0:T(8,128)} %data_ref.1), channel_id=1, source_target_pairs={{0,3},{1,2},{2,1},{3,0},{4,7},{5,6},{6,5},{7,4},{8,11},{9,10},{10,... | collective-permute-start | bytes 49160 | tf_op jit(solution)/shard_map/ppermute | solution.py:413
  3.6 4.9 %collective-permute-start.2 = (f32[32,128]{1,0:T(8,128)}, f32[32,128]{1,0:T(8,128)S(1)}, u32[]{:S(2)}, u32[]{:S(2)}) collective-permute-start(f32[32,128]{1,0:T(8,128)} %data_ref.1), channel_id=1, source_target_pairs={{0,7},{1,6},{2,5},{3,4},{4,3},{5,2},{6,1},{7,0},{8,15},{9,14},{10,... | collective-permute-start | bytes 49160 | tf_op jit(solution)/shard_map/ppermute | solution.py:413
  4.5 4.0 %collective-permute-start.1 = (f32[32,128]{1,0:T(8,128)}, f32[32,128]{1,0:T(8,128)S(1)}, u32[]{:S(2)}, u32[]{:S(2)}) collective-permute-start(f32[32,128]{1,0:T(8,128)} %data_ref.1), channel_id=1, source_target_pairs={{0,4},{1,5},{2,6},{3,7},{4,0},{5,1},{6,2},{7,3},{8,12},{9,13},{10,... | collective-permute-start | bytes 49160 | tf_op jit(solution)/shard_map/ppermute | solution.py:413
  8.5 7.3 %collective-permute-start.5 = (f32[128,128]{1,0:T(8,128)S(1)}, f32[128,128]{1,0:T(8,128)S(1)}, u32[]{:S(2)}, u32[]{:S(2)}) collective-permute-start(f32[128,128]{1,0:T(8,128)S(1)} %collect.1.after_ref.own_ref), channel_id=1, source_target_pairs={{0,13},{1,12},{2,15},{3,14},{4,9},{5,8},{6,11},{7,10},{8,5},{9,4},... | collective-permute-start | bytes 196616 | tf_op jit(solution)/shard_map/ppermute | solution.py:413
  10.2 5.6 %collective-permute-start.4 = (f32[128,128]{1,0:T(8,128)S(1)}, f32[128,128]{1,0:T(8,128)S(1)}, u32[]{:S(2)}, u32[]{:S(2)}) collective-permute-start(f32[128,128]{1,0:T(8,128)S(1)} %collect.1.after_ref.own_ref), channel_id=1, source_target_pairs={{0,12},{1,13},{2,14},{3,15},{4,8},{5,9},{6,10},{7,11},{8,4},{9,5},... | collective-permute-start | bytes 196616 | tf_op jit(solution)/shard_map/ppermute | solution.py:413
  11.1 4.6 %collective-permute-start.3 = (f32[128,128]{1,0:T(8,128)S(1)}, f32[128,128]{1,0:T(8,128)S(1)}, u32[]{:S(2)}, u32[]{:S(2)}) collective-permute-start(f32[128,128]{1,0:T(8,128)S(1)} %collect.1.after_ref.own_ref), channel_id=1, source_target_pairs={{0,1},{1,0},{2,3},{3,2},{4,5},{5,4},{6,7},{7,6},{8,9},{9,8},{10,11... | collective-permute-start | bytes 196616 | tf_op jit(solution)/shard_map/ppermute | solution.py:413
  21.9 7.8 %collective-permute-start.9 = (bf16[400,128]{1,0:T(8,128)(2,1)S(1)}, bf16[400,128]{1,0:T(8,128)(2,1)S(1)}, u32[]{:S(2)}, u32[]{:S(2)}) collective-permute-start(bf16[400,128]{1,0:T(8,128)(2,1)S(1)} %chip_sum.2.after_ref.own_ref), channel_id=1, source_target_pairs={{0,64},{16,80},{32,96},{48,112},{64,0},{80,16},{96,32},{112,48},{1... | collective-permute-start | bytes 307208 | tf_op jit(solution)/shard_map/ppermute | solution.py:400
  25.5 5.6 %collective-permute-start.8 = (bf16[400,128]{1,0:T(8,128)(2,1)S(1)}, bf16[400,128]{1,0:T(8,128)(2,1)S(1)}, u32[]{:S(2)}, u32[]{:S(2)}) collective-permute-start(bf16[400,128]{1,0:T(8,128)(2,1)S(1)} %chip_sum.2.after_ref.own_ref), channel_id=1, source_target_pairs={{0,96},{16,48},{32,64},{48,16},{64,32},{80,112},{96,0},{112,80},{1... | collective-permute-start | bytes 307208 | tf_op jit(solution)/shard_map/ppermute | solution.py:400
  26.3 5.8 %collective-permute-start.7 = (bf16[400,128]{1,0:T(8,128)(2,1)S(1)}, bf16[400,128]{1,0:T(8,128)(2,1)S(1)}, u32[]{:S(2)}, u32[]{:S(2)}) collective-permute-start(bf16[400,128]{1,0:T(8,128)(2,1)S(1)} %chip_sum.2.after_ref.own_ref), channel_id=1, source_target_pairs={{0,32},{16,112},{32,0},{48,80},{64,96},{80,48},{96,64},{112,16},{1... | collective-permute-start | bytes 307208 | tf_op jit(solution)/shard_map/ppermute | solution.py:400
  35.9 6.3 %collective-permute-start.13 = (bf16[528,128]{1,0:T(8,128)(2,1)S(1)}, bf16[528,128]{1,0:T(8,128)(2,1)S(1)}, u32[]{:S(2)}, u32[]{:S(2)}) collective-permute-start(bf16[528,128]{1,0:T(8,128)(2,1)S(1)} %forward.2.own_ref), channel_id=1, source_target_pairs={{0,7},{1,6},{2,5},{3,4},{4,3},{5,2},{6,1},{7,0},{8,15},{9,14},{10,... | collective-permute-start | bytes 405512 | tf_op jit(solution)/shard_map/ppermute | solution.py:406
  38.8 5.4 %collective-permute-start.12 = (bf16[528,128]{1,0:T(8,128)(2,1)S(1)}, bf16[528,128]{1,0:T(8,128)(2,1)S(1)}, u32[]{:S(2)}, u32[]{:S(2)}) collective-permute-start(bf16[528,128]{1,0:T(8,128)(2,1)S(1)} %forward.2.own_ref), channel_id=1, source_target_pairs={{0,4},{1,5},{2,6},{3,7},{4,0},{5,1},{6,2},{7,3},{8,12},{9,13},{10,... | collective-permute-start | bytes 405512 | tf_op jit(solution)/shard_map/ppermute | solution.py:406
  39.8 4.4 %collective-permute-start.11 = (bf16[528,128]{1,0:T(8,128)(2,1)S(1)}, bf16[528,128]{1,0:T(8,128)(2,1)S(1)}, u32[]{:S(2)}, u32[]{:S(2)}) collective-permute-start(bf16[528,128]{1,0:T(8,128)(2,1)S(1)} %forward.2.own_ref), channel_id=1, source_target_pairs={{0,3},{1,2},{2,1},{3,0},{4,7},{5,6},{6,5},{7,4},{8,11},{9,10},{10,... | collective-permute-start | bytes 405512 | tf_op jit(solution)/shard_map/ppermute | solution.py:406
  44.3 6.2 %collective-permute-start.16 = (bf16[528,128]{1,0:T(8,128)(2,1)S(1)}, bf16[528,128]{1,0:T(8,128)(2,1)S(1)}, u32[]{:S(2)}, u32[]{:S(2)}) collective-permute-start(bf16[528,128]{1,0:T(8,128)(2,1)S(1)} %row_sum.2.own_ref), channel_id=1, source_target_pairs={{0,13},{1,12},{2,15},{3,14},{4,9},{5,8},{6,11},{7,10},{8,5},{9,4},... | collective-permute-start | bytes 405512 | tf_op jit(solution)/shard_map/ppermute | solution.py:406
  44.6 6.5 %collective-permute-start.15 = (bf16[528,128]{1,0:T(8,128)(2,1)S(1)}, bf16[528,128]{1,0:T(8,128)(2,1)S(1)}, u32[]{:S(2)}, u32[]{:S(2)}) collective-permute-start(bf16[528,128]{1,0:T(8,128)(2,1)S(1)} %row_sum.2.own_ref), channel_id=1, source_target_pairs={{0,12},{1,13},{2,14},{3,15},{4,8},{5,9},{6,10},{7,11},{8,4},{9,5},... | collective-permute-start | bytes 405512 | tf_op jit(solution)/shard_map/ppermute | solution.py:406
  47.2 5.4 %collective-permute-start.14 = (bf16[528,128]{1,0:T(8,128)(2,1)S(1)}, bf16[528,128]{1,0:T(8,128)(2,1)S(1)}, u32[]{:S(2)}, u32[]{:S(2)}) collective-permute-start(bf16[528,128]{1,0:T(8,128)(2,1)S(1)} %row_sum.2.own_ref), channel_id=1, source_target_pairs={{0,1},{1,0},{2,3},{3,2},{4,5},{5,4},{6,7},{7,6},{8,9},{9,8},{10,11... | collective-permute-start | bytes 405512 | tf_op jit(solution)/shard_map/ppermute | solution.py:406
  58.1 5.7 %collective-permute-start.20 = (bf16[400,128]{1,0:T(8,128)(2,1)S(1)}, bf16[400,128]{1,0:T(8,128)(2,1)S(1)}, u32[]{:S(2)}, u32[]{:S(2)}) collective-permute-start(bf16[400,128]{1,0:T(8,128)(2,1)S(1)} %chip_sum.3.own_ref), channel_id=1, source_target_pairs={{0,64},{16,80},{32,96},{48,112},{64,0},{80,16},{96,32},{112,48},{1... | collective-permute-start | bytes 307208 | tf_op jit(solution)/shard_map/ppermute | solution.py:400
  60.0 5.5 %collective-permute-start.19 = (bf16[400,128]{1,0:T(8,128)(2,1)S(1)}, bf16[400,128]{1,0:T(8,128)(2,1)S(1)}, u32[]{:S(2)}, u32[]{:S(2)}) collective-permute-start(bf16[400,128]{1,0:T(8,128)(2,1)S(1)} %chip_sum.3.own_ref), channel_id=1, source_target_pairs={{0,96},{16,48},{32,64},{48,16},{64,32},{80,112},{96,0},{112,80},{1... | collective-permute-start | bytes 307208 | tf_op jit(solution)/shard_map/ppermute | solution.py:400
  60.7 6.3 %collective-permute-start.18 = (bf16[400,128]{1,0:T(8,128)(2,1)S(1)}, bf16[400,128]{1,0:T(8,128)(2,1)S(1)}, u32[]{:S(2)}, u32[]{:S(2)}) collective-permute-start(bf16[400,128]{1,0:T(8,128)(2,1)S(1)} %chip_sum.3.own_ref), channel_id=1, source_target_pairs={{0,32},{16,112},{32,0},{48,80},{64,96},{80,48},{96,64},{112,16},{1... | collective-permute-start | bytes 307208 | tf_op jit(solution)/shard_map/ppermute | solution.py:400
  70.8 6.3 %collective-permute-start.24 = (bf16[528,128]{1,0:T(8,128)(2,1)S(1)}, bf16[528,128]{1,0:T(8,128)(2,1)S(1)}, u32[]{:S(2)}, u32[]{:S(2)}) collective-permute-start(bf16[528,128]{1,0:T(8,128)(2,1)S(1)} %forward.3.own_ref), channel_id=1, source_target_pairs={{0,7},{1,6},{2,5},{3,4},{4,3},{5,2},{6,1},{7,0},{8,15},{9,14},{10,... | collective-permute-start | bytes 405512 | tf_op jit(solution)/shard_map/ppermute | solution.py:406
  73.7 5.4 %collective-permute-start.23 = (bf16[528,128]{1,0:T(8,128)(2,1)S(1)}, bf16[528,128]{1,0:T(8,128)(2,1)S(1)}, u32[]{:S(2)}, u32[]{:S(2)}) collective-permute-start(bf16[528,128]{1,0:T(8,128)(2,1)S(1)} %forward.3.own_ref), channel_id=1, source_target_pairs={{0,4},{1,5},{2,6},{3,7},{4,0},{5,1},{6,2},{7,3},{8,12},{9,13},{10,... | collective-permute-start | bytes 405512 | tf_op jit(solution)/shard_map/ppermute | solution.py:406
  74.6 4.4 %collective-permute-start.22 = (bf16[528,128]{1,0:T(8,128)(2,1)S(1)}, bf16[528,128]{1,0:T(8,128)(2,1)S(1)}, u32[]{:S(2)}, u32[]{:S(2)}) collective-permute-start(bf16[528,128]{1,0:T(8,128)(2,1)S(1)} %forward.3.own_ref), channel_id=1, source_target_pairs={{0,3},{1,2},{2,1},{3,0},{4,7},{5,6},{6,5},{7,4},{8,11},{9,10},{10,... | collective-permute-start | bytes 405512 | tf_op jit(solution)/shard_map/ppermute | solution.py:406
  79.2 6.0 %collective-permute-start.27 = (bf16[528,128]{1,0:T(8,128)(2,1)S(1)}, bf16[528,128]{1,0:T(8,128)(2,1)S(1)}, u32[]{:S(2)}, u32[]{:S(2)}) collective-permute-start(bf16[528,128]{1,0:T(8,128)(2,1)S(1)} %row_sum.3.own_ref), channel_id=1, source_target_pairs={{0,13},{1,12},{2,15},{3,14},{4,9},{5,8},{6,11},{7,10},{8,5},{9,4},... | collective-permute-start | bytes 405512 | tf_op jit(solution)/shard_map/ppermute | solution.py:406
  79.3 6.5 %collective-permute-start.26 = (bf16[528,128]{1,0:T(8,128)(2,1)S(1)}, bf16[528,128]{1,0:T(8,128)(2,1)S(1)}, u32[]{:S(2)}, u32[]{:S(2)}) collective-permute-start(bf16[528,128]{1,0:T(8,128)(2,1)S(1)} %row_sum.3.own_ref), channel_id=1, source_target_pairs={{0,12},{1,13},{2,14},{3,15},{4,8},{5,9},{6,10},{7,11},{8,4},{9,5},... | collective-permute-start | bytes 405512 | tf_op jit(solution)/shard_map/ppermute | solution.py:406
  81.6 5.4 %collective-permute-start.25 = (bf16[528,128]{1,0:T(8,128)(2,1)S(1)}, bf16[528,128]{1,0:T(8,128)(2,1)S(1)}, u32[]{:S(2)}, u32[]{:S(2)}) collective-permute-start(bf16[528,128]{1,0:T(8,128)(2,1)S(1)} %row_sum.3.own_ref), channel_id=1, source_target_pairs={{0,1},{1,0},{2,3},{3,2},{4,5},{5,4},{6,7},{7,6},{8,9},{9,8},{10,11... | collective-permute-start | bytes 405512 | tf_op jit(solution)/shard_map/ppermute | solution.py:406
  (8 other events, 23.6 us)
